TPU v7x, 32 devices: a whole 2x2x4 slice. The times are simulated.
32 devices in a mesh: groups: 2 (over y), expert: 4 (over z), dp: 2 (over x), mp: 2 (over core).
Axes of the slice: x: 2, y: 2, z: 4, core: 2. Of those that a mesh axis runs over, the one named last changes fastest.
Arguments:
- tokens: bfloat16 [768, 4096], P(('groups', 'expert', 'dp', 'mp')), parts along dimension 0, may hold values from -6 to 6
- pseudo: bfloat16 [768, 8, 1536], P(('groups', 'expert', 'dp', 'mp')), parts along dimension 0, may hold values from -6 to 6
- assign: int32 [768, 8], P(('groups', 'expert', 'dp', 'mp')), parts along dimension 0, may hold values from 0 to 127, all different within a row; in each aligned block of 24 rows (0 to 23, 24 to 47, ...) at most 2 rows name the same one
- counts: int32 [8], P(('groups', 'expert')), parts along dimension 0, may hold values from 12 to 48
- basis_act: bfloat16 [8, 4096, 2048], P(('groups', 'expert'), 'dp', 'mp'), parts along dimension 0, may hold values from -0.09375 to 0.09375
- basis_grad: bfloat16 [8, 1536, 1536], P(('groups', 'expert'), 'dp', 'mp'), parts along dimension 0, may hold values from -0.15625 to 0.15625
- queries_act: bfloat16 [32, 4096], P('groups', 'dp'), parts along dimension 0, may hold values from -6 to 6
- queries_grad: bfloat16 [32, 1536], P('groups', 'dp'), parts along dimension 0, may hold values from -6 to 6
- query_expert: int32 [32, 1], P('groups'), parts along dimension 0, may hold values from 0 to 3; in each aligned block of 16 rows (0 to 15, 16 to 31, ...) at most 6 rows name the same one
Outputs:
- act_cov: bfloat16 [8, 4096, 4096], P(('groups', 'expert'), 'dp', 'mp'), parts along dimension 0
- grad_cov: bfloat16 [8, 1536, 1536], P(('groups', 'expert'), 'dp', 'mp'), parts along dimension 0
- rot_act: bfloat16 [32, 2048], P(('groups', 'expert', 'dp'), 'mp'), parts along dimension 0
- rot_grad: bfloat16 [32, 1536], P(('groups', 'expert', 'dp'), 'mp'), parts along dimension 0
There are 2 independent parts, one for each index of `groups`. A program takes and returns all parts, laid end to end along the dimension named above; each array names one. Nothing has to cross between parts.
Inputs may be any that keep to these rules, and one draw needn't show every extreme that they name: `assign`: each token names 8 different experts; in each aligned block of 24 tokens (the tokens of one device) no expert is named by more than 2 tokens, a bound that some block reaches. `query_expert`: no expert is named by more than 6 query rows, a bound that some block reaches.
All inputs are finite; a program needn't handle non-finite values.
Results may differ from a plain program's by a relative error of at most 0.001.
Values may be sent and summed in bfloat16 or wider, within the bound.
No kernel may reach another device: no remote copies, remote signals or barrier semaphores. Data moves between devices by JAX's collectives and lax.ppermute only.
A program may use at most 64 MiB of HBM per device.

v0:
```python
import jax
import jax.numpy as jnp
from jax import lax
from jax.sharding import PartitionSpec as P

CAP = 2


def local(
    tokens, pseudo, assign, counts, basis_act, basis_grad, queries_act, queries_grad, query_expert
):
    owners = lax.axis_size("expert")
    tok_rows, feat_width = tokens.shape
    slot_count = assign.shape[1]
    grad_width = pseudo.shape[2]
    flat_len = tok_rows * slot_count
    flat_ids = assign.reshape(flat_len)
    picked_slots = (flat_ids[None, :] == lax.broadcasted_iota(jnp.int32, (owners, 1), 0)).astype(
        jnp.int32
    )
    slot_rank = jnp.cumsum(picked_slots, axis=1) - 1
    chosen = (picked_slots[:, None, :] == 1) & (
        slot_rank[:, None, :] == lax.broadcasted_iota(jnp.int32, (1, CAP, 1), 1)
    )
    chosen_f = chosen.astype(jnp.float32).reshape(owners * CAP, tok_rows, slot_count)
    token_pick = jnp.sum(chosen_f, axis=2).astype(jnp.bfloat16)
    slot_pick = chosen_f.reshape(owners * CAP, flat_len).astype(jnp.bfloat16)
    send_act = jnp.dot(token_pick, tokens, preferred_element_type=jnp.float32).astype(jnp.bfloat16)
    send_grad = jnp.dot(
        slot_pick, pseudo.reshape(flat_len, grad_width), preferred_element_type=jnp.float32
    ).astype(jnp.bfloat16)
    got_act, got_grad = (
        lax.all_to_all(
            send_act.reshape(owners, CAP, feat_width),
            "expert",
            split_axis=0,
            concat_axis=0,
            tiled=True,
        ),
        lax.all_to_all(
            send_grad.reshape(owners, CAP, grad_width),
            "expert",
            split_axis=0,
            concat_axis=0,
            tiled=True,
        ),
    )
    act_rows = got_act.reshape(owners * CAP, feat_width)
    grad_rows = got_grad.reshape(owners * CAP, grad_width)
    dp_count = lax.axis_size("dp")
    mp_count = lax.axis_size("mp")
    dp_index = lax.axis_index("dp")
    mp_index = lax.axis_index("mp")
    act_block = feat_width // dp_count
    act_half = feat_width // mp_count
    grad_block = grad_width // dp_count
    grad_half = grad_width // mp_count
    contract = (((0,), (0,)), ((), ()))
    act_piece = lax.all_gather(act_rows, ("dp", "mp"), axis=0, tiled=True)
    grad_piece = lax.all_gather(grad_rows, ("dp", "mp"), axis=0, tiled=True)
    left_cols = lax.dynamic_slice_in_dim(act_piece, dp_index * act_block, act_block, 1)
    right_cols = lax.dynamic_slice_in_dim(act_piece, mp_index * act_half, act_half, 1)
    grad_left = lax.dynamic_slice_in_dim(grad_piece, dp_index * grad_block, grad_block, 1)
    grad_right = lax.dynamic_slice_in_dim(grad_piece, mp_index * grad_half, grad_half, 1)
    act_acc = lax.dot_general(left_cols, right_cols, contract, preferred_element_type=jnp.float32)
    grad_acc = lax.dot_general(grad_left, grad_right, contract, preferred_element_type=jnp.float32)
    divisor = counts[0].astype(jnp.float32)
    act_cov = (act_acc / divisor).astype(jnp.bfloat16)[None]
    grad_cov = (grad_acc / divisor).astype(jnp.bfloat16)[None]
    my_expert = lax.axis_index("expert")
    query_ids = query_expert[:, 0]
    query_count = query_ids.shape[0]
    rows_out = query_count // (owners * dp_count)
    query_cap = 3 * rows_out * dp_count // 2
    is_mine = (query_ids == my_expert).astype(jnp.int32)
    query_rank = jnp.cumsum(is_mine) - 1
    pick_query = (is_mine[None, :] == 1) & (
        query_rank[None, :] == lax.broadcasted_iota(jnp.int32, (query_cap, 1), 0)
    )
    pick_bf = pick_query.astype(jnp.bfloat16)
    my_act = jnp.dot(pick_bf, queries_act, preferred_element_type=jnp.float32).astype(jnp.bfloat16)
    my_grad = jnp.dot(pick_bf, queries_grad, preferred_element_type=jnp.float32).astype(
        jnp.bfloat16
    )
    part_act = jnp.dot(my_act, basis_act[0], preferred_element_type=jnp.float32)
    part_grad = jnp.dot(my_grad, basis_grad[0], preferred_element_type=jnp.float32)
    partial_value = jnp.concatenate([part_act, part_grad], axis=1)
    eig_half = part_act.shape[1]
    spread = pick_query.T.astype(jnp.float32)
    result = lax.psum_scatter(
        jnp.dot(
            spread,
            partial_value,
            precision=lax.Precision.HIGHEST,
            preferred_element_type=jnp.float32,
        ),
        ("expert", "dp"),
        scatter_dimension=0,
        tiled=True,
    ).astype(jnp.bfloat16)
    return (act_cov, grad_cov, result[:, :eig_half], result[:, eig_half:])


def solution(mesh):
    return jax.shard_map(
        local,
        mesh=mesh,
        in_specs=(
            P(("groups", "expert", "dp", "mp"), None),
            P(("groups", "expert", "dp", "mp"), None, None),
            P(("groups", "expert", "dp", "mp"), None),
            P(("groups", "expert")),
            P(("groups", "expert"), "dp", "mp"),
            P(("groups", "expert"), "dp", "mp"),
            P("groups", "dp"),
            P("groups", "dp"),
            P("groups", None),
        ),
        out_specs=(
            P(("groups", "expert"), "dp", "mp"),
            P(("groups", "expert"), "dp", "mp"),
            P(("groups", "expert", "dp"), "mp"),
            P(("groups", "expert", "dp"), "mp"),
        ),
        check_vma=False,
    )
```

profile of v0, /device:TPU:0, one launch (start us, length us, event | category | flops | bytes accessed | tf_op | source)
XLA Modules:
  0.0 81.3 jit_solution(10996099778662321739)
XLA Ops:
  0.6 0.0 copy-start
  0.6 0.0 copy-start.3
  0.7 0.0 copy-start.2
  0.7 0.0 copy-start.1
  0.7 0.9 %copy.20 = s32[24,8]{1,0:T(8,128)S(1)} copy(s32[24,8]{0,1:T(8,128)} %param.11) | data formatting | bytes 1536 | tf_op args[2]
  1.5 0.1 eq.98
  1.7 1.2 %reduce-window.18 = s32[4,2,128]{2,1,0:T(2,128)S(1)} reduce-window(s32[4,2,128]{2,1,0:T(2,128)S(1)} %reshape.133, s32[]{:T(128)} %constant.12.clone.1), window={size=1x1x128 pad=0_0x0_0x127_0}, to_apply=%region_0.0 | reduce-window | flops 130048 | bytes 8196 | tf_op jit(solution)/shard_map/reduce-window
  2.9 0.1 slice.20
  3.0 0.1 copy.21
  3.1 0.1 copy.22
  3.2 0.1 add_bitcast_fusion
  3.3 1.2 %convolution_convert_fusion.2 = bf16[8,1536]{1,0:T(8,128)(2,1)S(1)} fusion(bf16[8,192]{1,0:T(8,128)(2,1)S(1)} %convert_element_type.83, bf16[24,8,1536]{2,1,0:T(8,128)(2,1)} %param.10), kind=kOutput, calls=%fused_computation.7 | convolution fusion | flops 4730880 | bytes 617472 | tf_op jit(solution)/shard_map/dot_general | solution.py:29
  4.6 0.6 reshape.138
  5.2 6.3 %all-to-all-start.1 = ((bf16[4,2,1536]{2,1,0:T(2,128)(2,1)}), bf16[4,2,1536]{2,1,0:T(2,128)(2,1)S(1)}, u32[]{:S(2)}, u32[]{:S(2)}) async-start(bf16[4,2,1536]{2,1,0:T(2,128)(2,1)} %reshape.138), calls=%async_computation.1 | async-start | bytes 49152 | tf_op jit(solution)/shard_map/all_to_all | solution.py:40
  11.5 0.1 eq.105
  11.7 0.1 and.33
  11.8 0.1 eq.107
  11.9 0.7 compare_bitcast_fusion
  12.5 0.1 copy.23
  12.7 0.1 add_reduce_fusion
  12.8 3.0 %fusion.1 = f32[6,1024]{1,0:T(8,128)S(1)} fusion(bf16[1,2048,1024]{2,1,0:T(8,128)(2,1)} %param.13, bf16[16,2048]{1,0:T(8,128)(2,1)} %param.15, s32[16]{0:T(128)S(1)} %add_reduce_fusion, pred[16]{0:T(512)(128)(4,1)S(1)} %get-tuple-element.4), kind=kOutput, calls=%fused_computation.3 | convolution fusion | flops 25571520 | bytes 4284496 | tf_op jit(solution)/shard_map/dot_general | solution.py:85
  15.7 0.0 copy-done
  15.7 0.0 copy-done.2
  15.7 0.4 fusion.4
  16.1 0.3 fusion.9
  16.4 38.9 %all-reduce.1 = bf16[16,1792]{1,0:T(8,128)(2,1)S(1)} all-reduce(f32[16,1792]{1,0:T(8,128)S(1)} %fusion.9), channel_id=2, replica_groups=mesh['groups'=2,'expert'=4,'dp'=2,'mp'=2] {'expert','dp'}, use_global_device_ids=true, to_apply=%region_4.5.clone | all-reduce | flops 28672 | bytes 172032
  55.3 0.2 convert_reduce_fusion
  55.5 0.0 copy-done.1
  55.5 0.2 convolution_convert_fusion
  55.6 0.0 copy-done.3
  55.7 0.6 dynamic-slice
  56.9 0.6 slice.22
  57.5 0.6 slice.23
  58.1 0.7 reshape.135
  59.4 0.0 all-to-all-done.1
  59.5 3.3 %all-to-all-start = ((bf16[4,2,4096]{2,1,0:T(2,128)(2,1)}), bf16[4,2,4096]{2,1,0:T(2,128)(2,1)S(1)}, u32[]{:S(2)}, u32[]{:S(2)}) async-start(bf16[4,2,4096]{2,1,0:T(2,128)(2,1)} %reshape.135), calls=%async_computation | async-start | bytes 131072 | tf_op jit(solution)/shard_map/all_to_all | solution.py:33
  62.8 5.3 %all_gather.7 = bf16[32,1536]{1,0:T(8,128)(2,1)S(1)} all-gather(bf16[8,1536]{1,0:T(8,128)(2,1)S(1)} %reshape.139), channel_id=1, replica_groups=mesh['groups'=2,'expert'=4,'dp'=2,'mp'=2] {'dp','mp'}, dimensions={0}, use_global_device_ids=true | all-gather | bytes 122880 | tf_op jit(solution)/shard_map/all_gather | solution.py:60
  68.1 1.5 %fusion.3 = bf16[1,768,768]{2,1,0:T(8,128)(2,1)} fusion(f32[]{:T(128)} %bitcast.1, bf16[32,1536]{1,0:T(8,128)(2,1)S(1)} %all_gather.7, s32[]{:T(128)S(6)} %select_n.15, s32[]{:T(128)S(6)} %select_n.14), kind=kOutput, calls=%fused_computation.8 | convolution fusion | flops 38928384 | bytes 1277964 | tf_op jit(solution)/shard_map/dot_general | solution.py:66
  69.6 0.0 all-to-all-done
  69.7 5.9 %all_gather.6 = bf16[32,4096]{1,0:T(8,128)(2,1)S(1)} all-gather(bf16[8,4096]{1,0:T(8,128)(2,1)S(1)} %reshape.136), channel_id=1, replica_groups=mesh['groups'=2,'expert'=4,'dp'=2,'mp'=2] {'dp','mp'}, dimensions={0}, use_global_device_ids=true | all-gather | bytes 327680 | tf_op jit(solution)/shard_map/all_gather | solution.py:59
  75.5 5.8 %fusion = bf16[1,2048,2048]{2,1,0:T(8,128)(2,1)} fusion(f32[]{:T(128)} %bitcast.1, bf16[32,4096]{1,0:T(8,128)(2,1)S(1)} %all_gather.6, s32[]{:T(128)S(6)} %select_n.13, s32[]{:T(128)S(6)} %select_n.12), kind=kOutput, calls=%fused_computation.1 | convolution fusion | flops 276824064 | bytes 8650764 | tf_op jit(solution)/shard_map/dot_general | solution.py:65
  (16 shorter events, 0.2 us)
Async XLA Ops:
  0.6 15.1 %copy-start = (bf16[1,768,768]{2,1,0:T(8,128)(2,1)S(1)}, bf16[1,768,768]{2,1,0:T(8,128)(2,1)}, u32[]{:S(2)}) copy-start(bf16[1,768,768]{2,1,0:T(8,128)(2,1)} %param.14) | copy-start | bytes 3538948
  0.6 55.0 %copy-start.3 = (u32[32]{0:T(128)S(1)}, u32[32]{0:T(128)}, u32[]{:S(2)}) copy-start(u32[32]{0:T(128)} %constant.47) | copy-start | bytes 388
  0.7 15.1 %copy-start.2 = (bf16[16,768]{1,0:T(8,128)(2,1)S(1)}, bf16[16,768]{1,0:T(8,128)(2,1)}, u32[]{:S(2)}) copy-start(bf16[16,768]{1,0:T(8,128)(2,1)} %param.16) | copy-start | bytes 73732
  0.7 54.8 %copy-start.1 = (bf16[24,4096]{1,0:T(8,128)(2,1)S(1)}, bf16[24,4096]{1,0:T(8,128)(2,1)}, u32[]{:S(2)}) copy-start(bf16[24,4096]{1,0:T(8,128)(2,1)} %param.9) | copy-start | bytes 589828
  5.2 54.2 %all-to-all-start.1 = ((bf16[4,2,1536]{2,1,0:T(2,128)(2,1)}), bf16[4,2,1536]{2,1,0:T(2,128)(2,1)S(1)}, u32[]{:S(2)}, u32[]{:S(2)}) async-start(bf16[4,2,1536]{2,1,0:T(2,128)(2,1)} %reshape.138), calls=%async_computation.1 | async-start | bytes 49152 | tf_op jit(solution)/shard_map/all_to_all | solution.py:40
  59.5 10.2 %all-to-all-start = ((bf16[4,2,4096]{2,1,0:T(2,128)(2,1)}), bf16[4,2,4096]{2,1,0:T(2,128)(2,1)S(1)}, u32[]{:S(2)}, u32[]{:S(2)}) async-start(bf16[4,2,4096]{2,1,0:T(2,128)(2,1)} %reshape.135), calls=%async_computation | async-start | bytes 131072 | tf_op jit(solution)/shard_map/all_to_all | solution.py:33
where the time goes:
time: 81.7 us; the launch traced here: 81.3 us
  blocking collectives  50.1 us (61%)
  matrix products  12.3 us (15%)
  starting transfers between devices  9.61 us (12%)
  local copies, waits for them, and re-layouts  4.84 us (6%)
  other arithmetic  2.35 us (3%)
  between operations  2.11 us (3%)
    unnamed x1, blocking collectives  38.9 us
    all_to_all x1, starting transfers between devices, local(): lax.all_to_all(send_grad.reshape(owners, CAP, grad_width), 'expert', spli...  6.32 us
    all_gather x1, blocking collectives, local(): act_piece = lax.all_gather(act_rows, ('dp', 'mp'), axis=0, tiled=True)  5.86 us
    dot_general x1, matrix products, local(): lax.dot_general(left_cols, right_cols, contract, preferred_element_type=j...  5.76 us
    all_gather x1, blocking collectives, local(): grad_piece = lax.all_gather(grad_rows, ('dp', 'mp'), axis=0, tiled=True)  5.34 us
    all_to_all x1, starting transfers between devices, local(): lax.all_to_all(send_act.reshape(owners, CAP, feat_width), 'expert', split...  3.3 us
    dot_general x1, matrix products, local(): part_act = jnp.dot(my_act, basis_act[0], preferred_element_type=jnp.float32)  2.96 us
  transfers between devices with their start and end apart: 2, of which 0 were waited for; matrix products, arithmetic and copies ran while one was open for 11% of the time, Pallas kernels for 0%

commit v1 on v0

v1 whole, which is shorter than its diff:
```python
import functools

import jax
import jax.numpy as jnp
from jax import lax
from jax.experimental import pallas as pl
from jax.experimental.pallas import tpu as pltpu
from jax.sharding import PartitionSpec as P

CAP = 2
F32 = jnp.float32
BF16 = jnp.bfloat16
HBM = pl.BlockSpec(memory_space=pl.ANY)
VMEM = pl.BlockSpec(memory_space=pltpu.VMEM)
SMEM = pl.BlockSpec(memory_space=pltpu.SMEM)


def partner_order(experts, blocks):
    away = [(de, dd) for dd in range(blocks) for de in range(experts - 1, 0, -1)]
    away += [(0, dd) for dd in range(1, blocks)] + [(0, 0)]
    half = experts * blocks // 2
    near = [p for p in away if p[1] == 0 and p[0] > 0] + [p for p in away if p[0] == 0 and p[1] > 0]
    far = [p for p in away if p not in near and p != (0, 0)] + [(0, 0)]
    order = (near + far)[:half], (near + far)[half:]
    return order


def dot(a, b):
    return jnp.dot(a, b, preferred_element_type=F32)


def by_row(table, rows, per):
    index = lax.broadcasted_iota(jnp.int32, (rows, 1), 0) // per
    value = jnp.zeros((rows, 1), jnp.int32)
    for i, entry in enumerate(table):
        if entry:
            value = jnp.where(index == i, entry, value)
    return value


def pack_kernel(
    order,
    row_out,
    assign_hbm,
    tokens_hbm,
    pseudo_hbm,
    qe_hbm,
    qa_hbm,
    qg_hbm,
    ba_hbm,
    bg_hbm,
    keep_ref,
    give_ref,
    assign_ref,
    tokens_ref,
    pseudo_ref,
    qe_ref,
    qa_ref,
    qg_ref,
    ba_ref,
    bg_ref,
    sems,
):
    chunks = 4
    deep = ba_ref.shape[0] // chunks
    small = [
        pltpu.make_async_copy(src, dst, sems.at[i])
        for i, (src, dst) in enumerate(
            [
                (assign_hbm, assign_ref),
                (qe_hbm, qe_ref),
                (qa_hbm, qa_ref),
                (qg_hbm, qg_ref),
                (tokens_hbm, tokens_ref),
                (pseudo_hbm, pseudo_ref),
                (bg_hbm, bg_ref),
            ]
        )
    ]
    large = [
        pltpu.make_async_copy(
            ba_hbm.at[pl.ds(i * deep, deep)], ba_ref.at[pl.ds(i * deep, deep)], sems.at[len(small) + i]
        )
        for i in range(chunks)
    ]
    for copy in small + large:
        copy.start()
    expert, block, core = lax.axis_index("expert"), lax.axis_index("dp"), lax.axis_index("mp")
    half = len(order[0])
    rows = 4 * half
    blocks = 1 + max(dd for _, dd in order[0] + order[1])
    slots, toks = assign_ref.shape
    flat = slots * toks
    d_model, hidden = tokens_ref.shape[1], pseudo_ref.shape[1]
    plan = [order[0] + order[1], order[1] + order[0]]
    step_e = jnp.where(core == 0, by_row([p[0] for p in plan[0]], rows, 2), by_row([p[0] for p in plan[1]], rows, 2))
    step_d = jnp.where(core == 0, by_row([p[1] for p in plan[0]], rows, 2), by_row([p[1] for p in plan[1]], rows, 2))
    to_e, to_d = step_e ^ expert, step_d ^ block
    second = lax.broadcasted_iota(jnp.int32, (rows, 1), 0) % 2

    small[0].wait()
    spread = (
        lax.broadcasted_iota(jnp.int32, (toks, flat), 0)
        == lax.broadcasted_iota(jnp.int32, (toks, flat), 1) // slots
    ).astype(F32)
    ids = dot(assign_ref[...].astype(F32), spread)
    mine = (
        lax.broadcasted_iota(jnp.int32, (slots, flat), 0)
        == lax.broadcasted_iota(jnp.int32, (slots, flat), 1) % slots
    )
    ids = jnp.sum(jnp.where(mine, ids, 0.0), axis=0, keepdims=True).astype(jnp.int32)
    place = lax.broadcasted_iota(jnp.int32, (rows, flat), 1)
    hit = ids == to_e
    first = jnp.min(jnp.where(hit, place, flat), axis=1, keepdims=True)
    last = jnp.max(jnp.where(hit, place, -1), axis=1, keepdims=True)
    chosen = jnp.where(second == 0, first, jnp.where(last == first, -1, last))
    slot_pick = (place == chosen).astype(BF16)
    low = lax.broadcasted_iota(jnp.int32, (rows, toks), 1) * slots
    token_pick = ((chosen >= low) & (chosen < low + slots)).astype(BF16)

    def put(column, value):
        value = value.astype(BF16)
        width = value.shape[1]
        for i in range(half):
            keep_ref[i, :, column : column + width] = value[2 * i : 2 * i + 2]
            give_ref[i, :, column : column + width] = value[2 * (half + i) : 2 * (half + i) + 2]

    small[4].wait()
    put(0, dot(token_pick, tokens_ref[...]))
    small[5].wait()
    put(d_model, dot(slot_pick, pseudo_ref[...]))

    for i in (1, 2, 3):
        small[i].wait()
    queries = qa_ref.shape[0]
    base = d_model + hidden
    act_cols, grad_cols = ba_ref.shape[1], bg_ref.shape[1]
    asked = qe_ref[...] == expert
    query = lax.broadcasted_iota(jnp.int32, (rows, queries), 1)
    picks = []
    for i in range(row_out // 2):
        picks.append(
            ((query == (to_e * blocks + to_d) * row_out + 2 * i + second) & asked).astype(BF16)
        )
    pick = jnp.concatenate(picks, axis=0) if len(picks) > 1 else picks[0]
    my_act = dot(pick, qa_ref[...]).astype(BF16)
    my_grad = dot(pick, qg_ref[...]).astype(BF16)
    small[6].wait()
    grad_part = dot(my_grad, bg_ref[...])
    act_part = jnp.zeros((my_act.shape[0], act_cols), F32)
    for c in range(chunks):
        large[c].wait()
        act_part += dot(my_act[:, c * deep : (c + 1) * deep], ba_ref[c * deep : (c + 1) * deep])
    act_high = act_part.astype(BF16)
    grad_high = grad_part.astype(BF16)
    act_low = act_part - act_high.astype(F32)
    grad_low = grad_part - grad_high.astype(F32)
    width = 2 * (act_cols + grad_cols)
    for i in range(row_out // 2):
        cut = slice(i * rows, (i + 1) * rows)
        at = base + i * width
        put(at, act_high[cut])
        put(at + act_cols, grad_high[cut])
        put(at + act_cols + grad_cols, act_low[cut])
        put(at + 2 * act_cols + grad_cols, grad_low[cut])


def pack(order, row_out, assign, tokens, pseudo, qe, qa, qg, ba, bg):
    width = tokens.shape[1] + pseudo.shape[1] + row_out * (ba.shape[1] + bg.shape[1])
    out = jax.ShapeDtypeStruct((len(order[0]), CAP, width), BF16)
    operands = (assign, tokens, pseudo, qe, qa, qg, ba, bg)
    return pl.pallas_call(
        functools.partial(pack_kernel, order, row_out),
        out_shape=(out, out),
        in_specs=[HBM] * len(operands),
        out_specs=(VMEM, VMEM),
        scratch_shapes=[pltpu.VMEM(x.shape, x.dtype) for x in operands]
        + [pltpu.SemaphoreType.DMA((11,))],
        compiler_params=pltpu.CompilerParams(vmem_limit_bytes=32 * 1024 * 1024),
        name="select_rows_and_rotate_queries",
    )(*operands)


def factor_kernel(
    act_width,
    row_out,
    act_cols,
    count_ref,
    here_ref,
    there_ref,
    act_hbm,
    grad_hbm,
    rot_act_ref,
    rot_grad_ref,
    rows_ref,
    act_ref,
    grad_ref,
    sems,
):
    block, core = lax.axis_index("dp"), lax.axis_index("mp")
    half = here_ref.shape[0]
    act_block, act_half = act_ref.shape
    grad_block, grad_half = grad_ref.shape
    wide = act_width + 2 * grad_half
    inverse = 1.0 / count_ref[0].astype(F32)
    pieces = []
    for ref in (here_ref, there_ref):
        for i in range(half):
            for c in range(2):
                pieces.append(ref[i, c, :, :wide])
    rows_ref[...] = jnp.concatenate(pieces, axis=0)

    contract = (((0,), (0,)), ((), ()))
    grad_left = rows_ref[:, pl.ds(pl.multiple_of(act_width + block * grad_block, 128), grad_block)]
    grad_right = rows_ref[:, pl.ds(pl.multiple_of(act_width + core * grad_half, 128), grad_half)]
    grad_sum = lax.dot_general(grad_left, grad_right, contract, preferred_element_type=F32)
    grad_ref[...] = (grad_sum * inverse).astype(BF16)
    grad_copy = pltpu.make_async_copy(grad_ref, grad_hbm, sems.at[0])
    grad_copy.start()

    step = 256
    count = act_block // step
    right = rows_ref[:, pl.ds(pl.multiple_of(core * act_half, 128), act_half)]
    copies = []
    for i in range(count):
        at = pl.multiple_of(block * act_block + i * step, 128)
        left = rows_ref[:, pl.ds(at, step)]
        part = lax.dot_general(left, right, contract, preferred_element_type=F32)
        act_ref[i * step : (i + 1) * step, :] = (part * inverse).astype(BF16)
        copy = pltpu.make_async_copy(
            act_ref.at[pl.ds(i * step, step)], act_hbm.at[pl.ds(i * step, step)], sems.at[1 + i]
        )
        copy.start()
        copies.append(copy)

    cols = act_cols + rot_grad_ref.shape[1]
    for i in range(row_out // 2):
        at = wide + i * 2 * cols
        total = jnp.zeros((2, cols), F32)
        for ref, c in ((here_ref, 0), (there_ref, 1)):
            for r in range(half):
                high = ref[r, c, :, at : at + cols].astype(F32)
                low = ref[r, c, :, at + cols : at + 2 * cols].astype(F32)
                total += high + low
        rot_act_ref[2 * i : 2 * i + 2, :] = total[:, :act_cols].astype(BF16)
        rot_grad_ref[2 * i : 2 * i + 2, :] = total[:, act_cols:].astype(BF16)
    grad_copy.wait()
    for copy in copies:
        copy.wait()


def factors(act_width, row_out, act_tile, grad_tile, act_cols, grad_cols, counts, here, there):
    rows = 2 * here.shape[0] * here.shape[1] * here.shape[2]
    wide = act_width + 2 * grad_tile[1]
    return pl.pallas_call(
        functools.partial(factor_kernel, act_width, row_out, act_cols),
        out_shape=(
            jax.ShapeDtypeStruct(act_tile, BF16),
            jax.ShapeDtypeStruct(grad_tile, BF16),
            jax.ShapeDtypeStruct((row_out, act_cols), BF16),
            jax.ShapeDtypeStruct((row_out, grad_cols), BF16),
        ),
        in_specs=[SMEM, VMEM, VMEM],
        out_specs=(HBM, HBM, VMEM, VMEM),
        scratch_shapes=[
            pltpu.VMEM((rows, wide), BF16),
            pltpu.VMEM(act_tile, BF16),
            pltpu.VMEM(grad_tile, BF16),
            pltpu.SemaphoreType.DMA((1 + act_tile[0] // 256,)),
        ],
        compiler_params=pltpu.CompilerParams(vmem_limit_bytes=40 * 1024 * 1024),
        name="factor_tiles",
    )(counts, here, there)


def local(
    tokens, pseudo, assign, counts, basis_act, basis_grad, queries_act, queries_grad, query_expert
):
    experts, blocks = lax.axis_size("expert"), lax.axis_size("dp")
    toks, d_model = tokens.shape
    slots, hidden = pseudo.shape[1], pseudo.shape[2]
    row_out = query_expert.shape[0] // (experts * blocks)
    order = partner_order(experts, blocks)
    half = len(order[0])
    keep, give = pack(
        order,
        row_out,
        assign.T,
        tokens,
        pseudo.reshape(toks * slots, hidden),
        query_expert.T,
        queries_act,
        queries_grad,
        basis_act[0],
        basis_grad[0],
    )
    swap = [(0, 1), (1, 0)]
    got = lax.ppermute(give, "mp", swap)
    arrived = []
    for r in range(half):
        pairs = [
            ((e * blocks + d) * 2 + m, ((e ^ order[m][r][0]) * blocks + (d ^ order[m][r][1])) * 2 + m)
            for e in range(experts)
            for d in range(blocks)
            for m in range(2)
        ]
        arrived.append(lax.ppermute(jnp.stack([keep[r], got[r]]), ("expert", "dp", "mp"), pairs))
    here = jnp.stack(arrived)
    there = lax.ppermute(here, "mp", swap)
    act_cov, grad_cov, rot_act, rot_grad = factors(
        d_model,
        row_out,
        (d_model // blocks, d_model // 2),
        (hidden // blocks, hidden // 2),
        basis_act.shape[2],
        basis_grad.shape[2],
        counts,
        here,
        there,
    )
    return act_cov[None], grad_cov[None], rot_act, rot_grad


def solution(mesh):
    return jax.shard_map(
        local,
        mesh=mesh,
        in_specs=(
            P(("groups", "expert", "dp", "mp"), None),
            P(("groups", "expert", "dp", "mp"), None, None),
            P(("groups", "expert", "dp", "mp"), None),
            P(("groups", "expert")),
            P(("groups", "expert"), "dp", "mp"),
            P(("groups", "expert"), "dp", "mp"),
            P("groups", "dp"),
            P("groups", "dp"),
            P("groups", None),
        ),
        out_specs=(
            P(("groups", "expert"), "dp", "mp"),
            P(("groups", "expert"), "dp", "mp"),
            P(("groups", "expert", "dp"), "mp"),
            P(("groups", "expert", "dp"), "mp"),
        ),
        check_vma=False,
    )
```

time: 81.7 us -> 37.3 us (0.46)
  blocking collectives: 50.1 us -> 0 us
  matrix products: 12.3 us -> 0 us
  Pallas kernels: 0 us -> 8.33 us
  waiting for transfers between devices: 0.01 us -> 7.75 us
  local copies, waits for them, and re-layouts: 4.84 us -> 8.56 us
  other arithmetic: 2.35 us -> 0.94 us
    unnamed x1 -> x0, blocking collectives: 38.9 us -> none
    dot_general x7 -> x0, matrix products: 12.3 us -> none  [the longest x1 5.76 us: local(): lax.dot_general(left_cols, right_cols, contract, preferred_element_type=j...]
    all_gather x2 -> x0, blocking collectives: 11.2 us -> none  [the longest x1 5.86 us: local(): act_piece = lax.all_gather(act_rows, ('dp', 'mp'), axis=0, tiled=True)]
    ppermute x0 -> x6, starting transfers between devices: none -> 9.93 us  [the longest x4 9.34 us: local(): lax.ppermute(jnp.stack([keep[r], got[r]]), ('expert', 'dp', 'mp'), pairs)]
    all_to_all x2 -> x0, starting transfers between devices: 9.61 us -> none  [the longest x1 6.32 us: local(): lax.all_to_all(send_grad.reshape(owners, CAP, grad_width), 'expert', spli...]
    pallas_call x0 -> x2, Pallas kernels: none -> 8.33 us  [the longest x1 5.03 us: factors(): pl.pallas_call(functools.partial(factor_kernel, act_width, row_out, act_c...]
    ppermute x0 -> x6, waiting for transfers between devices: none -> 7.75 us  [the longest x4 5.92 us: local(): lax.ppermute(jnp.stack([keep[r], got[r]]), ('expert', 'dp', 'mp'), pairs)]
    unnamed x11 -> x16, local copies, waits for them, and re-layouts: 1.48 us -> 8.36 us
  transfers between devices with their start and end apart: 2 -> 6, of which waited for: 0 -> 4; matrix products, arithmetic and copies ran while one was open for 11% -> 1% of each run, Pallas kernels for 0% -> 0%
where the time goes in v1:
time: 37.3 us; the launch traced here: 36.9 us
  starting transfers between devices  9.93 us (27%)
  local copies, waits for them, and re-layouts  8.56 us (23%)
  Pallas kernels  8.33 us (22%)
  waiting for transfers between devices  7.75 us (21%)
  between operations  1.36 us (4%)
  other arithmetic  0.94 us (3%)
    ppermute x4, starting transfers between devices, local(): lax.ppermute(jnp.stack([keep[r], got[r]]), ('expert', 'dp', 'mp'), pairs)  9.34 us
    unnamed x16, local copies, waits for them, and re-layouts  8.36 us
    ppermute x4, waiting for transfers between devices, local(): lax.ppermute(jnp.stack([keep[r], got[r]]), ('expert', 'dp', 'mp'), pairs)  5.92 us
    pallas_call x1, Pallas kernels, factors(): pl.pallas_call(functools.partial(factor_kernel, act_width, row_out, act_c...  5.03 us
    pallas_call x1, Pallas kernels, pack(): pl.pallas_call(functools.partial(pack_kernel, order, row_out), out_shape=...  3.31 us
    ppermute x1, waiting for transfers between devices, local(): there = lax.ppermute(here, 'mp', swap)  0.92 us
    ppermute x1, waiting for transfers between devices, local(): got = lax.ppermute(give, 'mp', swap)  0.9 us
  transfers between devices with their start and end apart: 6, of which 4 were waited for; matrix products, arithmetic and copies ran while one was open for 1% of the time, Pallas kernels for 0%

profile of v1, /device:TPU:0, one launch (start us, length us, event | category | flops | bytes accessed | tf_op | source)
XLA Modules:
  0.0 36.9 jit_solution(5254156524090632688)
XLA Ops:
  0.6 0.0 copy-start
  0.6 2.2 %copy-done = bf16[1,2048,1024]{2,1,0:T(8,128)(2,1)S(1)} copy-done((bf16[1,2048,1024]{2,1,0:T(8,128)(2,1)S(1)}, bf16[1,2048,1024]{2,1,0:T(8,128)(2,1)}, u32[]{:S(2)}) %copy-start) | copy-done | bytes 4194328
  2.8 0.0 copy-start.1
  2.8 1.3 %copy-done.1 = bf16[1,768,768]{2,1,0:T(8,128)(2,1)S(1)} copy-done((bf16[1,768,768]{2,1,0:T(8,128)(2,1)S(1)}, bf16[1,768,768]{2,1,0:T(8,128)(2,1)}, u32[]{:S(2)}) %copy-start.1) | copy-done | bytes 1179672
  4.1 0.0 copy-start.2
  4.1 1.1 %copy-done.2 = bf16[24,8,1536]{2,1,0:T(8,128)(2,1)S(1)} copy-done((bf16[24,8,1536]{2,1,0:T(8,128)(2,1)S(1)}, bf16[24,8,1536]{2,1,0:T(8,128)(2,1)}, u32[]{:S(2)}) %copy-start.2) | copy-done | bytes 589848
  5.2 0.0 copy-start.3
  5.2 0.9 %copy-done.3 = bf16[24,4096]{1,0:T(8,128)(2,1)S(1)} copy-done((bf16[24,4096]{1,0:T(8,128)(2,1)S(1)}, bf16[24,4096]{1,0:T(8,128)(2,1)}, u32[]{:S(2)}) %copy-start.3) | copy-done | bytes 196632
  6.1 0.0 copy-start.4
  6.1 0.8 %copy-done.4 = bf16[16,2048]{1,0:T(8,128)(2,1)S(1)} copy-done((bf16[16,2048]{1,0:T(8,128)(2,1)S(1)}, bf16[16,2048]{1,0:T(8,128)(2,1)}, u32[]{:S(2)}) %copy-start.4) | copy-done | bytes 65560
  6.9 0.0 copy-start.5
  6.9 0.7 %copy-done.5 = bf16[16,768]{1,0:T(8,128)(2,1)S(1)} copy-done((bf16[16,768]{1,0:T(8,128)(2,1)S(1)}, bf16[16,768]{1,0:T(8,128)(2,1)}, u32[]{:S(2)}) %copy-start.5) | copy-done | bytes 24600
  7.7 0.0 copy-start.6
  7.7 0.7 %copy-done.6 = s32[24,8]{0,1:T(8,128)S(1)} copy-done((s32[24,8]{0,1:T(8,128)S(1)}, s32[24,8]{0,1:T(8,128)}, u32[]{:S(2)}) %copy-start.6) | copy-done | bytes 792
  8.4 0.0 copy-start.7
  8.4 0.7 %copy-done.7 = s32[16,1]{0,1:T(1,128)S(1)} copy-done((s32[16,1]{0,1:T(1,128)S(1)}, s32[16,1]{0,1:T(1,128)}, u32[]{:S(2)}) %copy-start.7) | copy-done | bytes 88
  9.0 3.3 %select_rows_and_rotate_queries.1 = (bf16[4,2,9216]{2,1,0:T(2,128)(2,1)S(1)}, bf16[4,2,9216]{2,1,0:T(2,128)(2,1)S(1)}) custom-call(s32[8,24]{1,0:T(8,128)S(1)} %bitcast.14, bf16[24,4096]{1,0:T(8,128)(2,1)S(1)} %copy-done.3, bf16[192,1536]{1,0:T(8,128)(2,1)S(1)} %bitcast.13, s32[1,16]{1,0:T(1,128)S(1)} %bitcast.15, bf16[16,2048]{1,0:T(8,128)(2,1)S(1)} %copy-done.4, ...), custom_call_target="tpu_custom_call" | custom-call | tf_op jit(solution)/shard_map/select_rows_and_rotate_queries/pallas_call | solution.py:172
  12.3 0.5 %collective-permute-start = (bf16[4,2,9216]{2,1,0:T(2,128)(2,1)S(1)}, bf16[4,2,9216]{2,1,0:T(2,128)(2,1)S(1)}, u32[]{:S(2)}, u32[]{:S(2)}) collective-permute-start(bf16[4,2,9216]{2,1,0:T(2,128)(2,1)S(1)} %get-tuple-element.11), channel_id=1, source_target_pairs={{0,1},{1,0},{2,3},{3,2},{4,5},{5,4},{6,7},{7,6},{8,9},{9,8},{10,11... | collective-permute-start | bytes 442376 | tf_op jit(solution)/shard_map/ppermute | solution.py:298
  12.8 0.1 fusion
  12.9 0.9 %collective-permute-done = bf16[4,2,9216]{2,1,0:T(2,128)(2,1)S(1)} collective-permute-done((bf16[4,2,9216]{2,1,0:T(2,128)(2,1)S(1)}, bf16[4,2,9216]{2,1,0:T(2,128)(2,1)S(1)}, u32[]{:S(2)}, u32[]{:S(2)}) %collective-permute-start) | collective-permute-done | bytes 147488 | tf_op jit(solution)/shard_map/ppermute | solution.py:298
  13.8 0.1 fusion.1
  14.0 0.1 pad_maximum_fusion.2
  14.1 4.0 %collective-permute-start.2 = (bf16[2,2,9216]{2,1,0:T(2,128)(2,1)S(1)}, bf16[2,2,9216]{2,1,0:T(2,128)(2,1)S(1)}, u32[]{:S(2)}, u32[]{:S(2)}) collective-permute-start(bf16[2,2,9216]{2,1,0:T(2,128)(2,1)S(1)} %pad_maximum_fusion.2), channel_id=1, source_target_pairs={{0,8},{1,11},{2,10},{3,9},{4,12},{5,15},{6,14},{7,13},{8,0},{9,3},... | collective-permute-start | bytes 221192 | tf_op jit(solution)/shard_map/ppermute | solution.py:307
  18.1 0.1 pad_maximum_fusion.3
  18.2 1.6 %collective-permute-start.3 = (bf16[2,2,9216]{2,1,0:T(2,128)(2,1)S(1)}, bf16[2,2,9216]{2,1,0:T(2,128)(2,1)S(1)}, u32[]{:S(2)}, u32[]{:S(2)}) collective-permute-start(bf16[2,2,9216]{2,1,0:T(2,128)(2,1)S(1)} %pad_maximum_fusion.3), channel_id=1, source_target_pairs={{0,4},{1,7},{2,6},{3,5},{4,0},{5,3},{6,2},{7,1},{8,12},{9,15},{10,... | collective-permute-start | bytes 221192 | tf_op jit(solution)/shard_map/ppermute | solution.py:307
  19.8 0.1 pad_maximum_fusion.4
  19.9 3.4 %collective-permute-start.4 = (bf16[2,2,9216]{2,1,0:T(2,128)(2,1)S(1)}, bf16[2,2,9216]{2,1,0:T(2,128)(2,1)S(1)}, u32[]{:S(2)}, u32[]{:S(2)}) collective-permute-start(bf16[2,2,9216]{2,1,0:T(2,128)(2,1)S(1)} %pad_maximum_fusion.4), channel_id=1, source_target_pairs={{0,2},{1,1},{2,0},{3,3},{4,6},{5,5},{6,4},{7,7},{8,10},{9,9},{10,8... | collective-permute-start | bytes 221192 | tf_op jit(solution)/shard_map/ppermute | solution.py:307
  23.3 0.1 pad_maximum_fusion.1
  23.4 0.3 collective-permute-start.1
  23.7 0.0 collective-permute-done.2
  23.7 0.0 collective-permute-done.3
  23.7 2.4 %collective-permute-done.4 = bf16[2,2,9216]{2,1,0:T(2,128)(2,1)S(1)} collective-permute-done((bf16[2,2,9216]{2,1,0:T(2,128)(2,1)S(1)}, bf16[2,2,9216]{2,1,0:T(2,128)(2,1)S(1)}, u32[]{:S(2)}, u32[]{:S(2)}) %collective-permute-start.4) | collective-permute-done | bytes 73760 | tf_op jit(solution)/shard_map/ppermute | solution.py:307
  26.2 3.5 %collective-permute-done.1 = bf16[2,2,9216]{2,1,0:T(2,128)(2,1)S(1)} collective-permute-done((bf16[2,2,9216]{2,1,0:T(2,128)(2,1)S(1)}, bf16[2,2,9216]{2,1,0:T(2,128)(2,1)S(1)}, u32[]{:S(2)}, u32[]{:S(2)}) %collective-permute-start.1) | collective-permute-done | bytes 73760 | tf_op jit(solution)/shard_map/ppermute | solution.py:307
  29.7 0.5 %pad_maximum_fusion.here_ref = bf16[4,2,2,9216]{3,2,1,0:T(2,128)(2,1)S(1)} fusion(bf16[1,2,2,9216]{3,2,1,0:T(2,128)(2,1)S(1)} %bitcast.18, bf16[1,2,2,9216]{3,2,1,0:T(2,128)(2,1)S(1)} %bitcast.17, bf16[1,2,2,9216]{3,2,1,0:T(2,128)(2,1)S(1)} %bitcast.16, bf16[1,2,2,9216]{3,2,1,0:T(2,128)(2,1)S(1)} %bitcast.19), kind=kLoop, calls=%fused_computation | loop fusion | flops 442368 | bytes 589824 | tf_op jit(solution)/shard_map/stack | solution.py:308
  30.2 0.1 collective-permute-start.5
  30.9 0.9 %collective-permute-done.5.there_ref = bf16[4,2,2,9216]{3,2,1,0:T(2,128)(2,1)S(1)} collective-permute-done((bf16[4,2,2,9216]{3,2,1,0:T(2,128)(2,1)S(1)}, bf16[4,2,2,9216]{3,2,1,0:T(2,128)(2,1)S(1)}, u32[]{:S(2)}, u32[]{:S(2)}) %collective-permute-start.5) | collective-permute-done | bytes 294944 | tf_op jit(solution)/shard_map/ppermute | solution.py:309
  31.8 5.0 %factor_tiles.1 = (bf16[2048,2048]{1,0:T(8,128)(2,1)}, bf16[768,768]{1,0:T(8,128)(2,1)}, bf16[2,1024]{1,0:T(2,128)(2,1)}, bf16[2,768]{1,0:T(2,128)(2,1)}) custom-call(s32[1]{0:T(128)S(6)} %copy.13.count_ref, bf16[4,2,2,9216]{3,2,1,0:T(2,128)(2,1)S(1)} %pad_maximum_fusion.here_ref, bf16[4,2,2,9216]{3,2,1,0:T(2,128)(2,1)S(1)} %collective-permute-done.5.there_ref), custom_call_target="tpu_custom_call" | custom-call | tf_op jit(solution)/shard_map/factor_tiles/pallas_call | solution.py:255
Async XLA Ops:
  0.6 2.2 %copy-start = (bf16[1,2048,1024]{2,1,0:T(8,128)(2,1)S(1)}, bf16[1,2048,1024]{2,1,0:T(8,128)(2,1)}, u32[]{:S(2)}) copy-start(bf16[1,2048,1024]{2,1,0:T(8,128)(2,1)} %param.13) | copy-start | bytes 12582916
  2.8 1.3 %copy-start.1 = (bf16[1,768,768]{2,1,0:T(8,128)(2,1)S(1)}, bf16[1,768,768]{2,1,0:T(8,128)(2,1)}, u32[]{:S(2)}) copy-start(bf16[1,768,768]{2,1,0:T(8,128)(2,1)} %param.14) | copy-start | bytes 3538948
  4.1 1.1 %copy-start.2 = (bf16[24,8,1536]{2,1,0:T(8,128)(2,1)S(1)}, bf16[24,8,1536]{2,1,0:T(8,128)(2,1)}, u32[]{:S(2)}) copy-start(bf16[24,8,1536]{2,1,0:T(8,128)(2,1)} %param.10) | copy-start | bytes 1769476
  5.2 0.9 %copy-start.3 = (bf16[24,4096]{1,0:T(8,128)(2,1)S(1)}, bf16[24,4096]{1,0:T(8,128)(2,1)}, u32[]{:S(2)}) copy-start(bf16[24,4096]{1,0:T(8,128)(2,1)} %tokens_hbm.1) | copy-start | bytes 589828
  6.1 0.8 %copy-start.4 = (bf16[16,2048]{1,0:T(8,128)(2,1)S(1)}, bf16[16,2048]{1,0:T(8,128)(2,1)}, u32[]{:S(2)}) copy-start(bf16[16,2048]{1,0:T(8,128)(2,1)} %qa_hbm.1) | copy-start | bytes 196612
  6.9 0.7 %copy-start.5 = (bf16[16,768]{1,0:T(8,128)(2,1)S(1)}, bf16[16,768]{1,0:T(8,128)(2,1)}, u32[]{:S(2)}) copy-start(bf16[16,768]{1,0:T(8,128)(2,1)} %qg_hbm.1) | copy-start | bytes 73732
  7.7 0.7 %copy-start.6 = (s32[24,8]{0,1:T(8,128)S(1)}, s32[24,8]{0,1:T(8,128)}, u32[]{:S(2)}) copy-start(s32[24,8]{0,1:T(8,128)} %param.11) | copy-start | bytes 2308
  8.4 0.7 %copy-start.7 = (s32[16,1]{0,1:T(1,128)S(1)}, s32[16,1]{0,1:T(1,128)}, u32[]{:S(2)}) copy-start(s32[16,1]{0,1:T(1,128)} %param.17) | copy-start | bytes 196
  12.3 1.5 %collective-permute-start = (bf16[4,2,9216]{2,1,0:T(2,128)(2,1)S(1)}, bf16[4,2,9216]{2,1,0:T(2,128)(2,1)S(1)}, u32[]{:S(2)}, u32[]{:S(2)}) collective-permute-start(bf16[4,2,9216]{2,1,0:T(2,128)(2,1)S(1)} %get-tuple-element.11), channel_id=1, source_target_pairs={{0,1},{1,0},{2,3},{3,2},{4,5},{5,4},{6,7},{7,6},{8,9},{9,8},{10,11... | collective-permute-start | bytes 442376 | tf_op jit(solution)/shard_map/ppermute | solution.py:298
  14.1 9.7 %collective-permute-start.2 = (bf16[2,2,9216]{2,1,0:T(2,128)(2,1)S(1)}, bf16[2,2,9216]{2,1,0:T(2,128)(2,1)S(1)}, u32[]{:S(2)}, u32[]{:S(2)}) collective-permute-start(bf16[2,2,9216]{2,1,0:T(2,128)(2,1)S(1)} %pad_maximum_fusion.2), channel_id=1, source_target_pairs={{0,8},{1,11},{2,10},{3,9},{4,12},{5,15},{6,14},{7,13},{8,0},{9,3},... | collective-permute-start | bytes 221192 | tf_op jit(solution)/shard_map/ppermute | solution.py:307
  18.2 5.6 %collective-permute-start.3 = (bf16[2,2,9216]{2,1,0:T(2,128)(2,1)S(1)}, bf16[2,2,9216]{2,1,0:T(2,128)(2,1)S(1)}, u32[]{:S(2)}, u32[]{:S(2)}) collective-permute-start(bf16[2,2,9216]{2,1,0:T(2,128)(2,1)S(1)} %pad_maximum_fusion.3), channel_id=1, source_target_pairs={{0,4},{1,7},{2,6},{3,5},{4,0},{5,3},{6,2},{7,1},{8,12},{9,15},{10,... | collective-permute-start | bytes 221192 | tf_op jit(solution)/shard_map/ppermute | solution.py:307
  19.9 6.2 %collective-permute-start.4 = (bf16[2,2,9216]{2,1,0:T(2,128)(2,1)S(1)}, bf16[2,2,9216]{2,1,0:T(2,128)(2,1)S(1)}, u32[]{:S(2)}, u32[]{:S(2)}) collective-permute-start(bf16[2,2,9216]{2,1,0:T(2,128)(2,1)S(1)} %pad_maximum_fusion.4), channel_id=1, source_target_pairs={{0,2},{1,1},{2,0},{3,3},{4,6},{5,5},{6,4},{7,7},{8,10},{9,9},{10,8... | collective-permute-start | bytes 221192 | tf_op jit(solution)/shard_map/ppermute | solution.py:307
  23.4 6.2 %collective-permute-start.1 = (bf16[2,2,9216]{2,1,0:T(2,128)(2,1)S(1)}, bf16[2,2,9216]{2,1,0:T(2,128)(2,1)S(1)}, u32[]{:S(2)}, u32[]{:S(2)}) collective-permute-start(bf16[2,2,9216]{2,1,0:T(2,128)(2,1)S(1)} %pad_maximum_fusion.1), channel_id=1, source_target_pairs={{0,12},{1,15},{2,14},{3,13},{4,8},{5,11},{6,10},{7,9},{8,4},{9,7},... | collective-permute-start | bytes 221192 | tf_op jit(solution)/shard_map/ppermute | solution.py:307
  30.2 1.6 %collective-permute-start.5 = (bf16[4,2,2,9216]{3,2,1,0:T(2,128)(2,1)S(1)}, bf16[4,2,2,9216]{3,2,1,0:T(2,128)(2,1)S(1)}, u32[]{:S(2)}, u32[]{:S(2)}) collective-permute-start(bf16[4,2,2,9216]{3,2,1,0:T(2,128)(2,1)S(1)} %pad_maximum_fusion.here_ref), channel_id=1, source_target_pairs={{0,1},{1,0},{2,3},{3,2},{4,5},{5,4},{6,7},{7,6},{8,9},{9,8},{10,11... | collective-permute-start | bytes 884744 | tf_op jit(solution)/shard_map/ppermute | solution.py:309

commit v2 on v1

--- a/solution.py
+++ b/solution.py
@@ -10,7 +10,7 @@
 CAP = 2
 F32 = jnp.float32
 BF16 = jnp.bfloat16
-HBM = pl.BlockSpec(memory_space=pl.ANY)
+HBM = pl.BlockSpec(memory_space=pltpu.HBM)
 VMEM = pl.BlockSpec(memory_space=pltpu.VMEM)
 SMEM = pl.BlockSpec(memory_space=pltpu.SMEM)
 
@@ -169,6 +169,7 @@
     width = tokens.shape[1] + pseudo.shape[1] + row_out * (ba.shape[1] + bg.shape[1])
     out = jax.ShapeDtypeStruct((len(order[0]), CAP, width), BF16)
     operands = (assign, tokens, pseudo, qe, qa, qg, ba, bg)
+    operands = tuple(pltpu.with_memory_space_constraint(x, pltpu.HBM) for x in operands)
     return pl.pallas_call(
         functools.partial(pack_kernel, order, row_out),
         out_shape=(out, out),

time: 37.3 us -> 28.7 us (0.77)
  local copies, waits for them, and re-layouts: 8.56 us -> 0.21 us
    unnamed x16 -> x0, local copies, waits for them, and re-layouts: 8.36 us -> none
where the time goes in v2:
time: 28.7 us; the launch traced here: 28.5 us
  starting transfers between devices  9.93 us (35%)
  Pallas kernels  8.35 us (29%)
  waiting for transfers between devices  7.75 us (27%)
  between operations  1.34 us (5%)
  other arithmetic  0.94 us (3%)
    ppermute x4, starting transfers between devices, local(): lax.ppermute(jnp.stack([keep[r], got[r]]), ('expert', 'dp', 'mp'), pairs)  9.34 us
    ppermute x4, waiting for transfers between devices, local(): lax.ppermute(jnp.stack([keep[r], got[r]]), ('expert', 'dp', 'mp'), pairs)  5.93 us
    pallas_call x1, Pallas kernels, factors(): pl.pallas_call(functools.partial(factor_kernel, act_width, row_out, act_c...  5.03 us
    pallas_call x1, Pallas kernels, pack(): pl.pallas_call(functools.partial(pack_kernel, order, row_out), out_shape=...  3.33 us
    ppermute x1, waiting for transfers between devices, local(): there = lax.ppermute(here, 'mp', swap)  0.92 us
    ppermute x1, waiting for transfers between devices, local(): got = lax.ppermute(give, 'mp', swap)  0.9 us
  transfers between devices with their start and end apart: 6, of which 4 were waited for; matrix products, arithmetic and copies ran while one was open for 1% of the time, Pallas kernels for 0%

profile of v2, /device:TPU:0, one launch (start us, length us, event | category | flops | bytes accessed | tf_op | source)
XLA Modules:
  0.0 28.5 jit_solution(11038610670002991865)
XLA Ops:
  0.6 3.3 %select_rows_and_rotate_queries.1 = (bf16[4,2,9216]{2,1,0:T(2,128)(2,1)S(1)}, bf16[4,2,9216]{2,1,0:T(2,128)(2,1)S(1)}) custom-call(s32[8,24]{1,0:T(8,128)} %bitcast.18, bf16[24,4096]{1,0:T(8,128)(2,1)} %tokens_hbm.1, bf16[192,1536]{1,0:T(8,128)(2,1)} %bitcast.13, s32[1,16]{1,0:T(1,128)} %bitcast.19, bf16[16,2048]{1,0:T(8,128)(2,1)} %qa_hbm.1, ...), custom_call_target="tpu_custom_call" | custom-call | tf_op jit(solution)/shard_map/select_rows_and_rotate_queries/pallas_call | solution.py:173
  4.0 0.5 %collective-permute-start = (bf16[4,2,9216]{2,1,0:T(2,128)(2,1)S(1)}, bf16[4,2,9216]{2,1,0:T(2,128)(2,1)S(1)}, u32[]{:S(2)}, u32[]{:S(2)}) collective-permute-start(bf16[4,2,9216]{2,1,0:T(2,128)(2,1)S(1)} %get-tuple-element.11), channel_id=1, source_target_pairs={{0,1},{1,0},{2,3},{3,2},{4,5},{5,4},{6,7},{7,6},{8,9},{9,8},{10,11... | collective-permute-start | bytes 442376 | tf_op jit(solution)/shard_map/ppermute | solution.py:299
  4.5 0.1 fusion
  4.6 0.9 %collective-permute-done = bf16[4,2,9216]{2,1,0:T(2,128)(2,1)S(1)} collective-permute-done((bf16[4,2,9216]{2,1,0:T(2,128)(2,1)S(1)}, bf16[4,2,9216]{2,1,0:T(2,128)(2,1)S(1)}, u32[]{:S(2)}, u32[]{:S(2)}) %collective-permute-start) | collective-permute-done | bytes 147488 | tf_op jit(solution)/shard_map/ppermute | solution.py:299
  5.5 0.1 fusion.1
  5.6 0.1 pad_maximum_fusion.2
  5.7 4.0 %collective-permute-start.2 = (bf16[2,2,9216]{2,1,0:T(2,128)(2,1)S(1)}, bf16[2,2,9216]{2,1,0:T(2,128)(2,1)S(1)}, u32[]{:S(2)}, u32[]{:S(2)}) collective-permute-start(bf16[2,2,9216]{2,1,0:T(2,128)(2,1)S(1)} %pad_maximum_fusion.2), channel_id=1, source_target_pairs={{0,8},{1,11},{2,10},{3,9},{4,12},{5,15},{6,14},{7,13},{8,0},{9,3},... | collective-permute-start | bytes 221192 | tf_op jit(solution)/shard_map/ppermute | solution.py:308
  9.7 0.1 pad_maximum_fusion.3
  9.8 1.6 %collective-permute-start.3 = (bf16[2,2,9216]{2,1,0:T(2,128)(2,1)S(1)}, bf16[2,2,9216]{2,1,0:T(2,128)(2,1)S(1)}, u32[]{:S(2)}, u32[]{:S(2)}) collective-permute-start(bf16[2,2,9216]{2,1,0:T(2,128)(2,1)S(1)} %pad_maximum_fusion.3), channel_id=1, source_target_pairs={{0,4},{1,7},{2,6},{3,5},{4,0},{5,3},{6,2},{7,1},{8,12},{9,15},{10,... | collective-permute-start | bytes 221192 | tf_op jit(solution)/shard_map/ppermute | solution.py:308
  11.5 0.1 pad_maximum_fusion.4
  11.6 3.4 %collective-permute-start.4 = (bf16[2,2,9216]{2,1,0:T(2,128)(2,1)S(1)}, bf16[2,2,9216]{2,1,0:T(2,128)(2,1)S(1)}, u32[]{:S(2)}, u32[]{:S(2)}) collective-permute-start(bf16[2,2,9216]{2,1,0:T(2,128)(2,1)S(1)} %pad_maximum_fusion.4), channel_id=1, source_target_pairs={{0,2},{1,1},{2,0},{3,3},{4,6},{5,5},{6,4},{7,7},{8,10},{9,9},{10,8... | collective-permute-start | bytes 221192 | tf_op jit(solution)/shard_map/ppermute | solution.py:308
  15.0 0.1 pad_maximum_fusion.1
  15.1 0.3 %collective-permute-start.1 = (bf16[2,2,9216]{2,1,0:T(2,128)(2,1)S(1)}, bf16[2,2,9216]{2,1,0:T(2,128)(2,1)S(1)}, u32[]{:S(2)}, u32[]{:S(2)}) collective-permute-start(bf16[2,2,9216]{2,1,0:T(2,128)(2,1)S(1)} %pad_maximum_fusion.1), channel_id=1, source_target_pairs={{0,12},{1,15},{2,14},{3,13},{4,8},{5,11},{6,10},{7,9},{8,4},{9,7},... | collective-permute-start | bytes 221192 | tf_op jit(solution)/shard_map/ppermute | solution.py:308
  15.4 0.0 collective-permute-done.2
  15.4 0.0 collective-permute-done.3
  15.4 2.4 %collective-permute-done.4 = bf16[2,2,9216]{2,1,0:T(2,128)(2,1)S(1)} collective-permute-done((bf16[2,2,9216]{2,1,0:T(2,128)(2,1)S(1)}, bf16[2,2,9216]{2,1,0:T(2,128)(2,1)S(1)}, u32[]{:S(2)}, u32[]{:S(2)}) %collective-permute-start.4) | collective-permute-done | bytes 73760 | tf_op jit(solution)/shard_map/ppermute | solution.py:308
  17.8 3.5 %collective-permute-done.1 = bf16[2,2,9216]{2,1,0:T(2,128)(2,1)S(1)} collective-permute-done((bf16[2,2,9216]{2,1,0:T(2,128)(2,1)S(1)}, bf16[2,2,9216]{2,1,0:T(2,128)(2,1)S(1)}, u32[]{:S(2)}, u32[]{:S(2)}) %collective-permute-start.1) | collective-permute-done | bytes 73760 | tf_op jit(solution)/shard_map/ppermute | solution.py:308
  21.3 0.5 %pad_maximum_fusion.here_ref = bf16[4,2,2,9216]{3,2,1,0:T(2,128)(2,1)S(1)} fusion(bf16[1,2,2,9216]{3,2,1,0:T(2,128)(2,1)S(1)} %bitcast.16, bf16[1,2,2,9216]{3,2,1,0:T(2,128)(2,1)S(1)} %bitcast.15, bf16[1,2,2,9216]{3,2,1,0:T(2,128)(2,1)S(1)} %bitcast.14, bf16[1,2,2,9216]{3,2,1,0:T(2,128)(2,1)S(1)} %bitcast.17), kind=kLoop, calls=%fused_computation | loop fusion | flops 442368 | bytes 589824 | tf_op jit(solution)/shard_map/stack | solution.py:309
  21.8 0.1 collective-permute-start.5
  22.6 0.9 %collective-permute-done.5.there_ref = bf16[4,2,2,9216]{3,2,1,0:T(2,128)(2,1)S(1)} collective-permute-done((bf16[4,2,2,9216]{3,2,1,0:T(2,128)(2,1)S(1)}, bf16[4,2,2,9216]{3,2,1,0:T(2,128)(2,1)S(1)}, u32[]{:S(2)}, u32[]{:S(2)}) %collective-permute-start.5) | collective-permute-done | bytes 294944 | tf_op jit(solution)/shard_map/ppermute | solution.py:310
  23.5 5.0 %factor_tiles.1 = (bf16[2048,2048]{1,0:T(8,128)(2,1)}, bf16[768,768]{1,0:T(8,128)(2,1)}, bf16[2,1024]{1,0:T(2,128)(2,1)}, bf16[2,768]{1,0:T(2,128)(2,1)}) custom-call(s32[1]{0:T(128)S(6)} %copy.13.count_ref, bf16[4,2,2,9216]{3,2,1,0:T(2,128)(2,1)S(1)} %pad_maximum_fusion.here_ref, bf16[4,2,2,9216]{3,2,1,0:T(2,128)(2,1)S(1)} %collective-permute-done.5.there_ref), custom_call_target="tpu_custom_call" | custom-call | tf_op jit(solution)/shard_map/factor_tiles/pallas_call | solution.py:256
Async XLA Ops:
  4.0 1.5 %collective-permute-start = (bf16[4,2,9216]{2,1,0:T(2,128)(2,1)S(1)}, bf16[4,2,9216]{2,1,0:T(2,128)(2,1)S(1)}, u32[]{:S(2)}, u32[]{:S(2)}) collective-permute-start(bf16[4,2,9216]{2,1,0:T(2,128)(2,1)S(1)} %get-tuple-element.11), channel_id=1, source_target_pairs={{0,1},{1,0},{2,3},{3,2},{4,5},{5,4},{6,7},{7,6},{8,9},{9,8},{10,11... | collective-permute-start | bytes 442376 | tf_op jit(solution)/shard_map/ppermute | solution.py:299
  5.7 9.7 %collective-permute-start.2 = (bf16[2,2,9216]{2,1,0:T(2,128)(2,1)S(1)}, bf16[2,2,9216]{2,1,0:T(2,128)(2,1)S(1)}, u32[]{:S(2)}, u32[]{:S(2)}) collective-permute-start(bf16[2,2,9216]{2,1,0:T(2,128)(2,1)S(1)} %pad_maximum_fusion.2), channel_id=1, source_target_pairs={{0,8},{1,11},{2,10},{3,9},{4,12},{5,15},{6,14},{7,13},{8,0},{9,3},... | collective-permute-start | bytes 221192 | tf_op jit(solution)/shard_map/ppermute | solution.py:308
  9.8 5.6 %collective-permute-start.3 = (bf16[2,2,9216]{2,1,0:T(2,128)(2,1)S(1)}, bf16[2,2,9216]{2,1,0:T(2,128)(2,1)S(1)}, u32[]{:S(2)}, u32[]{:S(2)}) collective-permute-start(bf16[2,2,9216]{2,1,0:T(2,128)(2,1)S(1)} %pad_maximum_fusion.3), channel_id=1, source_target_pairs={{0,4},{1,7},{2,6},{3,5},{4,0},{5,3},{6,2},{7,1},{8,12},{9,15},{10,... | collective-permute-start | bytes 221192 | tf_op jit(solution)/shard_map/ppermute | solution.py:308
  11.6 6.2 %collective-permute-start.4 = (bf16[2,2,9216]{2,1,0:T(2,128)(2,1)S(1)}, bf16[2,2,9216]{2,1,0:T(2,128)(2,1)S(1)}, u32[]{:S(2)}, u32[]{:S(2)}) collective-permute-start(bf16[2,2,9216]{2,1,0:T(2,128)(2,1)S(1)} %pad_maximum_fusion.4), channel_id=1, source_target_pairs={{0,2},{1,1},{2,0},{3,3},{4,6},{5,5},{6,4},{7,7},{8,10},{9,9},{10,8... | collective-permute-start | bytes 221192 | tf_op jit(solution)/shard_map/ppermute | solution.py:308
  15.1 6.2 %collective-permute-start.1 = (bf16[2,2,9216]{2,1,0:T(2,128)(2,1)S(1)}, bf16[2,2,9216]{2,1,0:T(2,128)(2,1)S(1)}, u32[]{:S(2)}, u32[]{:S(2)}) collective-permute-start(bf16[2,2,9216]{2,1,0:T(2,128)(2,1)S(1)} %pad_maximum_fusion.1), channel_id=1, source_target_pairs={{0,12},{1,15},{2,14},{3,13},{4,8},{5,11},{6,10},{7,9},{8,4},{9,7},... | collective-permute-start | bytes 221192 | tf_op jit(solution)/shard_map/ppermute | solution.py:308
  21.8 1.6 %collective-permute-start.5 = (bf16[4,2,2,9216]{3,2,1,0:T(2,128)(2,1)S(1)}, bf16[4,2,2,9216]{3,2,1,0:T(2,128)(2,1)S(1)}, u32[]{:S(2)}, u32[]{:S(2)}) collective-permute-start(bf16[4,2,2,9216]{3,2,1,0:T(2,128)(2,1)S(1)} %pad_maximum_fusion.here_ref), channel_id=1, source_target_pairs={{0,1},{1,0},{2,3},{3,2},{4,5},{5,4},{6,7},{7,6},{8,9},{9,8},{10,11... | collective-permute-start | bytes 884744 | tf_op jit(solution)/shard_map/ppermute | solution.py:310

commit v3 on v2

--- a/solution.py
+++ b/solution.py
@@ -16,12 +16,13 @@
 
 
 def partner_order(experts, blocks):
-    away = [(de, dd) for dd in range(blocks) for de in range(experts - 1, 0, -1)]
-    away += [(0, dd) for dd in range(1, blocks)] + [(0, 0)]
-    half = experts * blocks // 2
-    near = [p for p in away if p[1] == 0 and p[0] > 0] + [p for p in away if p[0] == 0 and p[1] > 0]
-    far = [p for p in away if p not in near and p != (0, 0)] + [(0, 0)]
-    order = (near + far)[:half], (near + far)[half:]
+    far = list(range(experts // 2, experts)) + list(range(experts // 2 - 1, 0, -1))
+    order = [], []
+    for de in far:
+        for dd in range(blocks):
+            order[dd % 2].append((de, dd))
+    for i in range(blocks):
+        order[i % 2].append((0, (i + 1) % blocks))
     return order
 
 
@@ -182,96 +183,80 @@
     )(*operands)
 
 
-def factor_kernel(
-    act_width,
-    row_out,
-    act_cols,
-    count_ref,
-    here_ref,
-    there_ref,
-    act_hbm,
-    grad_hbm,
-    rot_act_ref,
-    rot_grad_ref,
-    rows_ref,
-    act_ref,
-    grad_ref,
-    sems,
-):
+def row_steps(rows):
+    return [(i * 128, 64 if i < 2 else 128) for i in range(rows // 128)]
+
+
+def factor_kernel(act_width, row_out, rounds, count_ref, *refs):
+    here, there = refs[:rounds], refs[rounds : 2 * rounds]
+    act_hbm, grad_hbm, rot_act_hbm, rot_grad_hbm = refs[2 * rounds : 2 * rounds + 4]
+    right_ref, act_ref, grad_ref, rot_act_ref, rot_grad_ref, sems = refs[2 * rounds + 4 :]
     block, core = lax.axis_index("dp"), lax.axis_index("mp")
-    half = here_ref.shape[0]
     act_block, act_half = act_ref.shape
     grad_block, grad_half = grad_ref.shape
-    wide = act_width + 2 * grad_half
     inverse = 1.0 / count_ref[0].astype(F32)
-    pieces = []
-    for ref in (here_ref, there_ref):
-        for i in range(half):
-            for c in range(2):
-                pieces.append(ref[i, c, :, :wide])
-    rows_ref[...] = jnp.concatenate(pieces, axis=0)
-
     contract = (((0,), (0,)), ((), ()))
-    grad_left = rows_ref[:, pl.ds(pl.multiple_of(act_width + block * grad_block, 128), grad_block)]
-    grad_right = rows_ref[:, pl.ds(pl.multiple_of(act_width + core * grad_half, 128), grad_half)]
-    grad_sum = lax.dot_general(grad_left, grad_right, contract, preferred_element_type=F32)
-    grad_ref[...] = (grad_sum * inverse).astype(BF16)
-    grad_copy = pltpu.make_async_copy(grad_ref, grad_hbm, sems.at[0])
-    grad_copy.start()
-
-    step = 256
-    count = act_block // step
-    right = rows_ref[:, pl.ds(pl.multiple_of(core * act_half, 128), act_half)]
     copies = []
-    for i in range(count):
-        at = pl.multiple_of(block * act_block + i * step, 128)
-        left = rows_ref[:, pl.ds(at, step)]
-        part = lax.dot_general(left, right, contract, preferred_element_type=F32)
-        act_ref[i * step : (i + 1) * step, :] = (part * inverse).astype(BF16)
-        copy = pltpu.make_async_copy(
-            act_ref.at[pl.ds(i * step, step)], act_hbm.at[pl.ds(i * step, step)], sems.at[1 + i]
-        )
+
+    def send(src, dst):
+        copy = pltpu.make_async_copy(src, dst, sems.at[len(copies)])
         copy.start()
         copies.append(copy)
 
+    def columns(at, width):
+        span = pl.ds(pl.multiple_of(at, 128), width)
+        return jnp.concatenate([ref[c, :, span] for ref in here + there for c in range(2)], axis=0)
+
+    def tile(left, right):
+        part = lax.dot_general(left, right, contract, preferred_element_type=F32)
+        return (part * inverse).astype(BF16)
+
+    right_ref[...] = columns(core * act_half, act_half)
+    for first, step in row_steps(act_block):
+        left = columns(block * act_block + first, 128)
+        for at in range(0, 128, step):
+            rows = pl.ds(first + at, step)
+            act_ref[rows, :] = tile(left[:, at : at + step], right_ref[...])
+            send(act_ref.at[rows], act_hbm.at[rows])
+
+    grad_ref[...] = tile(
+        columns(act_width + block * grad_block, grad_block),
+        columns(act_width + core * grad_half, grad_half),
+    )
+    send(grad_ref, grad_hbm)
+
+    act_cols = rot_act_ref.shape[1]
     cols = act_cols + rot_grad_ref.shape[1]
     for i in range(row_out // 2):
-        at = wide + i * 2 * cols
+        at = act_width + 2 * grad_half + i * 2 * cols
         total = jnp.zeros((2, cols), F32)
-        for ref, c in ((here_ref, 0), (there_ref, 1)):
-            for r in range(half):
-                high = ref[r, c, :, at : at + cols].astype(F32)
-                low = ref[r, c, :, at + cols : at + 2 * cols].astype(F32)
+        for group, c in ((here, 0), (there, 1)):
+            for ref in group:
+                high = ref[c, :, at : at + cols].astype(F32)
+                low = ref[c, :, at + cols : at + 2 * cols].astype(F32)
                 total += high + low
         rot_act_ref[2 * i : 2 * i + 2, :] = total[:, :act_cols].astype(BF16)
         rot_grad_ref[2 * i : 2 * i + 2, :] = total[:, act_cols:].astype(BF16)
-    grad_copy.wait()
+    send(rot_act_ref, rot_act_hbm)
+    send(rot_grad_ref, rot_grad_hbm)
     for copy in copies:
         copy.wait()
 
 
 def factors(act_width, row_out, act_tile, grad_tile, act_cols, grad_cols, counts, here, there):
-    rows = 2 * here.shape[0] * here.shape[1] * here.shape[2]
-    wide = act_width + 2 * grad_tile[1]
+    rounds = len(here)
+    shapes = (act_tile, grad_tile, (row_out, act_cols), (row_out, grad_cols))
     return pl.pallas_call(
-        functools.partial(factor_kernel, act_width, row_out, act_cols),
-        out_shape=(
-            jax.ShapeDtypeStruct(act_tile, BF16),
-            jax.ShapeDtypeStruct(grad_tile, BF16),
-            jax.ShapeDtypeStruct((row_out, act_cols), BF16),
-            jax.ShapeDtypeStruct((row_out, grad_cols), BF16),
-        ),
-        in_specs=[SMEM, VMEM, VMEM],
-        out_specs=(HBM, HBM, VMEM, VMEM),
-        scratch_shapes=[
-            pltpu.VMEM((rows, wide), BF16),
-            pltpu.VMEM(act_tile, BF16),
-            pltpu.VMEM(grad_tile, BF16),
-            pltpu.SemaphoreType.DMA((1 + act_tile[0] // 256,)),
-        ],
+        functools.partial(factor_kernel, act_width, row_out, rounds),
+        out_shape=tuple(jax.ShapeDtypeStruct(shape, BF16) for shape in shapes),
+        in_specs=[SMEM] + [VMEM] * (2 * rounds),
+        out_specs=(HBM,) * 4,
+        scratch_shapes=[pltpu.VMEM((2 * 2 * CAP * rounds, act_tile[1]), BF16)]
+        + [pltpu.VMEM(shape, BF16) for shape in shapes]
+        + [pltpu.SemaphoreType.DMA((act_tile[0] // 128 + 5,))],
         compiler_params=pltpu.CompilerParams(vmem_limit_bytes=40 * 1024 * 1024),
         name="factor_tiles",
-    )(counts, here, there)
+    )(counts, *here, *there)
 
 
 def local(
@@ -306,8 +291,7 @@
             for m in range(2)
         ]
         arrived.append(lax.ppermute(jnp.stack([keep[r], got[r]]), ("expert", "dp", "mp"), pairs))
-    here = jnp.stack(arrived)
-    there = lax.ppermute(here, "mp", swap)
+    there = [lax.ppermute(block, "mp", swap) for block in arrived]
     act_cov, grad_cov, rot_act, rot_grad = factors(
         d_model,
         row_out,
@@ -316,7 +300,7 @@
         basis_act.shape[2],
         basis_grad.shape[2],
         counts,
-        here,
+        arrived,
         there,
     )
     return act_cov[None], grad_cov[None], rot_act, rot_grad

time: 28.7 us -> 23.9 us (0.83)
  waiting for transfers between devices: 7.75 us -> 3.98 us
  Pallas kernels: 8.35 us -> 7.44 us
  other arithmetic: 0.94 us -> 0.41 us
  starting transfers between devices: 9.93 us -> 10.3 us
    ppermute x4, waiting for transfers between devices: 5.93 us -> 2.58 us  [local(): lax.ppermute(jnp.stack([keep[r], got[r]]), ('expert', 'dp', 'mp'), pairs)]
    pallas_call x1, Pallas kernels: 5.03 us -> 4.11 us  [factors(): pl.pallas_call(functools.partial(factor_kernel, act_width, row_out, round...]
    ppermute x1 -> x4, starting transfers between devices: 0.07 us -> 0.68 us  [local(): there = [lax.ppermute(block, 'mp', swap) for block in arrived]]
    another operation x1 -> x0, other arithmetic: 0.53 us -> none  [local(): here = jnp.stack(arrived)]
    ppermute x1 -> x4, waiting for transfers between devices: 0.92 us -> 0.5 us  [local(): there = [lax.ppermute(block, 'mp', swap) for block in arrived]]
  transfers between devices with their start and end apart: 6 -> 9, of which waited for: 4 -> 6; matrix products, arithmetic and copies ran while one was open for 1% -> 2% of each run, Pallas kernels for 0% -> 0%
where the time goes in v3:
time: 23.9 us; the launch traced here: 23.7 us
  starting transfers between devices  10.3 us (43%)
  Pallas kernels  7.44 us (31%)
  waiting for transfers between devices  3.98 us (17%)
  between operations  1.36 us (6%)
  other arithmetic  0.41 us (2%)
    ppermute x4, starting transfers between devices, local(): lax.ppermute(jnp.stack([keep[r], got[r]]), ('expert', 'dp', 'mp'), pairs)  9.14 us
    pallas_call x1, Pallas kernels, factors(): pl.pallas_call(functools.partial(factor_kernel, act_width, row_out, round...  4.11 us
    pallas_call x1, Pallas kernels, pack(): pl.pallas_call(functools.partial(pack_kernel, order, row_out), out_shape=...  3.33 us
    ppermute x4, waiting for transfers between devices, local(): lax.ppermute(jnp.stack([keep[r], got[r]]), ('expert', 'dp', 'mp'), pairs)  2.58 us
    ppermute x1, waiting for transfers between devices, local(): got = lax.ppermute(give, 'mp', swap)  0.9 us
    ppermute x4, starting transfers between devices, local(): there = [lax.ppermute(block, 'mp', swap) for block in arrived]  0.68 us
    ppermute x1, starting transfers between devices, local(): got = lax.ppermute(give, 'mp', swap)  0.52 us
    ppermute x4, waiting for transfers between devices, local(): there = [lax.ppermute(block, 'mp', swap) for block in arrived]  0.5 us
  transfers between devices with their start and end apart: 9, of which 6 were waited for; matrix products, arithmetic and copies ran while one was open for 2% of the time, Pallas kernels for 0%

profile of v3, /device:TPU:0, one launch (start us, length us, event | category | flops | bytes accessed | tf_op | source)
XLA Modules:
  0.0 23.7 jit_solution(12604796974683911653)
XLA Ops:
  0.6 3.3 %select_rows_and_rotate_queries.1 = (bf16[4,2,9216]{2,1,0:T(2,128)(2,1)S(1)}, bf16[4,2,9216]{2,1,0:T(2,128)(2,1)S(1)}) custom-call(s32[8,24]{1,0:T(8,128)} %bitcast.10, bf16[24,4096]{1,0:T(8,128)(2,1)} %tokens_hbm.1, bf16[192,1536]{1,0:T(8,128)(2,1)} %bitcast.9, s32[1,16]{1,0:T(1,128)} %bitcast.11, bf16[16,2048]{1,0:T(8,128)(2,1)} %qa_hbm.1, ...), custom_call_target="tpu_custom_call" | custom-call | tf_op jit(solution)/shard_map/select_rows_and_rotate_queries/pallas_call | solution.py:174
  4.0 0.5 %collective-permute-start = (bf16[4,2,9216]{2,1,0:T(2,128)(2,1)S(1)}, bf16[4,2,9216]{2,1,0:T(2,128)(2,1)S(1)}, u32[]{:S(2)}, u32[]{:S(2)}) collective-permute-start(bf16[4,2,9216]{2,1,0:T(2,128)(2,1)S(1)} %get-tuple-element.11), channel_id=1, source_target_pairs={{0,1},{1,0},{2,3},{3,2},{4,5},{5,4},{6,7},{7,6},{8,9},{9,8},{10,11... | collective-permute-start | bytes 442376 | tf_op jit(solution)/shard_map/ppermute | solution.py:284
  4.5 0.1 fusion
  4.6 0.9 %collective-permute-done = bf16[4,2,9216]{2,1,0:T(2,128)(2,1)S(1)} collective-permute-done((bf16[4,2,9216]{2,1,0:T(2,128)(2,1)S(1)}, bf16[4,2,9216]{2,1,0:T(2,128)(2,1)S(1)}, u32[]{:S(2)}, u32[]{:S(2)}) %collective-permute-start) | collective-permute-done | bytes 147488 | tf_op jit(solution)/shard_map/ppermute | solution.py:284
  5.5 0.1 fusion.1
  5.6 0.1 pad_maximum_fusion
  5.7 4.0 %collective-permute-start.1 = (bf16[2,2,9216]{2,1,0:T(2,128)(2,1)S(1)}, bf16[2,2,9216]{2,1,0:T(2,128)(2,1)S(1)}, u32[]{:S(2)}, u32[]{:S(2)}) collective-permute-start(bf16[2,2,9216]{2,1,0:T(2,128)(2,1)S(1)} %pad_maximum_fusion), channel_id=1, source_target_pairs={{0,8},{1,11},{2,10},{3,9},{4,12},{5,15},{6,14},{7,13},{8,0},{9,3},... | collective-permute-start | bytes 221192 | tf_op jit(solution)/shard_map/ppermute | solution.py:293
  9.7 0.1 pad_maximum_fusion.1
  9.8 1.4 %collective-permute-start.2 = (bf16[2,2,9216]{2,1,0:T(2,128)(2,1)S(1)}, bf16[2,2,9216]{2,1,0:T(2,128)(2,1)S(1)}, u32[]{:S(2)}, u32[]{:S(2)}) collective-permute-start(bf16[2,2,9216]{2,1,0:T(2,128)(2,1)S(1)} %pad_maximum_fusion.1), channel_id=1, source_target_pairs={{0,12},{1,15},{2,14},{3,13},{4,8},{5,11},{6,10},{7,9},{8,4},{9,7},... | collective-permute-start | bytes 221192 | tf_op jit(solution)/shard_map/ppermute | solution.py:293
  11.2 0.1 pad_maximum_fusion.2
  11.3 0.3 %collective-permute-start.3 = (bf16[2,2,9216]{2,1,0:T(2,128)(2,1)S(1)}, bf16[2,2,9216]{2,1,0:T(2,128)(2,1)S(1)}, u32[]{:S(2)}, u32[]{:S(2)}) collective-permute-start(bf16[2,2,9216]{2,1,0:T(2,128)(2,1)S(1)} %pad_maximum_fusion.2), channel_id=1, source_target_pairs={{0,4},{1,7},{2,6},{3,5},{4,0},{5,3},{6,2},{7,1},{8,12},{9,15},{10,... | collective-permute-start | bytes 221192 | tf_op jit(solution)/shard_map/ppermute | solution.py:293
  11.7 0.1 pad_maximum_fusion.3
  11.8 3.4 %collective-permute-start.4 = (bf16[2,2,9216]{2,1,0:T(2,128)(2,1)S(1)}, bf16[2,2,9216]{2,1,0:T(2,128)(2,1)S(1)}, u32[]{:S(2)}, u32[]{:S(2)}) collective-permute-start(bf16[2,2,9216]{2,1,0:T(2,128)(2,1)S(1)} %pad_maximum_fusion.3), channel_id=1, source_target_pairs={{0,2},{1,1},{2,0},{3,3},{4,6},{5,5},{6,4},{7,7},{8,10},{9,9},{10,8... | collective-permute-start | bytes 221192 | tf_op jit(solution)/shard_map/ppermute | solution.py:293
  15.2 0.0 collective-permute-done.1.refs_0_
  15.2 0.1 collective-permute-start.5
  15.3 1.5 %collective-permute-done.2.refs_1_ = bf16[2,2,9216]{2,1,0:T(2,128)(2,1)S(1)} collective-permute-done((bf16[2,2,9216]{2,1,0:T(2,128)(2,1)S(1)}, bf16[2,2,9216]{2,1,0:T(2,128)(2,1)S(1)}, u32[]{:S(2)}, u32[]{:S(2)}) %collective-permute-start.2) | collective-permute-done | bytes 73760 | tf_op jit(solution)/shard_map/ppermute | solution.py:293
  16.8 0.5 %collective-permute-start.6 = (bf16[2,2,9216]{2,1,0:T(2,128)(2,1)S(1)}, bf16[2,2,9216]{2,1,0:T(2,128)(2,1)S(1)}, u32[]{:S(2)}, u32[]{:S(2)}) collective-permute-start(bf16[2,2,9216]{2,1,0:T(2,128)(2,1)S(1)} %collective-permute-done.2.refs_1_), channel_id=1, source_target_pairs={{0,1},{1,0},{2,3},{3,2},{4,5},{5,4},{6,7},{7,6},{8,9},{9,8},{10,11... | collective-permute-start | bytes 221192 | tf_op jit(solution)/shard_map/ppermute | solution.py:294
  17.3 0.7 %collective-permute-done.3.refs_2_ = bf16[2,2,9216]{2,1,0:T(2,128)(2,1)S(1)} collective-permute-done((bf16[2,2,9216]{2,1,0:T(2,128)(2,1)S(1)}, bf16[2,2,9216]{2,1,0:T(2,128)(2,1)S(1)}, u32[]{:S(2)}, u32[]{:S(2)}) %collective-permute-start.3) | collective-permute-done | bytes 73760 | tf_op jit(solution)/shard_map/ppermute | solution.py:293
  17.9 0.0 collective-permute-start.7
  17.9 0.4 %collective-permute-done.4.refs_3_ = bf16[2,2,9216]{2,1,0:T(2,128)(2,1)S(1)} collective-permute-done((bf16[2,2,9216]{2,1,0:T(2,128)(2,1)S(1)}, bf16[2,2,9216]{2,1,0:T(2,128)(2,1)S(1)}, u32[]{:S(2)}, u32[]{:S(2)}) %collective-permute-start.4) | collective-permute-done | bytes 73760 | tf_op jit(solution)/shard_map/ppermute | solution.py:293
  18.4 0.1 collective-permute-start.8
  19.1 0.0 collective-permute-done.5.refs_4_
  19.1 0.0 collective-permute-done.6.refs_5_
  19.1 0.1 collective-permute-done.7.refs_6_
  19.2 0.4 %collective-permute-done.8.refs_7_ = bf16[2,2,9216]{2,1,0:T(2,128)(2,1)S(1)} collective-permute-done((bf16[2,2,9216]{2,1,0:T(2,128)(2,1)S(1)}, bf16[2,2,9216]{2,1,0:T(2,128)(2,1)S(1)}, u32[]{:S(2)}, u32[]{:S(2)}) %collective-permute-start.8) | collective-permute-done | bytes 73760 | tf_op jit(solution)/shard_map/ppermute | solution.py:294
  19.6 4.1 %factor_tiles.1 = (bf16[2048,2048]{1,0:T(8,128)(2,1)}, bf16[768,768]{1,0:T(8,128)(2,1)}, bf16[2,1024]{1,0:T(2,128)(2,1)}, bf16[2,768]{1,0:T(2,128)(2,1)}) custom-call(s32[1]{0:T(128)S(6)} %copy.13.count_ref, bf16[2,2,9216]{2,1,0:T(2,128)(2,1)S(1)} %collective-permute-done.1.refs_0_, bf16[2,2,9216]{2,1,0:T(2,128)(2,1)S(1)} %collective-permute-done.2.refs_1_, ...), custom_call_target="tpu_custom_call" | custom-call | tf_op jit(solution)/shard_map/factor_tiles/pallas_call | solution.py:249
Async XLA Ops:
  4.0 1.5 %collective-permute-start = (bf16[4,2,9216]{2,1,0:T(2,128)(2,1)S(1)}, bf16[4,2,9216]{2,1,0:T(2,128)(2,1)S(1)}, u32[]{:S(2)}, u32[]{:S(2)}) collective-permute-start(bf16[4,2,9216]{2,1,0:T(2,128)(2,1)S(1)} %get-tuple-element.11), channel_id=1, source_target_pairs={{0,1},{1,0},{2,3},{3,2},{4,5},{5,4},{6,7},{7,6},{8,9},{9,8},{10,11... | collective-permute-start | bytes 442376 | tf_op jit(solution)/shard_map/ppermute | solution.py:284
  5.7 9.5 %collective-permute-start.1 = (bf16[2,2,9216]{2,1,0:T(2,128)(2,1)S(1)}, bf16[2,2,9216]{2,1,0:T(2,128)(2,1)S(1)}, u32[]{:S(2)}, u32[]{:S(2)}) collective-permute-start(bf16[2,2,9216]{2,1,0:T(2,128)(2,1)S(1)} %pad_maximum_fusion), channel_id=1, source_target_pairs={{0,8},{1,11},{2,10},{3,9},{4,12},{5,15},{6,14},{7,13},{8,0},{9,3},... | collective-permute-start | bytes 221192 | tf_op jit(solution)/shard_map/ppermute | solution.py:293
  9.8 6.9 %collective-permute-start.2 = (bf16[2,2,9216]{2,1,0:T(2,128)(2,1)S(1)}, bf16[2,2,9216]{2,1,0:T(2,128)(2,1)S(1)}, u32[]{:S(2)}, u32[]{:S(2)}) collective-permute-start(bf16[2,2,9216]{2,1,0:T(2,128)(2,1)S(1)} %pad_maximum_fusion.1), channel_id=1, source_target_pairs={{0,12},{1,15},{2,14},{3,13},{4,8},{5,11},{6,10},{7,9},{8,4},{9,7},... | collective-permute-start | bytes 221192 | tf_op jit(solution)/shard_map/ppermute | solution.py:293
  11.3 6.6 %collective-permute-start.3 = (bf16[2,2,9216]{2,1,0:T(2,128)(2,1)S(1)}, bf16[2,2,9216]{2,1,0:T(2,128)(2,1)S(1)}, u32[]{:S(2)}, u32[]{:S(2)}) collective-permute-start(bf16[2,2,9216]{2,1,0:T(2,128)(2,1)S(1)} %pad_maximum_fusion.2), channel_id=1, source_target_pairs={{0,4},{1,7},{2,6},{3,5},{4,0},{5,3},{6,2},{7,1},{8,12},{9,15},{10,... | collective-permute-start | bytes 221192 | tf_op jit(solution)/shard_map/ppermute | solution.py:293
  11.8 6.6 %collective-permute-start.4 = (bf16[2,2,9216]{2,1,0:T(2,128)(2,1)S(1)}, bf16[2,2,9216]{2,1,0:T(2,128)(2,1)S(1)}, u32[]{:S(2)}, u32[]{:S(2)}) collective-permute-start(bf16[2,2,9216]{2,1,0:T(2,128)(2,1)S(1)} %pad_maximum_fusion.3), channel_id=1, source_target_pairs={{0,2},{1,1},{2,0},{3,3},{4,6},{5,5},{6,4},{7,7},{8,10},{9,9},{10,8... | collective-permute-start | bytes 221192 | tf_op jit(solution)/shard_map/ppermute | solution.py:293
  15.2 3.9 %collective-permute-start.5 = (bf16[2,2,9216]{2,1,0:T(2,128)(2,1)S(1)}, bf16[2,2,9216]{2,1,0:T(2,128)(2,1)S(1)}, u32[]{:S(2)}, u32[]{:S(2)}) collective-permute-start(bf16[2,2,9216]{2,1,0:T(2,128)(2,1)S(1)} %collective-permute-done.1.refs_0_), channel_id=1, source_target_pairs={{0,1},{1,0},{2,3},{3,2},{4,5},{5,4},{6,7},{7,6},{8,9},{9,8},{10,11... | collective-permute-start | bytes 221192 | tf_op jit(solution)/shard_map/ppermute | solution.py:294
  16.8 2.3 %collective-permute-start.6 = (bf16[2,2,9216]{2,1,0:T(2,128)(2,1)S(1)}, bf16[2,2,9216]{2,1,0:T(2,128)(2,1)S(1)}, u32[]{:S(2)}, u32[]{:S(2)}) collective-permute-start(bf16[2,2,9216]{2,1,0:T(2,128)(2,1)S(1)} %collective-permute-done.2.refs_1_), channel_id=1, source_target_pairs={{0,1},{1,0},{2,3},{3,2},{4,5},{5,4},{6,7},{7,6},{8,9},{9,8},{10,11... | collective-permute-start | bytes 221192 | tf_op jit(solution)/shard_map/ppermute | solution.py:294
  17.9 1.3 %collective-permute-start.7 = (bf16[2,2,9216]{2,1,0:T(2,128)(2,1)S(1)}, bf16[2,2,9216]{2,1,0:T(2,128)(2,1)S(1)}, u32[]{:S(2)}, u32[]{:S(2)}) collective-permute-start(bf16[2,2,9216]{2,1,0:T(2,128)(2,1)S(1)} %collective-permute-done.3.refs_2_), channel_id=1, source_target_pairs={{0,1},{1,0},{2,3},{3,2},{4,5},{5,4},{6,7},{7,6},{8,9},{9,8},{10,11... | collective-permute-start | bytes 221192 | tf_op jit(solution)/shard_map/ppermute | solution.py:294
  18.4 1.3 %collective-permute-start.8 = (bf16[2,2,9216]{2,1,0:T(2,128)(2,1)S(1)}, bf16[2,2,9216]{2,1,0:T(2,128)(2,1)S(1)}, u32[]{:S(2)}, u32[]{:S(2)}) collective-permute-start(bf16[2,2,9216]{2,1,0:T(2,128)(2,1)S(1)} %collective-permute-done.4.refs_3_), channel_id=1, source_target_pairs={{0,1},{1,0},{2,3},{3,2},{4,5},{5,4},{6,7},{7,6},{8,9},{9,8},{10,11... | collective-permute-start | bytes 221192 | tf_op jit(solution)/shard_map/ppermute | solution.py:294

commit v4 on v3

--- a/solution.py
+++ b/solution.py
@@ -8,6 +8,7 @@
 from jax.sharding import PartitionSpec as P
 
 CAP = 2
+CHUNKS = 8
 F32 = jnp.float32
 BF16 = jnp.bfloat16
 HBM = pl.BlockSpec(memory_space=pltpu.HBM)
@@ -50,19 +51,12 @@
     qg_hbm,
     ba_hbm,
     bg_hbm,
-    keep_ref,
-    give_ref,
-    assign_ref,
-    tokens_ref,
-    pseudo_ref,
-    qe_ref,
-    qa_ref,
-    qg_ref,
-    ba_ref,
-    bg_ref,
-    sems,
+    *refs,
 ):
-    chunks = 4
+    half = len(order[0])
+    send_refs, give_ref = refs[:half], refs[half]
+    assign_ref, tokens_ref, pseudo_ref, qe_ref, qa_ref, qg_ref, ba_ref, bg_ref, sems = refs[half + 1 :]
+    chunks = CHUNKS
     deep = ba_ref.shape[0] // chunks
     small = [
         pltpu.make_async_copy(src, dst, sems.at[i])
@@ -87,7 +81,6 @@
     for copy in small + large:
         copy.start()
     expert, block, core = lax.axis_index("expert"), lax.axis_index("dp"), lax.axis_index("mp")
-    half = len(order[0])
     rows = 4 * half
     blocks = 1 + max(dd for _, dd in order[0] + order[1])
     slots, toks = assign_ref.shape
@@ -123,7 +116,7 @@
         value = value.astype(BF16)
         width = value.shape[1]
         for i in range(half):
-            keep_ref[i, :, column : column + width] = value[2 * i : 2 * i + 2]
+            send_refs[i][0, :, column : column + width] = value[2 * i : 2 * i + 2]
             give_ref[i, :, column : column + width] = value[2 * (half + i) : 2 * (half + i) + 2]
 
     small[4].wait()
@@ -146,38 +139,39 @@
     pick = jnp.concatenate(picks, axis=0) if len(picks) > 1 else picks[0]
     my_act = dot(pick, qa_ref[...]).astype(BF16)
     my_grad = dot(pick, qg_ref[...]).astype(BF16)
+    width = 2 * (act_cols + grad_cols)
+
+    def put_pair(column, value):
+        high = value.astype(BF16)
+        low = value - high.astype(F32)
+        for i in range(row_out // 2):
+            cut = slice(i * rows, (i + 1) * rows)
+            put(base + i * width + column, high[cut])
+            put(base + i * width + column + act_cols + grad_cols, low[cut])
+
     small[6].wait()
-    grad_part = dot(my_grad, bg_ref[...])
+    put_pair(act_cols, dot(my_grad, bg_ref[...]))
     act_part = jnp.zeros((my_act.shape[0], act_cols), F32)
     for c in range(chunks):
         large[c].wait()
         act_part += dot(my_act[:, c * deep : (c + 1) * deep], ba_ref[c * deep : (c + 1) * deep])
-    act_high = act_part.astype(BF16)
-    grad_high = grad_part.astype(BF16)
-    act_low = act_part - act_high.astype(F32)
-    grad_low = grad_part - grad_high.astype(F32)
-    width = 2 * (act_cols + grad_cols)
-    for i in range(row_out // 2):
-        cut = slice(i * rows, (i + 1) * rows)
-        at = base + i * width
-        put(at, act_high[cut])
-        put(at + act_cols, grad_high[cut])
-        put(at + act_cols + grad_cols, act_low[cut])
-        put(at + 2 * act_cols + grad_cols, grad_low[cut])
+    put_pair(0, act_part)
 
 
 def pack(order, row_out, assign, tokens, pseudo, qe, qa, qg, ba, bg):
     width = tokens.shape[1] + pseudo.shape[1] + row_out * (ba.shape[1] + bg.shape[1])
-    out = jax.ShapeDtypeStruct((len(order[0]), CAP, width), BF16)
+    half = len(order[0])
+    send = jax.ShapeDtypeStruct((2, CAP, width), BF16)
+    give = jax.ShapeDtypeStruct((half, CAP, width), BF16)
     operands = (assign, tokens, pseudo, qe, qa, qg, ba, bg)
     operands = tuple(pltpu.with_memory_space_constraint(x, pltpu.HBM) for x in operands)
     return pl.pallas_call(
         functools.partial(pack_kernel, order, row_out),
-        out_shape=(out, out),
+        out_shape=(send,) * half + (give,),
         in_specs=[HBM] * len(operands),
-        out_specs=(VMEM, VMEM),
+        out_specs=(VMEM,) * (half + 1),
         scratch_shapes=[pltpu.VMEM(x.shape, x.dtype) for x in operands]
-        + [pltpu.SemaphoreType.DMA((11,))],
+        + [pltpu.SemaphoreType.DMA((7 + CHUNKS,))],
         compiler_params=pltpu.CompilerParams(vmem_limit_bytes=32 * 1024 * 1024),
         name="select_rows_and_rotate_queries",
     )(*operands)
@@ -268,7 +262,7 @@
     row_out = query_expert.shape[0] // (experts * blocks)
     order = partner_order(experts, blocks)
     half = len(order[0])
-    keep, give = pack(
+    *sends, give = pack(
         order,
         row_out,
         assign.T,
@@ -283,14 +277,15 @@
     swap = [(0, 1), (1, 0)]
     got = lax.ppermute(give, "mp", swap)
     arrived = []
-    for r in range(half):
+    for r in reversed(range(half)):
         pairs = [
             ((e * blocks + d) * 2 + m, ((e ^ order[m][r][0]) * blocks + (d ^ order[m][r][1])) * 2 + m)
             for e in range(experts)
             for d in range(blocks)
             for m in range(2)
         ]
-        arrived.append(lax.ppermute(jnp.stack([keep[r], got[r]]), ("expert", "dp", "mp"), pairs))
+        merged = sends[r].at[1].set(got[r])
+        arrived.append(lax.ppermute(merged, ("expert", "dp", "mp"), pairs))
     there = [lax.ppermute(block, "mp", swap) for block in arrived]
     act_cov, grad_cov, rot_act, rot_grad = factors(
         d_model,

time: 23.9 us -> 23.4 us (0.979)
  other arithmetic: 0.41 us -> 0 us
    another operation x4 -> x0, other arithmetic: 0.41 us -> none  [local(): jnp.stack([keep[r], got[r]])]
  transfers between devices with their start and end apart: 9 -> 9, of which waited for: 6 -> 6; matrix products, arithmetic and copies ran while one was open for 2% -> 0% of each run, Pallas kernels for 0% -> 0%
where the time goes in v4:
time: 23.4 us; the launch traced here: 23.2 us
  starting transfers between devices  10.2 us (44%)
  Pallas kernels  7.33 us (31%)
  waiting for transfers between devices  4.21 us (18%)
  between operations  1.34 us (6%)
    ppermute x4, starting transfers between devices, local(): arrived.append(lax.ppermute(merged, ('expert', 'dp', 'mp'), pairs))  8.98 us
    pallas_call x1, Pallas kernels, factors(): pl.pallas_call(functools.partial(factor_kernel, act_width, row_out, round...  4.11 us
    pallas_call x1, Pallas kernels, pack(): pl.pallas_call(functools.partial(pack_kernel, order, row_out), out_shape=...  3.22 us
    ppermute x4, waiting for transfers between devices, local(): arrived.append(lax.ppermute(merged, ('expert', 'dp', 'mp'), pairs))  2.65 us
    ppermute x1, waiting for transfers between devices, local(): got = lax.ppermute(give, 'mp', swap)  1.01 us
    ppermute x4, starting transfers between devices, local(): there = [lax.ppermute(block, 'mp', swap) for block in arrived]  0.68 us
    ppermute x4, waiting for transfers between devices, local(): there = [lax.ppermute(block, 'mp', swap) for block in arrived]  0.56 us
    ppermute x1, starting transfers between devices, local(): got = lax.ppermute(give, 'mp', swap)  0.52 us
  transfers between devices with their start and end apart: 9, of which 6 were waited for; matrix products, arithmetic and copies ran while one was open for 0% of the time, Pallas kernels for 0%

profile of v4, /device:TPU:0, one launch (start us, length us, event | category | flops | bytes accessed | tf_op | source)
XLA Modules:
  0.0 23.2 jit_solution(5934836547370104437)
XLA Ops:
  0.6 3.2 %select_rows_and_rotate_queries.1 = (bf16[2,2,9216]{2,1,0:T(2,128)(2,1)S(1)}, bf16[2,2,9216]{2,1,0:T(2,128)(2,1)S(1)}, bf16[2,2,9216]{2,1,0:T(2,128)(2,1)S(1)}, ...) custom-call(s32[8,24]{1,0:T(8,128)} %bitcast.10, bf16[24,4096]{1,0:T(8,128)(2,1)} %tokens_hbm.1, ...), custom_call_target="tpu_custom_call" | custom-call | tf_op jit(solution)/shard_map/select_rows_and_rotate_queries/pallas_call | solution.py:168
  3.9 0.5 %collective-permute-start = (bf16[4,2,9216]{2,1,0:T(2,128)(2,1)S(1)}, bf16[4,2,9216]{2,1,0:T(2,128)(2,1)S(1)}, u32[]{:S(2)}, u32[]{:S(2)}) collective-permute-start(bf16[4,2,9216]{2,1,0:T(2,128)(2,1)S(1)} %get-tuple-element.62), channel_id=1, source_target_pairs={{0,1},{1,0},{2,3},{3,2},{4,5},{5,4},{6,7},{7,6},{8,9},{9,8},{10,11... | collective-permute-start | bytes 442376 | tf_op jit(solution)/shard_map/ppermute | solution.py:278
  4.4 1.0 %collective-permute-done = bf16[4,2,9216]{2,1,0:T(2,128)(2,1)S(1)} collective-permute-done((bf16[4,2,9216]{2,1,0:T(2,128)(2,1)S(1)}, bf16[4,2,9216]{2,1,0:T(2,128)(2,1)S(1)}, u32[]{:S(2)}, u32[]{:S(2)}) %collective-permute-start) | collective-permute-done | bytes 147488 | tf_op jit(solution)/shard_map/ppermute | solution.py:278
  5.4 0.1 slice_dynamic-update-slice_fusion
  5.5 4.0 %collective-permute-start.4 = (bf16[2,2,9216]{2,1,0:T(2,128)(2,1)S(1)}, bf16[2,2,9216]{2,1,0:T(2,128)(2,1)S(1)}, u32[]{:S(2)}, u32[]{:S(2)}) collective-permute-start(bf16[2,2,9216]{2,1,0:T(2,128)(2,1)S(1)} %get-tuple-element.70), channel_id=1, source_target_pairs={{0,8},{1,11},{2,10},{3,9},{4,12},{5,15},{6,14},{7,13},{8,0},{9,3},... | collective-permute-start | bytes 221192 | tf_op jit(solution)/shard_map/ppermute | solution.py:288
  9.5 1.3 %collective-permute-start.3 = (bf16[2,2,9216]{2,1,0:T(2,128)(2,1)S(1)}, bf16[2,2,9216]{2,1,0:T(2,128)(2,1)S(1)}, u32[]{:S(2)}, u32[]{:S(2)}) collective-permute-start(bf16[2,2,9216]{2,1,0:T(2,128)(2,1)S(1)} %get-tuple-element.71), channel_id=1, source_target_pairs={{0,12},{1,15},{2,14},{3,13},{4,8},{5,11},{6,10},{7,9},{8,4},{9,7},... | collective-permute-start | bytes 221192 | tf_op jit(solution)/shard_map/ppermute | solution.py:288
  10.9 0.2 collective-permute-start.2
  11.1 3.4 %collective-permute-start.1 = (bf16[2,2,9216]{2,1,0:T(2,128)(2,1)S(1)}, bf16[2,2,9216]{2,1,0:T(2,128)(2,1)S(1)}, u32[]{:S(2)}, u32[]{:S(2)}) collective-permute-start(bf16[2,2,9216]{2,1,0:T(2,128)(2,1)S(1)} %get-tuple-element.73), channel_id=1, source_target_pairs={{0,2},{1,1},{2,0},{3,3},{4,6},{5,5},{6,4},{7,7},{8,10},{9,9},{10,8... | collective-permute-start | bytes 221192 | tf_op jit(solution)/shard_map/ppermute | solution.py:288
  14.5 0.0 collective-permute-done.4.refs_3_
  14.5 0.1 collective-permute-start.8
  14.6 1.9 %collective-permute-done.3.refs_2_ = bf16[2,2,9216]{2,1,0:T(2,128)(2,1)S(1)} collective-permute-done((bf16[2,2,9216]{2,1,0:T(2,128)(2,1)S(1)}, bf16[2,2,9216]{2,1,0:T(2,128)(2,1)S(1)}, u32[]{:S(2)}, u32[]{:S(2)}) %collective-permute-start.3) | collective-permute-done | bytes 73760 | tf_op jit(solution)/shard_map/ppermute | solution.py:288
  16.5 0.4 %collective-permute-start.7 = (bf16[2,2,9216]{2,1,0:T(2,128)(2,1)S(1)}, bf16[2,2,9216]{2,1,0:T(2,128)(2,1)S(1)}, u32[]{:S(2)}, u32[]{:S(2)}) collective-permute-start(bf16[2,2,9216]{2,1,0:T(2,128)(2,1)S(1)} %collective-permute-done.3.refs_2_), channel_id=1, source_target_pairs={{0,1},{1,0},{2,3},{3,2},{4,5},{5,4},{6,7},{7,6},{8,9},{9,8},{10,11... | collective-permute-start | bytes 221192 | tf_op jit(solution)/shard_map/ppermute | solution.py:289
  16.9 0.4 %collective-permute-done.2.refs_1_ = bf16[2,2,9216]{2,1,0:T(2,128)(2,1)S(1)} collective-permute-done((bf16[2,2,9216]{2,1,0:T(2,128)(2,1)S(1)}, bf16[2,2,9216]{2,1,0:T(2,128)(2,1)S(1)}, u32[]{:S(2)}, u32[]{:S(2)}) %collective-permute-start.2) | collective-permute-done | bytes 73760 | tf_op jit(solution)/shard_map/ppermute | solution.py:288
  17.3 0.2 collective-permute-start.6
  17.5 0.3 %collective-permute-done.1.refs_0_ = bf16[2,2,9216]{2,1,0:T(2,128)(2,1)S(1)} collective-permute-done((bf16[2,2,9216]{2,1,0:T(2,128)(2,1)S(1)}, bf16[2,2,9216]{2,1,0:T(2,128)(2,1)S(1)}, u32[]{:S(2)}, u32[]{:S(2)}) %collective-permute-start.1) | collective-permute-done | bytes 73760 | tf_op jit(solution)/shard_map/ppermute | solution.py:288
  17.8 0.0 collective-permute-start.5
  18.5 0.0 collective-permute-done.8.refs_7_
  18.5 0.0 collective-permute-done.7.refs_6_
  18.5 0.1 collective-permute-done.6.refs_5_
  18.6 0.5 %collective-permute-done.5.refs_4_ = bf16[2,2,9216]{2,1,0:T(2,128)(2,1)S(1)} collective-permute-done((bf16[2,2,9216]{2,1,0:T(2,128)(2,1)S(1)}, bf16[2,2,9216]{2,1,0:T(2,128)(2,1)S(1)}, u32[]{:S(2)}, u32[]{:S(2)}) %collective-permute-start.5) | collective-permute-done | bytes 73760 | tf_op jit(solution)/shard_map/ppermute | solution.py:289
  19.1 4.1 %factor_tiles.1 = (bf16[2048,2048]{1,0:T(8,128)(2,1)}, bf16[768,768]{1,0:T(8,128)(2,1)}, bf16[2,1024]{1,0:T(2,128)(2,1)}, bf16[2,768]{1,0:T(2,128)(2,1)}) custom-call(s32[1]{0:T(128)S(6)} %copy.17.count_ref, bf16[2,2,9216]{2,1,0:T(2,128)(2,1)S(1)} %collective-permute-done.1.refs_0_, bf16[2,2,9216]{2,1,0:T(2,128)(2,1)S(1)} %collective-permute-done.2.refs_1_, ...), custom_call_target="tpu_custom_call" | custom-call | tf_op jit(solution)/shard_map/factor_tiles/pallas_call | solution.py:243
Async XLA Ops:
  3.9 1.5 %collective-permute-start = (bf16[4,2,9216]{2,1,0:T(2,128)(2,1)S(1)}, bf16[4,2,9216]{2,1,0:T(2,128)(2,1)S(1)}, u32[]{:S(2)}, u32[]{:S(2)}) collective-permute-start(bf16[4,2,9216]{2,1,0:T(2,128)(2,1)S(1)} %get-tuple-element.62), channel_id=1, source_target_pairs={{0,1},{1,0},{2,3},{3,2},{4,5},{5,4},{6,7},{7,6},{8,9},{9,8},{10,11... | collective-permute-start | bytes 442376 | tf_op jit(solution)/shard_map/ppermute | solution.py:278
  5.5 9.0 %collective-permute-start.4 = (bf16[2,2,9216]{2,1,0:T(2,128)(2,1)S(1)}, bf16[2,2,9216]{2,1,0:T(2,128)(2,1)S(1)}, u32[]{:S(2)}, u32[]{:S(2)}) collective-permute-start(bf16[2,2,9216]{2,1,0:T(2,128)(2,1)S(1)} %get-tuple-element.70), channel_id=1, source_target_pairs={{0,8},{1,11},{2,10},{3,9},{4,12},{5,15},{6,14},{7,13},{8,0},{9,3},... | collective-permute-start | bytes 221192 | tf_op jit(solution)/shard_map/ppermute | solution.py:288
  9.5 7.0 %collective-permute-start.3 = (bf16[2,2,9216]{2,1,0:T(2,128)(2,1)S(1)}, bf16[2,2,9216]{2,1,0:T(2,128)(2,1)S(1)}, u32[]{:S(2)}, u32[]{:S(2)}) collective-permute-start(bf16[2,2,9216]{2,1,0:T(2,128)(2,1)S(1)} %get-tuple-element.71), channel_id=1, source_target_pairs={{0,12},{1,15},{2,14},{3,13},{4,8},{5,11},{6,10},{7,9},{8,4},{9,7},... | collective-permute-start | bytes 221192 | tf_op jit(solution)/shard_map/ppermute | solution.py:288
  10.9 6.5 %collective-permute-start.2 = (bf16[2,2,9216]{2,1,0:T(2,128)(2,1)S(1)}, bf16[2,2,9216]{2,1,0:T(2,128)(2,1)S(1)}, u32[]{:S(2)}, u32[]{:S(2)}) collective-permute-start(bf16[2,2,9216]{2,1,0:T(2,128)(2,1)S(1)} %get-tuple-element.72), channel_id=1, source_target_pairs={{0,4},{1,7},{2,6},{3,5},{4,0},{5,3},{6,2},{7,1},{8,12},{9,15},{10,... | collective-permute-start | bytes 221192 | tf_op jit(solution)/shard_map/ppermute | solution.py:288
  11.1 6.7 %collective-permute-start.1 = (bf16[2,2,9216]{2,1,0:T(2,128)(2,1)S(1)}, bf16[2,2,9216]{2,1,0:T(2,128)(2,1)S(1)}, u32[]{:S(2)}, u32[]{:S(2)}) collective-permute-start(bf16[2,2,9216]{2,1,0:T(2,128)(2,1)S(1)} %get-tuple-element.73), channel_id=1, source_target_pairs={{0,2},{1,1},{2,0},{3,3},{4,6},{5,5},{6,4},{7,7},{8,10},{9,9},{10,8... | collective-permute-start | bytes 221192 | tf_op jit(solution)/shard_map/ppermute | solution.py:288
  14.5 4.0 %collective-permute-start.8 = (bf16[2,2,9216]{2,1,0:T(2,128)(2,1)S(1)}, bf16[2,2,9216]{2,1,0:T(2,128)(2,1)S(1)}, u32[]{:S(2)}, u32[]{:S(2)}) collective-permute-start(bf16[2,2,9216]{2,1,0:T(2,128)(2,1)S(1)} %collective-permute-done.4.refs_3_), channel_id=1, source_target_pairs={{0,1},{1,0},{2,3},{3,2},{4,5},{5,4},{6,7},{7,6},{8,9},{9,8},{10,11... | collective-permute-start | bytes 221192 | tf_op jit(solution)/shard_map/ppermute | solution.py:289
  16.5 2.0 %collective-permute-start.7 = (bf16[2,2,9216]{2,1,0:T(2,128)(2,1)S(1)}, bf16[2,2,9216]{2,1,0:T(2,128)(2,1)S(1)}, u32[]{:S(2)}, u32[]{:S(2)}) collective-permute-start(bf16[2,2,9216]{2,1,0:T(2,128)(2,1)S(1)} %collective-permute-done.3.refs_2_), channel_id=1, source_target_pairs={{0,1},{1,0},{2,3},{3,2},{4,5},{5,4},{6,7},{7,6},{8,9},{9,8},{10,11... | collective-permute-start | bytes 221192 | tf_op jit(solution)/shard_map/ppermute | solution.py:289
  17.3 1.3 %collective-permute-start.6 = (bf16[2,2,9216]{2,1,0:T(2,128)(2,1)S(1)}, bf16[2,2,9216]{2,1,0:T(2,128)(2,1)S(1)}, u32[]{:S(2)}, u32[]{:S(2)}) collective-permute-start(bf16[2,2,9216]{2,1,0:T(2,128)(2,1)S(1)} %collective-permute-done.2.refs_1_), channel_id=1, source_target_pairs={{0,1},{1,0},{2,3},{3,2},{4,5},{5,4},{6,7},{7,6},{8,9},{9,8},{10,11... | collective-permute-start | bytes 221192 | tf_op jit(solution)/shard_map/ppermute | solution.py:289
  17.8 1.3 %collective-permute-start.5 = (bf16[2,2,9216]{2,1,0:T(2,128)(2,1)S(1)}, bf16[2,2,9216]{2,1,0:T(2,128)(2,1)S(1)}, u32[]{:S(2)}, u32[]{:S(2)}) collective-permute-start(bf16[2,2,9216]{2,1,0:T(2,128)(2,1)S(1)} %collective-permute-done.1.refs_0_), channel_id=1, source_target_pairs={{0,1},{1,0},{2,3},{3,2},{4,5},{5,4},{6,7},{7,6},{8,9},{9,8},{10,11... | collective-permute-start | bytes 221192 | tf_op jit(solution)/shard_map/ppermute | solution.py:289

commit v5 on v4

--- a/solution.py
+++ b/solution.py
@@ -18,13 +18,7 @@
 
 def partner_order(experts, blocks):
     far = list(range(experts // 2, experts)) + list(range(experts // 2 - 1, 0, -1))
-    order = [], []
-    for de in far:
-        for dd in range(blocks):
-            order[dd % 2].append((de, dd))
-    for i in range(blocks):
-        order[i % 2].append((0, (i + 1) % blocks))
-    return order
+    return tuple([(de, dd) for de in far for dd in range(core, blocks, 2)] for core in range(2))
 
 
 def dot(a, b):
@@ -40,22 +34,11 @@
     return value
 
 
-def pack_kernel(
-    order,
-    row_out,
-    assign_hbm,
-    tokens_hbm,
-    pseudo_hbm,
-    qe_hbm,
-    qa_hbm,
-    qg_hbm,
-    ba_hbm,
-    bg_hbm,
-    *refs,
-):
+def pack_kernel(order, blocks, row_out, *refs):
+    assign_hbm, tokens_hbm, pseudo_hbm, qe_hbm, qa_hbm, qg_hbm, ba_hbm, bg_hbm = refs[:8]
     half = len(order[0])
-    send_refs, give_ref = refs[:half], refs[half]
-    assign_ref, tokens_ref, pseudo_ref, qe_ref, qa_ref, qg_ref, ba_ref, bg_ref, sems = refs[half + 1 :]
+    send_refs, near_refs, give_ref = refs[8 : 8 + half], refs[8 + half : 8 + half + blocks], refs[8 + half + blocks]
+    assign_ref, tokens_ref, pseudo_ref, qe_ref, qa_ref, qg_ref, ba_ref, bg_ref, sems = refs[9 + half + blocks :]
     chunks = CHUNKS
     deep = ba_ref.shape[0] // chunks
     small = [
@@ -81,12 +64,12 @@
     for copy in small + large:
         copy.start()
     expert, block, core = lax.axis_index("expert"), lax.axis_index("dp"), lax.axis_index("mp")
-    rows = 4 * half
-    blocks = 1 + max(dd for _, dd in order[0] + order[1])
+    rows = 2 * (2 * half + blocks)
     slots, toks = assign_ref.shape
     flat = slots * toks
     d_model, hidden = tokens_ref.shape[1], pseudo_ref.shape[1]
-    plan = [order[0] + order[1], order[1] + order[0]]
+    same_expert = [(0, dd) for dd in range(blocks)]
+    plan = [order[0] + order[1] + same_expert, order[1] + order[0] + same_expert]
     step_e = jnp.where(core == 0, by_row([p[0] for p in plan[0]], rows, 2), by_row([p[0] for p in plan[1]], rows, 2))
     step_d = jnp.where(core == 0, by_row([p[1] for p in plan[0]], rows, 2), by_row([p[1] for p in plan[1]], rows, 2))
     to_e, to_d = step_e ^ expert, step_d ^ block
@@ -113,16 +96,24 @@
     token_pick = ((chosen >= low) & (chosen < low + slots)).astype(BF16)
 
     def put(column, value):
-        value = value.astype(BF16)
         width = value.shape[1]
         for i in range(half):
             send_refs[i][0, :, column : column + width] = value[2 * i : 2 * i + 2]
             give_ref[i, :, column : column + width] = value[2 * (half + i) : 2 * (half + i) + 2]
 
+    def put_rows(column, value):
+        value = value.astype(BF16)
+        put(column, value)
+        width = value.shape[1]
+        mine = value[4 * half : 4 * half + 2]
+        give_ref[half, :, column : column + width] = mine
+        for ref in near_refs:
+            ref[0, :, column : column + width] = mine
+
     small[4].wait()
-    put(0, dot(token_pick, tokens_ref[...]))
+    put_rows(0, dot(token_pick, tokens_ref[...]))
     small[5].wait()
-    put(d_model, dot(slot_pick, pseudo_ref[...]))
+    put_rows(d_model, dot(slot_pick, pseudo_ref[...]))
 
     for i in (1, 2, 3):
         small[i].wait()
@@ -139,15 +130,21 @@
     pick = jnp.concatenate(picks, axis=0) if len(picks) > 1 else picks[0]
     my_act = dot(pick, qa_ref[...]).astype(BF16)
     my_grad = dot(pick, qg_ref[...]).astype(BF16)
-    width = 2 * (act_cols + grad_cols)
+    cols = act_cols + grad_cols
 
     def put_pair(column, value):
         high = value.astype(BF16)
-        low = value - high.astype(F32)
+        low = (value - high.astype(F32)).astype(BF16)
+        width = value.shape[1]
         for i in range(row_out // 2):
-            cut = slice(i * rows, (i + 1) * rows)
-            put(base + i * width + column, high[cut])
-            put(base + i * width + column + act_cols + grad_cols, low[cut])
+            at = base + 2 * i * cols + column
+            put(at, high[i * rows : (i + 1) * rows])
+            put(at + cols, low[i * rows : (i + 1) * rows])
+            at = base + i * cols + column
+            for dd, ref in enumerate(near_refs):
+                first = i * rows + 4 * half + 2 * dd
+                ref[0, :, at : at + width] = high[first : first + 2]
+                ref[1, :, at : at + width] = low[first : first + 2]
 
     small[6].wait()
     put_pair(act_cols, dot(my_grad, bg_ref[...]))
@@ -158,33 +155,56 @@
     put_pair(0, act_part)
 
 
-def pack(order, row_out, assign, tokens, pseudo, qe, qa, qg, ba, bg):
-    width = tokens.shape[1] + pseudo.shape[1] + row_out * (ba.shape[1] + bg.shape[1])
+def pack(order, blocks, row_out, assign, tokens, pseudo, qe, qa, qg, ba, bg):
     half = len(order[0])
-    send = jax.ShapeDtypeStruct((2, CAP, width), BF16)
-    give = jax.ShapeDtypeStruct((half, CAP, width), BF16)
+    width = tokens.shape[1] + pseudo.shape[1]
+    cols = row_out // 2 * (ba.shape[1] + bg.shape[1])
+    send = jax.ShapeDtypeStruct((2, CAP, width + 2 * cols), BF16)
+    near = jax.ShapeDtypeStruct((2, CAP, width + cols), BF16)
+    give = jax.ShapeDtypeStruct((half + 1, CAP, width + 2 * cols), BF16)
     operands = (assign, tokens, pseudo, qe, qa, qg, ba, bg)
     operands = tuple(pltpu.with_memory_space_constraint(x, pltpu.HBM) for x in operands)
-    return pl.pallas_call(
-        functools.partial(pack_kernel, order, row_out),
-        out_shape=(send,) * half + (give,),
+    outs = pl.pallas_call(
+        functools.partial(pack_kernel, order, blocks, row_out),
+        out_shape=(send,) * half + (near,) * blocks + (give,),
         in_specs=[HBM] * len(operands),
-        out_specs=(VMEM,) * (half + 1),
+        out_specs=(VMEM,) * (half + blocks + 1),
         scratch_shapes=[pltpu.VMEM(x.shape, x.dtype) for x in operands]
         + [pltpu.SemaphoreType.DMA((7 + CHUNKS,))],
         compiler_params=pltpu.CompilerParams(vmem_limit_bytes=32 * 1024 * 1024),
         name="select_rows_and_rotate_queries",
     )(*operands)
+    return outs[:half], outs[half:-1], outs[-1]
+
+
+def gather_kernel(*refs):
+    *blocks, out_ref = refs
+    width = out_ref.shape[1]
+    out_ref[...] = jnp.concatenate([ref[c, :, :width] for ref in blocks for c in range(2)], axis=0)
+
+
+def gather_rows(width, blocks):
+    return pl.pallas_call(
+        gather_kernel,
+        out_shape=jax.ShapeDtypeStruct((2 * CAP * len(blocks), width), BF16),
+        in_specs=[VMEM] * len(blocks),
+        out_specs=VMEM,
+        cost_estimate=pl.CostEstimate(flops=1000000000, bytes_accessed=8 * CAP * len(blocks) * width, transcendentals=0),
+        name="gather_rows",
+    )(*blocks)
 
 
 def row_steps(rows):
     return [(i * 128, 64 if i < 2 else 128) for i in range(rows // 128)]
 
 
-def factor_kernel(act_width, row_out, rounds, count_ref, *refs):
+def factor_kernel(act_width, row_out, rounds, blocks, count_ref, *refs):
     here, there = refs[:rounds], refs[rounds : 2 * rounds]
-    act_hbm, grad_hbm, rot_act_hbm, rot_grad_hbm = refs[2 * rounds : 2 * rounds + 4]
-    right_ref, act_ref, grad_ref, rot_act_ref, rot_grad_ref, sems = refs[2 * rounds + 4 :]
+    refs = refs[2 * rounds :]
+    near, ready_ref = refs[:blocks], refs[blocks]
+    refs = refs[1:]
+    act_hbm, grad_hbm, rot_act_hbm, rot_grad_hbm = refs[blocks : blocks + 4]
+    right_ref, act_ref, grad_ref, rot_act_ref, rot_grad_ref, sems = refs[blocks + 4 :]
     block, core = lax.axis_index("dp"), lax.axis_index("mp")
     act_block, act_half = act_ref.shape
     grad_block, grad_half = grad_ref.shape
@@ -199,7 +219,8 @@
 
     def columns(at, width):
         span = pl.ds(pl.multiple_of(at, 128), width)
-        return jnp.concatenate([ref[c, :, span] for ref in here + there for c in range(2)], axis=0)
+        late = [ref[c, :, span] for ref in there for c in range(2)]
+        return jnp.concatenate([ready_ref[:, span]] + late, axis=0)
 
     def tile(left, right):
         part = lax.dot_general(left, right, contract, preferred_element_type=F32)
@@ -221,14 +242,18 @@
 
     act_cols = rot_act_ref.shape[1]
     cols = act_cols + rot_grad_ref.shape[1]
+    base = act_width + 2 * grad_half
     for i in range(row_out // 2):
-        at = act_width + 2 * grad_half + i * 2 * cols
         total = jnp.zeros((2, cols), F32)
+        at = base + i * 2 * cols
         for group, c in ((here, 0), (there, 1)):
             for ref in group:
                 high = ref[c, :, at : at + cols].astype(F32)
                 low = ref[c, :, at + cols : at + 2 * cols].astype(F32)
                 total += high + low
+        at = base + i * cols
+        for ref in near:
+            total += ref[0, :, at : at + cols].astype(F32) + ref[1, :, at : at + cols].astype(F32)
         rot_act_ref[2 * i : 2 * i + 2, :] = total[:, :act_cols].astype(BF16)
         rot_grad_ref[2 * i : 2 * i + 2, :] = total[:, act_cols:].astype(BF16)
     send(rot_act_ref, rot_act_hbm)
@@ -237,20 +262,20 @@
         copy.wait()
 
 
-def factors(act_width, row_out, act_tile, grad_tile, act_cols, grad_cols, counts, here, there):
-    rounds = len(here)
+def factors(act_width, row_out, act_tile, grad_tile, act_cols, grad_cols, counts, here, there, near, ready):
+    rounds, blocks = len(here), len(near)
     shapes = (act_tile, grad_tile, (row_out, act_cols), (row_out, grad_cols))
     return pl.pallas_call(
-        functools.partial(factor_kernel, act_width, row_out, rounds),
+        functools.partial(factor_kernel, act_width, row_out, rounds, blocks),
         out_shape=tuple(jax.ShapeDtypeStruct(shape, BF16) for shape in shapes),
-        in_specs=[SMEM] + [VMEM] * (2 * rounds),
+        in_specs=[SMEM] + [VMEM] * (2 * rounds + blocks + 1),
         out_specs=(HBM,) * 4,
-        scratch_shapes=[pltpu.VMEM((2 * 2 * CAP * rounds, act_tile[1]), BF16)]
+        scratch_shapes=[pltpu.VMEM((2 * CAP * (2 * rounds + blocks), act_tile[1]), BF16)]
         + [pltpu.VMEM(shape, BF16) for shape in shapes]
         + [pltpu.SemaphoreType.DMA((act_tile[0] // 128 + 5,))],
         compiler_params=pltpu.CompilerParams(vmem_limit_bytes=40 * 1024 * 1024),
         name="factor_tiles",
-    )(counts, *here, *there)
+    )(counts, *here, *there, *near, ready)
 
 
 def local(
@@ -262,8 +287,9 @@
     row_out = query_expert.shape[0] // (experts * blocks)
     order = partner_order(experts, blocks)
     half = len(order[0])
-    *sends, give = pack(
+    sends, nears, give = pack(
         order,
+        blocks,
         row_out,
         assign.T,
         tokens,
@@ -276,7 +302,11 @@
     )
     swap = [(0, 1), (1, 0)]
     got = lax.ppermute(give, "mp", swap)
-    arrived = []
+    width = d_model + hidden
+    nears = [near.at[1, :, :width].set(got[half, :, :width]) for near in nears]
+    for dd in range(1, blocks):
+        nears[dd] = lax.ppermute(nears[dd], "dp", [(d, d ^ dd) for d in range(blocks)])
+    here = []
     for r in reversed(range(half)):
         pairs = [
             ((e * blocks + d) * 2 + m, ((e ^ order[m][r][0]) * blocks + (d ^ order[m][r][1])) * 2 + m)
@@ -284,9 +314,8 @@
             for d in range(blocks)
             for m in range(2)
         ]
-        merged = sends[r].at[1].set(got[r])
-        arrived.append(lax.ppermute(merged, ("expert", "dp", "mp"), pairs))
-    there = [lax.ppermute(block, "mp", swap) for block in arrived]
+        here.append(lax.ppermute(sends[r].at[1].set(got[r]), ("expert", "dp", "mp"), pairs))
+    there = [lax.ppermute(rows, "mp", swap) for rows in here]
     act_cov, grad_cov, rot_act, rot_grad = factors(
         d_model,
         row_out,
@@ -295,8 +324,10 @@
         basis_act.shape[2],
         basis_grad.shape[2],
         counts,
-        arrived,
+        here,
         there,
+        nears,
+        gather_rows(width, here + nears),
     )
     return act_cov[None], grad_cov[None], rot_act, rot_grad
 

time: 23.4 us -> 29.7 us (1.27)
  local copies, waits for them, and re-layouts: 0.12 us -> 5.99 us
  Pallas kernels: 7.33 us -> 9.17 us
  starting transfers between devices: 10.2 us -> 8.49 us
    unnamed x0 -> x22, local copies, waits for them, and re-layouts: none -> 5.86 us
    pallas_call x1 -> x2, Pallas kernels: 3.22 us -> 5.07 us  [the longest x1 3.22 us: pack(): pl.pallas_call(functools.partial(pack_kernel, order, blocks, row_out), ou...]
    ppermute x8 -> x7, starting transfers between devices: 9.65 us -> 7.97 us  [the longest x3 5.59 us: local(): lax.ppermute(sends[r].at[1].set(got[r]), ('expert', 'dp', 'mp'), pairs)]
    ppermute x8 -> x7, waiting for transfers between devices: 3.2 us -> 3.29 us  [the longest x3 3.28 us: local(): lax.ppermute(sends[r].at[1].set(got[r]), ('expert', 'dp', 'mp'), pairs)]
  transfers between devices with their start and end apart: 9 -> 8, of which waited for: 6 -> 3; matrix products, arithmetic and copies ran while one was open for 0% -> 0% of each run, Pallas kernels for 0% -> 6%
where the time goes in v5:
time: 29.7 us; the launch traced here: 29.3 us
  Pallas kernels  9.17 us (31%)
  starting transfers between devices  8.49 us (29%)
  local copies, waits for them, and re-layouts  5.99 us (20%)
  waiting for transfers between devices  4.3 us (14%)
  between operations  1.36 us (5%)
    unnamed x22, local copies, waits for them, and re-layouts  5.86 us
    ppermute x3, starting transfers between devices, local(): lax.ppermute(sends[r].at[1].set(got[r]), ('expert', 'dp', 'mp'), pairs)  5.59 us
    pallas_call x1, Pallas kernels, factors(): pl.pallas_call(functools.partial(factor_kernel, act_width, row_out, round...  4.1 us
    ppermute x3, waiting for transfers between devices, local(): lax.ppermute(sends[r].at[1].set(got[r]), ('expert', 'dp', 'mp'), pairs)  3.28 us
    pallas_call x1, Pallas kernels, pack(): pl.pallas_call(functools.partial(pack_kernel, order, blocks, row_out), ou...  3.22 us
    pallas_call x1, Pallas kernels, gather_rows(): pl.pallas_call(gather_kernel, out_shape=jax.ShapeDtypeStruct((2 * CAP * l...  1.85 us
    ppermute x1, starting transfers between devices, local(): lax.ppermute(nears[dd], 'dp', [(d, d ^ dd) for d in range(blocks)])  1.56 us
    ppermute x1, waiting for transfers between devices, local(): got = lax.ppermute(give, 'mp', swap)  1.01 us
  transfers between devices with their start and end apart: 8, of which 3 were waited for; matrix products, arithmetic and copies ran while one was open for 0% of the time, Pallas kernels for 6%

profile of v5, /device:TPU:0, one launch (start us, length us, event | category | flops | bytes accessed | tf_op | source)
XLA Modules:
  0.0 29.3 jit_solution(5913672001959412058)
XLA Ops:
  0.6 3.2 %select_rows_and_rotate_queries.1 = (bf16[2,2,9216]{2,1,0:T(2,128)(2,1)S(1)}, bf16[2,2,9216]{2,1,0:T(2,128)(2,1)S(1)}, bf16[2,2,9216]{2,1,0:T(2,128)(2,1)S(1)}, ...) custom-call(s32[8,24]{1,0:T(8,128)} %bitcast.10, ...), custom_call_target="tpu_custom_call" | custom-call | tf_op jit(solution)/shard_map/select_rows_and_rotate_queries/pallas_call | solution.py:167
  3.9 0.5 %collective-permute-start = (bf16[4,2,9216]{2,1,0:T(2,128)(2,1)S(1)}, bf16[4,2,9216]{2,1,0:T(2,128)(2,1)S(1)}, u32[]{:S(2)}, u32[]{:S(2)}) collective-permute-start(bf16[4,2,9216]{2,1,0:T(2,128)(2,1)S(1)} %get-tuple-element.75), channel_id=1, source_target_pairs={{0,1},{1,0},{2,3},{3,2},{4,5},{5,4},{6,7},{7,6},{8,9},{9,8},{10,11... | collective-permute-start | bytes 442376 | tf_op jit(solution)/shard_map/ppermute | solution.py:304
  4.4 1.0 %collective-permute-done = bf16[4,2,9216]{2,1,0:T(2,128)(2,1)S(1)} collective-permute-done((bf16[4,2,9216]{2,1,0:T(2,128)(2,1)S(1)}, bf16[4,2,9216]{2,1,0:T(2,128)(2,1)S(1)}, u32[]{:S(2)}, u32[]{:S(2)}) %collective-permute-start) | collective-permute-done | bytes 147488 | tf_op jit(solution)/shard_map/ppermute | solution.py:304
  5.4 0.1 slice_dynamic-update-slice_fusion
  5.5 4.0 %collective-permute-start.3 = (bf16[2,2,9216]{2,1,0:T(2,128)(2,1)S(1)}, bf16[2,2,9216]{2,1,0:T(2,128)(2,1)S(1)}, u32[]{:S(2)}, u32[]{:S(2)}) collective-permute-start(bf16[2,2,9216]{2,1,0:T(2,128)(2,1)S(1)} %get-tuple-element.86), channel_id=1, source_target_pairs={{0,8},{1,11},{2,10},{3,9},{4,12},{5,15},{6,14},{7,13},{8,0},{9,3},... | collective-permute-start | bytes 221192 | tf_op jit(solution)/shard_map/ppermute | solution.py:317
  9.5 1.3 %collective-permute-start.2 = (bf16[2,2,9216]{2,1,0:T(2,128)(2,1)S(1)}, bf16[2,2,9216]{2,1,0:T(2,128)(2,1)S(1)}, u32[]{:S(2)}, u32[]{:S(2)}) collective-permute-start(bf16[2,2,9216]{2,1,0:T(2,128)(2,1)S(1)} %get-tuple-element.87), channel_id=1, source_target_pairs={{0,12},{1,15},{2,14},{3,13},{4,8},{5,11},{6,10},{7,9},{8,4},{9,7},... | collective-permute-start | bytes 221192 | tf_op jit(solution)/shard_map/ppermute | solution.py:317
  10.8 0.2 collective-permute-start.1
  11.1 0.0 copy-start.9
  11.1 1.6 %collective-permute-start.7 = (bf16[2,2,7424]{2,1,0:T(2,128)(2,1)S(1)}, bf16[2,2,7424]{2,1,0:T(2,128)(2,1)S(1)}, u32[]{:S(2)}, u32[]{:S(2)}) collective-permute-start(bf16[2,2,7424]{2,1,0:T(2,128)(2,1)S(1)} %get-tuple-element.84), channel_id=1, source_target_pairs={{0,2},{2,0},{1,3},{3,1},{4,6},{6,4},{5,7},{7,5},{8,10},{10,8},{9,1... | collective-permute-start | bytes 178184 | tf_op jit(solution)/shard_map/ppermute | solution.py:308
  13.3 0.0 collective-permute-done.3.refs_2_
  13.3 0.0 copy-start.1
  13.3 0.3 collective-permute-start.6
  13.6 2.9 %collective-permute-done.2.refs_1_ = bf16[2,2,9216]{2,1,0:T(2,128)(2,1)S(1)} collective-permute-done((bf16[2,2,9216]{2,1,0:T(2,128)(2,1)S(1)}, bf16[2,2,9216]{2,1,0:T(2,128)(2,1)S(1)}, u32[]{:S(2)}, u32[]{:S(2)}) %collective-permute-start.2) | collective-permute-done | bytes 73760 | tf_op jit(solution)/shard_map/ppermute | solution.py:317
  16.5 0.0 copy-start.3
  16.5 0.4 %collective-permute-start.5 = (bf16[2,2,9216]{2,1,0:T(2,128)(2,1)S(1)}, bf16[2,2,9216]{2,1,0:T(2,128)(2,1)S(1)}, u32[]{:S(2)}, u32[]{:S(2)}) collective-permute-start(bf16[2,2,9216]{2,1,0:T(2,128)(2,1)S(1)} %collective-permute-done.2.refs_1_), channel_id=1, source_target_pairs={{0,1},{1,0},{2,3},{3,2},{4,5},{5,4},{6,7},{7,6},{8,9},{9,8},{10,11... | collective-permute-start | bytes 221192 | tf_op jit(solution)/shard_map/ppermute | solution.py:318
  16.9 0.4 %collective-permute-done.1.refs_0_ = bf16[2,2,9216]{2,1,0:T(2,128)(2,1)S(1)} collective-permute-done((bf16[2,2,9216]{2,1,0:T(2,128)(2,1)S(1)}, bf16[2,2,9216]{2,1,0:T(2,128)(2,1)S(1)}, u32[]{:S(2)}, u32[]{:S(2)}) %collective-permute-start.1) | collective-permute-done | bytes 73760 | tf_op jit(solution)/shard_map/ppermute | solution.py:317
  17.3 0.0 copy-start.5
  17.3 0.2 collective-permute-start.4
  17.5 0.0 collective-permute-done.7.refs_4_.refs_7_
  17.5 0.0 copy-start.7
  17.5 0.0 copy-done.9
  17.5 0.0 copy-done.1
  17.5 0.0 copy-done.3
  17.5 0.4 %copy-done.5 = bf16[2,2,9216]{2,1,0:T(2,128)(2,1)} copy-done((bf16[2,2,9216]{2,1,0:T(2,128)(2,1)}, bf16[2,2,9216]{2,1,0:T(2,128)(2,1)S(1)}, u32[]{:S(2)}) %copy-start.5) | copy-done | bytes 73752
  17.9 0.2 copy-done.7
  18.1 1.9 %gather_rows.1.refs_8_ = bf16[20,5632]{1,0:T(8,128)(2,1)} custom-call(bf16[2,2,9216]{2,1,0:T(2,128)(2,1)} %copy-done.5, bf16[2,2,9216]{2,1,0:T(2,128)(2,1)} %copy-done.3, bf16[2,2,9216]{2,1,0:T(2,128)(2,1)} %copy-done.1, bf16[2,2,7424]{2,1,0:T(2,128)(2,1)} %copy-done.9, bf16[2,2,7424]{2,1,0:T(2,128)(2,1)} %copy-done.7), custom_call_target="tpu_custom_call" | custom-call | flops 1000000000 | bytes 450560 | tf_op jit(solution)/shard_map/gather_rows/pallas_call | solution.py:187
  19.9 0.0 collective-permute-done.6.refs_5_
  19.9 0.0 collective-permute-done.5.refs_4_
  19.9 0.0 collective-permute-done.4.refs_3_
  19.9 0.0 copy-start
  20.0 0.9 %copy-done = bf16[20,5632]{1,0:T(8,128)(2,1)S(1)} copy-done((bf16[20,5632]{1,0:T(8,128)(2,1)S(1)}, bf16[20,5632]{1,0:T(8,128)(2,1)}, u32[]{:S(2)}) %copy-start) | copy-done | bytes 225304
  20.9 0.0 copy-start.2
  20.9 0.9 %copy-done.2 = bf16[2,2,9216]{2,1,0:T(2,128)(2,1)S(1)} copy-done((bf16[2,2,9216]{2,1,0:T(2,128)(2,1)S(1)}, bf16[2,2,9216]{2,1,0:T(2,128)(2,1)}, u32[]{:S(2)}) %copy-start.2) | copy-done | bytes 73752
  21.8 0.0 copy-start.4
  21.8 0.9 %copy-done.4 = bf16[2,2,9216]{2,1,0:T(2,128)(2,1)S(1)} copy-done((bf16[2,2,9216]{2,1,0:T(2,128)(2,1)S(1)}, bf16[2,2,9216]{2,1,0:T(2,128)(2,1)}, u32[]{:S(2)}) %copy-start.4) | copy-done | bytes 73752
  22.7 0.0 copy-start.6
  22.7 0.9 %copy-done.6 = bf16[2,2,9216]{2,1,0:T(2,128)(2,1)S(1)} copy-done((bf16[2,2,9216]{2,1,0:T(2,128)(2,1)S(1)}, bf16[2,2,9216]{2,1,0:T(2,128)(2,1)}, u32[]{:S(2)}) %copy-start.6) | copy-done | bytes 73752
  23.6 0.0 copy-start.8
  23.6 0.8 %copy-done.8 = bf16[2,2,7424]{2,1,0:T(2,128)(2,1)S(1)} copy-done((bf16[2,2,7424]{2,1,0:T(2,128)(2,1)S(1)}, bf16[2,2,7424]{2,1,0:T(2,128)(2,1)}, u32[]{:S(2)}) %copy-start.8) | copy-done | bytes 59416
  24.4 0.0 copy-start.10
  24.4 0.8 %copy-done.10 = bf16[2,2,7424]{2,1,0:T(2,128)(2,1)S(1)} copy-done((bf16[2,2,7424]{2,1,0:T(2,128)(2,1)S(1)}, bf16[2,2,7424]{2,1,0:T(2,128)(2,1)}, u32[]{:S(2)}) %copy-start.10) | copy-done | bytes 59416
  25.2 4.1 %factor_tiles.1 = (bf16[2048,2048]{1,0:T(8,128)(2,1)}, bf16[768,768]{1,0:T(8,128)(2,1)}, bf16[2,1024]{1,0:T(2,128)(2,1)}, bf16[2,768]{1,0:T(2,128)(2,1)}) custom-call(s32[1]{0:T(128)S(6)} %copy.18.count_ref, bf16[2,2,9216]{2,1,0:T(2,128)(2,1)S(1)} %copy-done.6, bf16[2,2,9216]{2,1,0:T(2,128)(2,1)S(1)} %copy-done.4, bf16[2,2,9216]{2,1,0:T(2,128)(2,1)S(1)} %copy-done.2, ...), custom_call_target="tpu_custom_call" | custom-call | tf_op jit(solution)/shard_map/factor_tiles/pallas_call | solution.py:268
  (1 shorter events, 0.0 us)
Async XLA Ops:
  3.9 1.5 %collective-permute-start = (bf16[4,2,9216]{2,1,0:T(2,128)(2,1)S(1)}, bf16[4,2,9216]{2,1,0:T(2,128)(2,1)S(1)}, u32[]{:S(2)}, u32[]{:S(2)}) collective-permute-start(bf16[4,2,9216]{2,1,0:T(2,128)(2,1)S(1)} %get-tuple-element.75), channel_id=1, source_target_pairs={{0,1},{1,0},{2,3},{3,2},{4,5},{5,4},{6,7},{7,6},{8,9},{9,8},{10,11... | collective-permute-start | bytes 442376 | tf_op jit(solution)/shard_map/ppermute | solution.py:304
  5.5 7.8 %collective-permute-start.3 = (bf16[2,2,9216]{2,1,0:T(2,128)(2,1)S(1)}, bf16[2,2,9216]{2,1,0:T(2,128)(2,1)S(1)}, u32[]{:S(2)}, u32[]{:S(2)}) collective-permute-start(bf16[2,2,9216]{2,1,0:T(2,128)(2,1)S(1)} %get-tuple-element.86), channel_id=1, source_target_pairs={{0,8},{1,11},{2,10},{3,9},{4,12},{5,15},{6,14},{7,13},{8,0},{9,3},... | collective-permute-start | bytes 221192 | tf_op jit(solution)/shard_map/ppermute | solution.py:317
  9.5 7.0 %collective-permute-start.2 = (bf16[2,2,9216]{2,1,0:T(2,128)(2,1)S(1)}, bf16[2,2,9216]{2,1,0:T(2,128)(2,1)S(1)}, u32[]{:S(2)}, u32[]{:S(2)}) collective-permute-start(bf16[2,2,9216]{2,1,0:T(2,128)(2,1)S(1)} %get-tuple-element.87), channel_id=1, source_target_pairs={{0,12},{1,15},{2,14},{3,13},{4,8},{5,11},{6,10},{7,9},{8,4},{9,7},... | collective-permute-start | bytes 221192 | tf_op jit(solution)/shard_map/ppermute | solution.py:317
  10.8 6.5 %collective-permute-start.1 = (bf16[2,2,9216]{2,1,0:T(2,128)(2,1)S(1)}, bf16[2,2,9216]{2,1,0:T(2,128)(2,1)S(1)}, u32[]{:S(2)}, u32[]{:S(2)}) collective-permute-start(bf16[2,2,9216]{2,1,0:T(2,128)(2,1)S(1)} %get-tuple-element.88), channel_id=1, source_target_pairs={{0,4},{1,7},{2,6},{3,5},{4,0},{5,3},{6,2},{7,1},{8,12},{9,15},{10,... | collective-permute-start | bytes 221192 | tf_op jit(solution)/shard_map/ppermute | solution.py:317
  11.1 6.4 %copy-start.9 = (bf16[2,2,7424]{2,1,0:T(2,128)(2,1)}, bf16[2,2,7424]{2,1,0:T(2,128)(2,1)S(1)}, u32[]{:S(2)}) copy-start(bf16[2,2,7424]{2,1,0:T(2,128)(2,1)S(1)} %get-tuple-element.85.refs_3_.refs_6_) | copy-start | bytes 178180
  11.1 6.3 %collective-permute-start.7 = (bf16[2,2,7424]{2,1,0:T(2,128)(2,1)S(1)}, bf16[2,2,7424]{2,1,0:T(2,128)(2,1)S(1)}, u32[]{:S(2)}, u32[]{:S(2)}) collective-permute-start(bf16[2,2,7424]{2,1,0:T(2,128)(2,1)S(1)} %get-tuple-element.84), channel_id=1, source_target_pairs={{0,2},{2,0},{1,3},{3,1},{4,6},{6,4},{5,7},{7,5},{8,10},{10,8},{9,1... | collective-permute-start | bytes 178184 | tf_op jit(solution)/shard_map/ppermute | solution.py:308
  13.3 4.1 %copy-start.1 = (bf16[2,2,9216]{2,1,0:T(2,128)(2,1)}, bf16[2,2,9216]{2,1,0:T(2,128)(2,1)S(1)}, u32[]{:S(2)}) copy-start(bf16[2,2,9216]{2,1,0:T(2,128)(2,1)S(1)} %collective-permute-done.3.refs_2_) | copy-start | bytes 221188
  13.3 6.6 %collective-permute-start.6 = (bf16[2,2,9216]{2,1,0:T(2,128)(2,1)S(1)}, bf16[2,2,9216]{2,1,0:T(2,128)(2,1)S(1)}, u32[]{:S(2)}, u32[]{:S(2)}) collective-permute-start(bf16[2,2,9216]{2,1,0:T(2,128)(2,1)S(1)} %collective-permute-done.3.refs_2_), channel_id=1, source_target_pairs={{0,1},{1,0},{2,3},{3,2},{4,5},{5,4},{6,7},{7,6},{8,9},{9,8},{10,11... | collective-permute-start | bytes 221192 | tf_op jit(solution)/shard_map/ppermute | solution.py:318
  16.5 1.0 %copy-start.3 = (bf16[2,2,9216]{2,1,0:T(2,128)(2,1)}, bf16[2,2,9216]{2,1,0:T(2,128)(2,1)S(1)}, u32[]{:S(2)}) copy-start(bf16[2,2,9216]{2,1,0:T(2,128)(2,1)S(1)} %collective-permute-done.2.refs_1_) | copy-start | bytes 221188
  16.5 3.5 %collective-permute-start.5 = (bf16[2,2,9216]{2,1,0:T(2,128)(2,1)S(1)}, bf16[2,2,9216]{2,1,0:T(2,128)(2,1)S(1)}, u32[]{:S(2)}, u32[]{:S(2)}) collective-permute-start(bf16[2,2,9216]{2,1,0:T(2,128)(2,1)S(1)} %collective-permute-done.2.refs_1_), channel_id=1, source_target_pairs={{0,1},{1,0},{2,3},{3,2},{4,5},{5,4},{6,7},{7,6},{8,9},{9,8},{10,11... | collective-permute-start | bytes 221192 | tf_op jit(solution)/shard_map/ppermute | solution.py:318
  17.3 0.6 %copy-start.5 = (bf16[2,2,9216]{2,1,0:T(2,128)(2,1)}, bf16[2,2,9216]{2,1,0:T(2,128)(2,1)S(1)}, u32[]{:S(2)}) copy-start(bf16[2,2,9216]{2,1,0:T(2,128)(2,1)S(1)} %collective-permute-done.1.refs_0_) | copy-start | bytes 221188
  17.3 2.6 %collective-permute-start.4 = (bf16[2,2,9216]{2,1,0:T(2,128)(2,1)S(1)}, bf16[2,2,9216]{2,1,0:T(2,128)(2,1)S(1)}, u32[]{:S(2)}, u32[]{:S(2)}) collective-permute-start(bf16[2,2,9216]{2,1,0:T(2,128)(2,1)S(1)} %collective-permute-done.1.refs_0_), channel_id=1, source_target_pairs={{0,1},{1,0},{2,3},{3,2},{4,5},{5,4},{6,7},{7,6},{8,9},{9,8},{10,11... | collective-permute-start | bytes 221192 | tf_op jit(solution)/shard_map/ppermute | solution.py:318
  17.5 0.6 %copy-start.7 = (bf16[2,2,7424]{2,1,0:T(2,128)(2,1)}, bf16[2,2,7424]{2,1,0:T(2,128)(2,1)S(1)}, u32[]{:S(2)}) copy-start(bf16[2,2,7424]{2,1,0:T(2,128)(2,1)S(1)} %collective-permute-done.7.refs_4_.refs_7_) | copy-start | bytes 178180
  19.9 1.0 %copy-start = (bf16[20,5632]{1,0:T(8,128)(2,1)S(1)}, bf16[20,5632]{1,0:T(8,128)(2,1)}, u32[]{:S(2)}) copy-start(bf16[20,5632]{1,0:T(8,128)(2,1)} %gather_rows.1.refs_8_) | copy-start | bytes 675844
  20.9 0.9 %copy-start.2 = (bf16[2,2,9216]{2,1,0:T(2,128)(2,1)S(1)}, bf16[2,2,9216]{2,1,0:T(2,128)(2,1)}, u32[]{:S(2)}) copy-start(bf16[2,2,9216]{2,1,0:T(2,128)(2,1)} %copy-done.1) | copy-start | bytes 221188
  21.8 0.9 %copy-start.4 = (bf16[2,2,9216]{2,1,0:T(2,128)(2,1)S(1)}, bf16[2,2,9216]{2,1,0:T(2,128)(2,1)}, u32[]{:S(2)}) copy-start(bf16[2,2,9216]{2,1,0:T(2,128)(2,1)} %copy-done.3) | copy-start | bytes 221188
  22.7 0.9 %copy-start.6 = (bf16[2,2,9216]{2,1,0:T(2,128)(2,1)S(1)}, bf16[2,2,9216]{2,1,0:T(2,128)(2,1)}, u32[]{:S(2)}) copy-start(bf16[2,2,9216]{2,1,0:T(2,128)(2,1)} %copy-done.5) | copy-start | bytes 221188
  23.6 0.8 %copy-start.8 = (bf16[2,2,7424]{2,1,0:T(2,128)(2,1)S(1)}, bf16[2,2,7424]{2,1,0:T(2,128)(2,1)}, u32[]{:S(2)}) copy-start(bf16[2,2,7424]{2,1,0:T(2,128)(2,1)} %copy-done.7) | copy-start | bytes 178180
  24.4 0.8 %copy-start.10 = (bf16[2,2,7424]{2,1,0:T(2,128)(2,1)S(1)}, bf16[2,2,7424]{2,1,0:T(2,128)(2,1)}, u32[]{:S(2)}) copy-start(bf16[2,2,7424]{2,1,0:T(2,128)(2,1)} %copy-done.9) | copy-start | bytes 178180

commit v6 on v5

--- a/solution.py
+++ b/solution.py
@@ -189,6 +189,7 @@
         out_shape=jax.ShapeDtypeStruct((2 * CAP * len(blocks), width), BF16),
         in_specs=[VMEM] * len(blocks),
         out_specs=VMEM,
+        compiler_params=pltpu.CompilerParams(vmem_limit_bytes=(2 << 20) + 16 * CAP * len(blocks) * width),
         cost_estimate=pl.CostEstimate(flops=1000000000, bytes_accessed=8 * CAP * len(blocks) * width, transcendentals=0),
         name="gather_rows",
     )(*blocks)

time: 29.7 us -> 22.8 us (0.77)
  local copies, waits for them, and re-layouts: 5.99 us -> 0.13 us
  Pallas kernels: 9.17 us -> 7.48 us
  waiting for transfers between devices: 4.3 us -> 5.25 us
    unnamed x22 -> x0, local copies, waits for them, and re-layouts: 5.86 us -> none
    pallas_call x1, Pallas kernels: 1.85 us -> 0.16 us  [gather_rows(): pl.pallas_call(gather_kernel, out_shape=jax.ShapeDtypeStruct((2 * CAP * l...]
    ppermute x3, waiting for transfers between devices: 0.01 us -> 0.93 us  [local(): there = [lax.ppermute(rows, 'mp', swap) for rows in here]]
  transfers between devices with their start and end apart: 8 -> 8, of which waited for: 3 -> 5; matrix products, arithmetic and copies ran while one was open for 0% -> 0% of each run, Pallas kernels for 6% -> 1%
where the time goes in v6:
time: 22.8 us; the launch traced here: 22.7 us
  starting transfers between devices  8.49 us (37%)
  Pallas kernels  7.48 us (33%)
  waiting for transfers between devices  5.25 us (23%)
  between operations  1.32 us (6%)
    ppermute x3, starting transfers between devices, local(): lax.ppermute(sends[r].at[1].set(got[r]), ('expert', 'dp', 'mp'), pairs)  5.59 us
    pallas_call x1, Pallas kernels, factors(): pl.pallas_call(functools.partial(factor_kernel, act_width, row_out, round...  4.1 us
    ppermute x3, waiting for transfers between devices, local(): lax.ppermute(sends[r].at[1].set(got[r]), ('expert', 'dp', 'mp'), pairs)  3.31 us
    pallas_call x1, Pallas kernels, pack(): pl.pallas_call(functools.partial(pack_kernel, order, blocks, row_out), ou...  3.22 us
    ppermute x1, starting transfers between devices, local(): lax.ppermute(nears[dd], 'dp', [(d, d ^ dd) for d in range(blocks)])  1.55 us
    ppermute x1, waiting for transfers between devices, local(): got = lax.ppermute(give, 'mp', swap)  1.01 us
    ppermute x3, waiting for transfers between devices, local(): there = [lax.ppermute(rows, 'mp', swap) for rows in here]  0.93 us
    ppermute x3, starting transfers between devices, local(): there = [lax.ppermute(rows, 'mp', swap) for rows in here]  0.83 us
  transfers between devices with their start and end apart: 8, of which 5 were waited for; matrix products, arithmetic and copies ran while one was open for 0% of the time, Pallas kernels for 1%

profile of v6, /device:TPU:0, one launch (start us, length us, event | category | flops | bytes accessed | tf_op | source)
XLA Modules:
  0.0 22.7 jit_solution(7710323554616294103)
XLA Ops:
  0.6 3.2 %select_rows_and_rotate_queries.1 = (bf16[2,2,9216]{2,1,0:T(2,128)(2,1)S(1)}, bf16[2,2,9216]{2,1,0:T(2,128)(2,1)S(1)}, bf16[2,2,9216]{2,1,0:T(2,128)(2,1)S(1)}, ...) custom-call(s32[8,24]{1,0:T(8,128)} %bitcast.10, ...), custom_call_target="tpu_custom_call" | custom-call | tf_op jit(solution)/shard_map/select_rows_and_rotate_queries/pallas_call | solution.py:167
  3.9 0.5 %collective-permute-start = (bf16[4,2,9216]{2,1,0:T(2,128)(2,1)S(1)}, bf16[4,2,9216]{2,1,0:T(2,128)(2,1)S(1)}, u32[]{:S(2)}, u32[]{:S(2)}) collective-permute-start(bf16[4,2,9216]{2,1,0:T(2,128)(2,1)S(1)} %get-tuple-element.75), channel_id=1, source_target_pairs={{0,1},{1,0},{2,3},{3,2},{4,5},{5,4},{6,7},{7,6},{8,9},{9,8},{10,11... | collective-permute-start | bytes 442376 | tf_op jit(solution)/shard_map/ppermute | solution.py:305
  4.4 1.0 %collective-permute-done = bf16[4,2,9216]{2,1,0:T(2,128)(2,1)S(1)} collective-permute-done((bf16[4,2,9216]{2,1,0:T(2,128)(2,1)S(1)}, bf16[4,2,9216]{2,1,0:T(2,128)(2,1)S(1)}, u32[]{:S(2)}, u32[]{:S(2)}) %collective-permute-start) | collective-permute-done | bytes 147488 | tf_op jit(solution)/shard_map/ppermute | solution.py:305
  5.4 0.1 slice_dynamic-update-slice_fusion
  5.5 4.0 %collective-permute-start.3 = (bf16[2,2,9216]{2,1,0:T(2,128)(2,1)S(1)}, bf16[2,2,9216]{2,1,0:T(2,128)(2,1)S(1)}, u32[]{:S(2)}, u32[]{:S(2)}) collective-permute-start(bf16[2,2,9216]{2,1,0:T(2,128)(2,1)S(1)} %get-tuple-element.86), channel_id=1, source_target_pairs={{0,8},{1,11},{2,10},{3,9},{4,12},{5,15},{6,14},{7,13},{8,0},{9,3},... | collective-permute-start | bytes 221192 | tf_op jit(solution)/shard_map/ppermute | solution.py:318
  9.5 1.3 %collective-permute-start.2 = (bf16[2,2,9216]{2,1,0:T(2,128)(2,1)S(1)}, bf16[2,2,9216]{2,1,0:T(2,128)(2,1)S(1)}, u32[]{:S(2)}, u32[]{:S(2)}) collective-permute-start(bf16[2,2,9216]{2,1,0:T(2,128)(2,1)S(1)} %get-tuple-element.87), channel_id=1, source_target_pairs={{0,12},{1,15},{2,14},{3,13},{4,8},{5,11},{6,10},{7,9},{8,4},{9,7},... | collective-permute-start | bytes 221192 | tf_op jit(solution)/shard_map/ppermute | solution.py:318
  10.8 0.2 %collective-permute-start.1 = (bf16[2,2,9216]{2,1,0:T(2,128)(2,1)S(1)}, bf16[2,2,9216]{2,1,0:T(2,128)(2,1)S(1)}, u32[]{:S(2)}, u32[]{:S(2)}) collective-permute-start(bf16[2,2,9216]{2,1,0:T(2,128)(2,1)S(1)} %get-tuple-element.88), channel_id=1, source_target_pairs={{0,4},{1,7},{2,6},{3,5},{4,0},{5,3},{6,2},{7,1},{8,12},{9,15},{10,... | collective-permute-start | bytes 221192 | tf_op jit(solution)/shard_map/ppermute | solution.py:318
  11.1 1.6 %collective-permute-start.7 = (bf16[2,2,7424]{2,1,0:T(2,128)(2,1)S(1)}, bf16[2,2,7424]{2,1,0:T(2,128)(2,1)S(1)}, u32[]{:S(2)}, u32[]{:S(2)}) collective-permute-start(bf16[2,2,7424]{2,1,0:T(2,128)(2,1)S(1)} %get-tuple-element.84), channel_id=1, source_target_pairs={{0,2},{2,0},{1,3},{3,1},{4,6},{6,4},{5,7},{7,5},{8,10},{10,8},{9,1... | collective-permute-start | bytes 178184 | tf_op jit(solution)/shard_map/ppermute | solution.py:309
  13.3 0.0 collective-permute-done.3.refs_2_
  13.3 0.3 %collective-permute-start.6 = (bf16[2,2,9216]{2,1,0:T(2,128)(2,1)S(1)}, bf16[2,2,9216]{2,1,0:T(2,128)(2,1)S(1)}, u32[]{:S(2)}, u32[]{:S(2)}) collective-permute-start(bf16[2,2,9216]{2,1,0:T(2,128)(2,1)S(1)} %collective-permute-done.3.refs_2_), channel_id=1, source_target_pairs={{0,1},{1,0},{2,3},{3,2},{4,5},{5,4},{6,7},{7,6},{8,9},{9,8},{10,11... | collective-permute-start | bytes 221192 | tf_op jit(solution)/shard_map/ppermute | solution.py:319
  13.6 2.9 %collective-permute-done.2.refs_1_ = bf16[2,2,9216]{2,1,0:T(2,128)(2,1)S(1)} collective-permute-done((bf16[2,2,9216]{2,1,0:T(2,128)(2,1)S(1)}, bf16[2,2,9216]{2,1,0:T(2,128)(2,1)S(1)}, u32[]{:S(2)}, u32[]{:S(2)}) %collective-permute-start.2) | collective-permute-done | bytes 73760 | tf_op jit(solution)/shard_map/ppermute | solution.py:318
  16.5 0.4 %collective-permute-start.5 = (bf16[2,2,9216]{2,1,0:T(2,128)(2,1)S(1)}, bf16[2,2,9216]{2,1,0:T(2,128)(2,1)S(1)}, u32[]{:S(2)}, u32[]{:S(2)}) collective-permute-start(bf16[2,2,9216]{2,1,0:T(2,128)(2,1)S(1)} %collective-permute-done.2.refs_1_), channel_id=1, source_target_pairs={{0,1},{1,0},{2,3},{3,2},{4,5},{5,4},{6,7},{7,6},{8,9},{9,8},{10,11... | collective-permute-start | bytes 221192 | tf_op jit(solution)/shard_map/ppermute | solution.py:319
  16.9 0.4 %collective-permute-done.1.refs_0_ = bf16[2,2,9216]{2,1,0:T(2,128)(2,1)S(1)} collective-permute-done((bf16[2,2,9216]{2,1,0:T(2,128)(2,1)S(1)}, bf16[2,2,9216]{2,1,0:T(2,128)(2,1)S(1)}, u32[]{:S(2)}, u32[]{:S(2)}) %collective-permute-start.1) | collective-permute-done | bytes 73760 | tf_op jit(solution)/shard_map/ppermute | solution.py:318
  17.3 0.2 collective-permute-start.4
  17.5 0.0 collective-permute-done.7.refs_4_.refs_7_
  17.5 0.2 gather_rows.1.refs_8_
  17.6 0.0 collective-permute-done.6.refs_5_
  17.6 0.2 collective-permute-done.5.refs_4_
  17.8 0.8 %collective-permute-done.4.refs_3_ = bf16[2,2,9216]{2,1,0:T(2,128)(2,1)S(1)} collective-permute-done((bf16[2,2,9216]{2,1,0:T(2,128)(2,1)S(1)}, bf16[2,2,9216]{2,1,0:T(2,128)(2,1)S(1)}, u32[]{:S(2)}, u32[]{:S(2)}) %collective-permute-start.4) | collective-permute-done | bytes 73760 | tf_op jit(solution)/shard_map/ppermute | solution.py:319
  18.6 4.1 %factor_tiles.1 = (bf16[2048,2048]{1,0:T(8,128)(2,1)}, bf16[768,768]{1,0:T(8,128)(2,1)}, bf16[2,1024]{1,0:T(2,128)(2,1)}, bf16[2,768]{1,0:T(2,128)(2,1)}) custom-call(s32[1]{0:T(128)S(6)} %copy.18.count_ref, bf16[2,2,9216]{2,1,0:T(2,128)(2,1)S(1)} %collective-permute-done.1.refs_0_, bf16[2,2,9216]{2,1,0:T(2,128)(2,1)S(1)} %collective-permute-done.2.refs_1_, ...), custom_call_target="tpu_custom_call" | custom-call | tf_op jit(solution)/shard_map/factor_tiles/pallas_call | solution.py:269
  (1 shorter events, 0.0 us)
Async XLA Ops:
  3.9 1.5 %collective-permute-start = (bf16[4,2,9216]{2,1,0:T(2,128)(2,1)S(1)}, bf16[4,2,9216]{2,1,0:T(2,128)(2,1)S(1)}, u32[]{:S(2)}, u32[]{:S(2)}) collective-permute-start(bf16[4,2,9216]{2,1,0:T(2,128)(2,1)S(1)} %get-tuple-element.75), channel_id=1, source_target_pairs={{0,1},{1,0},{2,3},{3,2},{4,5},{5,4},{6,7},{7,6},{8,9},{9,8},{10,11... | collective-permute-start | bytes 442376 | tf_op jit(solution)/shard_map/ppermute | solution.py:305
  5.5 7.8 %collective-permute-start.3 = (bf16[2,2,9216]{2,1,0:T(2,128)(2,1)S(1)}, bf16[2,2,9216]{2,1,0:T(2,128)(2,1)S(1)}, u32[]{:S(2)}, u32[]{:S(2)}) collective-permute-start(bf16[2,2,9216]{2,1,0:T(2,128)(2,1)S(1)} %get-tuple-element.86), channel_id=1, source_target_pairs={{0,8},{1,11},{2,10},{3,9},{4,12},{5,15},{6,14},{7,13},{8,0},{9,3},... | collective-permute-start | bytes 221192 | tf_op jit(solution)/shard_map/ppermute | solution.py:318
  9.5 7.0 %collective-permute-start.2 = (bf16[2,2,9216]{2,1,0:T(2,128)(2,1)S(1)}, bf16[2,2,9216]{2,1,0:T(2,128)(2,1)S(1)}, u32[]{:S(2)}, u32[]{:S(2)}) collective-permute-start(bf16[2,2,9216]{2,1,0:T(2,128)(2,1)S(1)} %get-tuple-element.87), channel_id=1, source_target_pairs={{0,12},{1,15},{2,14},{3,13},{4,8},{5,11},{6,10},{7,9},{8,4},{9,7},... | collective-permute-start | bytes 221192 | tf_op jit(solution)/shard_map/ppermute | solution.py:318
  10.8 6.5 %collective-permute-start.1 = (bf16[2,2,9216]{2,1,0:T(2,128)(2,1)S(1)}, bf16[2,2,9216]{2,1,0:T(2,128)(2,1)S(1)}, u32[]{:S(2)}, u32[]{:S(2)}) collective-permute-start(bf16[2,2,9216]{2,1,0:T(2,128)(2,1)S(1)} %get-tuple-element.88), channel_id=1, source_target_pairs={{0,4},{1,7},{2,6},{3,5},{4,0},{5,3},{6,2},{7,1},{8,12},{9,15},{10,... | collective-permute-start | bytes 221192 | tf_op jit(solution)/shard_map/ppermute | solution.py:318
  11.1 6.4 %collective-permute-start.7 = (bf16[2,2,7424]{2,1,0:T(2,128)(2,1)S(1)}, bf16[2,2,7424]{2,1,0:T(2,128)(2,1)S(1)}, u32[]{:S(2)}, u32[]{:S(2)}) collective-permute-start(bf16[2,2,7424]{2,1,0:T(2,128)(2,1)S(1)} %get-tuple-element.84), channel_id=1, source_target_pairs={{0,2},{2,0},{1,3},{3,1},{4,6},{6,4},{5,7},{7,5},{8,10},{10,8},{9,1... | collective-permute-start | bytes 178184 | tf_op jit(solution)/shard_map/ppermute | solution.py:309
  13.3 4.3 %collective-permute-start.6 = (bf16[2,2,9216]{2,1,0:T(2,128)(2,1)S(1)}, bf16[2,2,9216]{2,1,0:T(2,128)(2,1)S(1)}, u32[]{:S(2)}, u32[]{:S(2)}) collective-permute-start(bf16[2,2,9216]{2,1,0:T(2,128)(2,1)S(1)} %collective-permute-done.3.refs_2_), channel_id=1, source_target_pairs={{0,1},{1,0},{2,3},{3,2},{4,5},{5,4},{6,7},{7,6},{8,9},{9,8},{10,11... | collective-permute-start | bytes 221192 | tf_op jit(solution)/shard_map/ppermute | solution.py:319
  16.5 1.3 %collective-permute-start.5 = (bf16[2,2,9216]{2,1,0:T(2,128)(2,1)S(1)}, bf16[2,2,9216]{2,1,0:T(2,128)(2,1)S(1)}, u32[]{:S(2)}, u32[]{:S(2)}) collective-permute-start(bf16[2,2,9216]{2,1,0:T(2,128)(2,1)S(1)} %collective-permute-done.2.refs_1_), channel_id=1, source_target_pairs={{0,1},{1,0},{2,3},{3,2},{4,5},{5,4},{6,7},{7,6},{8,9},{9,8},{10,11... | collective-permute-start | bytes 221192 | tf_op jit(solution)/shard_map/ppermute | solution.py:319
  17.3 1.3 %collective-permute-start.4 = (bf16[2,2,9216]{2,1,0:T(2,128)(2,1)S(1)}, bf16[2,2,9216]{2,1,0:T(2,128)(2,1)S(1)}, u32[]{:S(2)}, u32[]{:S(2)}) collective-permute-start(bf16[2,2,9216]{2,1,0:T(2,128)(2,1)S(1)} %collective-permute-done.1.refs_0_), channel_id=1, source_target_pairs={{0,1},{1,0},{2,3},{3,2},{4,5},{5,4},{6,7},{7,6},{8,9},{9,8},{10,11... | collective-permute-start | bytes 221192 | tf_op jit(solution)/shard_map/ppermute | solution.py:319

commit v7 on v6

--- a/solution.py
+++ b/solution.py
@@ -219,9 +219,14 @@
         copies.append(copy)
 
     def columns(at, width):
-        span = pl.ds(pl.multiple_of(at, 128), width)
+        extra = 64 if width % 128 else 0
+        start = at - at % 128 if extra else at
+        span = pl.ds(pl.multiple_of(start, 128), width + extra)
         late = [ref[c, :, span] for ref in there for c in range(2)]
-        return jnp.concatenate([ready_ref[:, span]] + late, axis=0)
+        rows = jnp.concatenate([ready_ref[:, span]] + late, axis=0)
+        if extra:
+            rows = jnp.where(at % 128 == 0, rows[:, :width], rows[:, extra:])
+        return rows
 
     def tile(left, right):
         part = lax.dot_general(left, right, contract, preferred_element_type=F32)

time: 22.8 us -> 22.8 us (level)
  no operation moved by 1% of the time
where the time goes in v7:
time: 22.8 us; the launch traced here: 22.7 us
  starting transfers between devices  8.49 us (37%)
  Pallas kernels  7.48 us (33%)
  waiting for transfers between devices  5.25 us (23%)
  between operations  1.32 us (6%)
    ppermute x3, starting transfers between devices, local(): lax.ppermute(sends[r].at[1].set(got[r]), ('expert', 'dp', 'mp'), pairs)  5.59 us
    pallas_call x1, Pallas kernels, factors(): pl.pallas_call(functools.partial(factor_kernel, act_width, row_out, round...  4.1 us
    ppermute x3, waiting for transfers between devices, local(): lax.ppermute(sends[r].at[1].set(got[r]), ('expert', 'dp', 'mp'), pairs)  3.31 us
    pallas_call x1, Pallas kernels, pack(): pl.pallas_call(functools.partial(pack_kernel, order, blocks, row_out), ou...  3.22 us
    ppermute x1, starting transfers between devices, local(): lax.ppermute(nears[dd], 'dp', [(d, d ^ dd) for d in range(blocks)])  1.55 us
    ppermute x1, waiting for transfers between devices, local(): got = lax.ppermute(give, 'mp', swap)  1.01 us
    ppermute x3, waiting for transfers between devices, local(): there = [lax.ppermute(rows, 'mp', swap) for rows in here]  0.93 us
    ppermute x3, starting transfers between devices, local(): there = [lax.ppermute(rows, 'mp', swap) for rows in here]  0.83 us
  transfers between devices with their start and end apart: 8, of which 5 were waited for; matrix products, arithmetic and copies ran while one was open for 0% of the time, Pallas kernels for 1%

profile of v7, /device:TPU:0, one launch (start us, length us, event | category | flops | bytes accessed | tf_op | source)
XLA Modules:
  0.0 22.7 jit_solution(7710323554616294103)
XLA Ops:
  0.6 3.2 %select_rows_and_rotate_queries.1 = (bf16[2,2,9216]{2,1,0:T(2,128)(2,1)S(1)}, bf16[2,2,9216]{2,1,0:T(2,128)(2,1)S(1)}, bf16[2,2,9216]{2,1,0:T(2,128)(2,1)S(1)}, ...) custom-call(s32[8,24]{1,0:T(8,128)} %bitcast.10, ...), custom_call_target="tpu_custom_call" | custom-call | tf_op jit(solution)/shard_map/select_rows_and_rotate_queries/pallas_call | solution.py:167
  3.9 0.5 %collective-permute-start = (bf16[4,2,9216]{2,1,0:T(2,128)(2,1)S(1)}, bf16[4,2,9216]{2,1,0:T(2,128)(2,1)S(1)}, u32[]{:S(2)}, u32[]{:S(2)}) collective-permute-start(bf16[4,2,9216]{2,1,0:T(2,128)(2,1)S(1)} %get-tuple-element.75), channel_id=1, source_target_pairs={{0,1},{1,0},{2,3},{3,2},{4,5},{5,4},{6,7},{7,6},{8,9},{9,8},{10,11... | collective-permute-start | bytes 442376 | tf_op jit(solution)/shard_map/ppermute | solution.py:310
  4.4 1.0 %collective-permute-done = bf16[4,2,9216]{2,1,0:T(2,128)(2,1)S(1)} collective-permute-done((bf16[4,2,9216]{2,1,0:T(2,128)(2,1)S(1)}, bf16[4,2,9216]{2,1,0:T(2,128)(2,1)S(1)}, u32[]{:S(2)}, u32[]{:S(2)}) %collective-permute-start) | collective-permute-done | bytes 147488 | tf_op jit(solution)/shard_map/ppermute | solution.py:310
  5.4 0.1 slice_dynamic-update-slice_fusion
  5.5 4.0 %collective-permute-start.3 = (bf16[2,2,9216]{2,1,0:T(2,128)(2,1)S(1)}, bf16[2,2,9216]{2,1,0:T(2,128)(2,1)S(1)}, u32[]{:S(2)}, u32[]{:S(2)}) collective-permute-start(bf16[2,2,9216]{2,1,0:T(2,128)(2,1)S(1)} %get-tuple-element.86), channel_id=1, source_target_pairs={{0,8},{1,11},{2,10},{3,9},{4,12},{5,15},{6,14},{7,13},{8,0},{9,3},... | collective-permute-start | bytes 221192 | tf_op jit(solution)/shard_map/ppermute | solution.py:323
  9.5 1.3 %collective-permute-start.2 = (bf16[2,2,9216]{2,1,0:T(2,128)(2,1)S(1)}, bf16[2,2,9216]{2,1,0:T(2,128)(2,1)S(1)}, u32[]{:S(2)}, u32[]{:S(2)}) collective-permute-start(bf16[2,2,9216]{2,1,0:T(2,128)(2,1)S(1)} %get-tuple-element.87), channel_id=1, source_target_pairs={{0,12},{1,15},{2,14},{3,13},{4,8},{5,11},{6,10},{7,9},{8,4},{9,7},... | collective-permute-start | bytes 221192 | tf_op jit(solution)/shard_map/ppermute | solution.py:323
  10.8 0.2 %collective-permute-start.1 = (bf16[2,2,9216]{2,1,0:T(2,128)(2,1)S(1)}, bf16[2,2,9216]{2,1,0:T(2,128)(2,1)S(1)}, u32[]{:S(2)}, u32[]{:S(2)}) collective-permute-start(bf16[2,2,9216]{2,1,0:T(2,128)(2,1)S(1)} %get-tuple-element.88), channel_id=1, source_target_pairs={{0,4},{1,7},{2,6},{3,5},{4,0},{5,3},{6,2},{7,1},{8,12},{9,15},{10,... | collective-permute-start | bytes 221192 | tf_op jit(solution)/shard_map/ppermute | solution.py:323
  11.1 1.6 %collective-permute-start.7 = (bf16[2,2,7424]{2,1,0:T(2,128)(2,1)S(1)}, bf16[2,2,7424]{2,1,0:T(2,128)(2,1)S(1)}, u32[]{:S(2)}, u32[]{:S(2)}) collective-permute-start(bf16[2,2,7424]{2,1,0:T(2,128)(2,1)S(1)} %get-tuple-element.84), channel_id=1, source_target_pairs={{0,2},{2,0},{1,3},{3,1},{4,6},{6,4},{5,7},{7,5},{8,10},{10,8},{9,1... | collective-permute-start | bytes 178184 | tf_op jit(solution)/shard_map/ppermute | solution.py:314
  13.3 0.0 collective-permute-done.3.refs_2_
  13.3 0.3 %collective-permute-start.6 = (bf16[2,2,9216]{2,1,0:T(2,128)(2,1)S(1)}, bf16[2,2,9216]{2,1,0:T(2,128)(2,1)S(1)}, u32[]{:S(2)}, u32[]{:S(2)}) collective-permute-start(bf16[2,2,9216]{2,1,0:T(2,128)(2,1)S(1)} %collective-permute-done.3.refs_2_), channel_id=1, source_target_pairs={{0,1},{1,0},{2,3},{3,2},{4,5},{5,4},{6,7},{7,6},{8,9},{9,8},{10,11... | collective-permute-start | bytes 221192 | tf_op jit(solution)/shard_map/ppermute | solution.py:324
  13.6 2.9 %collective-permute-done.2.refs_1_ = bf16[2,2,9216]{2,1,0:T(2,128)(2,1)S(1)} collective-permute-done((bf16[2,2,9216]{2,1,0:T(2,128)(2,1)S(1)}, bf16[2,2,9216]{2,1,0:T(2,128)(2,1)S(1)}, u32[]{:S(2)}, u32[]{:S(2)}) %collective-permute-start.2) | collective-permute-done | bytes 73760 | tf_op jit(solution)/shard_map/ppermute | solution.py:323
  16.5 0.4 %collective-permute-start.5 = (bf16[2,2,9216]{2,1,0:T(2,128)(2,1)S(1)}, bf16[2,2,9216]{2,1,0:T(2,128)(2,1)S(1)}, u32[]{:S(2)}, u32[]{:S(2)}) collective-permute-start(bf16[2,2,9216]{2,1,0:T(2,128)(2,1)S(1)} %collective-permute-done.2.refs_1_), channel_id=1, source_target_pairs={{0,1},{1,0},{2,3},{3,2},{4,5},{5,4},{6,7},{7,6},{8,9},{9,8},{10,11... | collective-permute-start | bytes 221192 | tf_op jit(solution)/shard_map/ppermute | solution.py:324
  16.9 0.4 %collective-permute-done.1.refs_0_ = bf16[2,2,9216]{2,1,0:T(2,128)(2,1)S(1)} collective-permute-done((bf16[2,2,9216]{2,1,0:T(2,128)(2,1)S(1)}, bf16[2,2,9216]{2,1,0:T(2,128)(2,1)S(1)}, u32[]{:S(2)}, u32[]{:S(2)}) %collective-permute-start.1) | collective-permute-done | bytes 73760 | tf_op jit(solution)/shard_map/ppermute | solution.py:323
  17.3 0.2 collective-permute-start.4
  17.5 0.0 collective-permute-done.7.refs_4_.refs_7_
  17.5 0.2 gather_rows.1.refs_8_
  17.6 0.0 collective-permute-done.6.refs_5_
  17.6 0.2 collective-permute-done.5.refs_4_
  17.8 0.8 %collective-permute-done.4.refs_3_ = bf16[2,2,9216]{2,1,0:T(2,128)(2,1)S(1)} collective-permute-done((bf16[2,2,9216]{2,1,0:T(2,128)(2,1)S(1)}, bf16[2,2,9216]{2,1,0:T(2,128)(2,1)S(1)}, u32[]{:S(2)}, u32[]{:S(2)}) %collective-permute-start.4) | collective-permute-done | bytes 73760 | tf_op jit(solution)/shard_map/ppermute | solution.py:324
  18.6 4.1 %factor_tiles.1 = (bf16[2048,2048]{1,0:T(8,128)(2,1)}, bf16[768,768]{1,0:T(8,128)(2,1)}, bf16[2,1024]{1,0:T(2,128)(2,1)}, bf16[2,768]{1,0:T(2,128)(2,1)}) custom-call(s32[1]{0:T(128)S(6)} %copy.18.count_ref, bf16[2,2,9216]{2,1,0:T(2,128)(2,1)S(1)} %collective-permute-done.1.refs_0_, bf16[2,2,9216]{2,1,0:T(2,128)(2,1)S(1)} %collective-permute-done.2.refs_1_, ...), custom_call_target="tpu_custom_call" | custom-call | tf_op jit(solution)/shard_map/factor_tiles/pallas_call | solution.py:274
  (1 shorter events, 0.0 us)
Async XLA Ops:
  3.9 1.5 %collective-permute-start = (bf16[4,2,9216]{2,1,0:T(2,128)(2,1)S(1)}, bf16[4,2,9216]{2,1,0:T(2,128)(2,1)S(1)}, u32[]{:S(2)}, u32[]{:S(2)}) collective-permute-start(bf16[4,2,9216]{2,1,0:T(2,128)(2,1)S(1)} %get-tuple-element.75), channel_id=1, source_target_pairs={{0,1},{1,0},{2,3},{3,2},{4,5},{5,4},{6,7},{7,6},{8,9},{9,8},{10,11... | collective-permute-start | bytes 442376 | tf_op jit(solution)/shard_map/ppermute | solution.py:310
  5.5 7.8 %collective-permute-start.3 = (bf16[2,2,9216]{2,1,0:T(2,128)(2,1)S(1)}, bf16[2,2,9216]{2,1,0:T(2,128)(2,1)S(1)}, u32[]{:S(2)}, u32[]{:S(2)}) collective-permute-start(bf16[2,2,9216]{2,1,0:T(2,128)(2,1)S(1)} %get-tuple-element.86), channel_id=1, source_target_pairs={{0,8},{1,11},{2,10},{3,9},{4,12},{5,15},{6,14},{7,13},{8,0},{9,3},... | collective-permute-start | bytes 221192 | tf_op jit(solution)/shard_map/ppermute | solution.py:323
  9.5 7.0 %collective-permute-start.2 = (bf16[2,2,9216]{2,1,0:T(2,128)(2,1)S(1)}, bf16[2,2,9216]{2,1,0:T(2,128)(2,1)S(1)}, u32[]{:S(2)}, u32[]{:S(2)}) collective-permute-start(bf16[2,2,9216]{2,1,0:T(2,128)(2,1)S(1)} %get-tuple-element.87), channel_id=1, source_target_pairs={{0,12},{1,15},{2,14},{3,13},{4,8},{5,11},{6,10},{7,9},{8,4},{9,7},... | collective-permute-start | bytes 221192 | tf_op jit(solution)/shard_map/ppermute | solution.py:323
  10.8 6.5 %collective-permute-start.1 = (bf16[2,2,9216]{2,1,0:T(2,128)(2,1)S(1)}, bf16[2,2,9216]{2,1,0:T(2,128)(2,1)S(1)}, u32[]{:S(2)}, u32[]{:S(2)}) collective-permute-start(bf16[2,2,9216]{2,1,0:T(2,128)(2,1)S(1)} %get-tuple-element.88), channel_id=1, source_target_pairs={{0,4},{1,7},{2,6},{3,5},{4,0},{5,3},{6,2},{7,1},{8,12},{9,15},{10,... | collective-permute-start | bytes 221192 | tf_op jit(solution)/shard_map/ppermute | solution.py:323
  11.1 6.4 %collective-permute-start.7 = (bf16[2,2,7424]{2,1,0:T(2,128)(2,1)S(1)}, bf16[2,2,7424]{2,1,0:T(2,128)(2,1)S(1)}, u32[]{:S(2)}, u32[]{:S(2)}) collective-permute-start(bf16[2,2,7424]{2,1,0:T(2,128)(2,1)S(1)} %get-tuple-element.84), channel_id=1, source_target_pairs={{0,2},{2,0},{1,3},{3,1},{4,6},{6,4},{5,7},{7,5},{8,10},{10,8},{9,1... | collective-permute-start | bytes 178184 | tf_op jit(solution)/shard_map/ppermute | solution.py:314
  13.3 4.3 %collective-permute-start.6 = (bf16[2,2,9216]{2,1,0:T(2,128)(2,1)S(1)}, bf16[2,2,9216]{2,1,0:T(2,128)(2,1)S(1)}, u32[]{:S(2)}, u32[]{:S(2)}) collective-permute-start(bf16[2,2,9216]{2,1,0:T(2,128)(2,1)S(1)} %collective-permute-done.3.refs_2_), channel_id=1, source_target_pairs={{0,1},{1,0},{2,3},{3,2},{4,5},{5,4},{6,7},{7,6},{8,9},{9,8},{10,11... | collective-permute-start | bytes 221192 | tf_op jit(solution)/shard_map/ppermute | solution.py:324
  16.5 1.3 %collective-permute-start.5 = (bf16[2,2,9216]{2,1,0:T(2,128)(2,1)S(1)}, bf16[2,2,9216]{2,1,0:T(2,128)(2,1)S(1)}, u32[]{:S(2)}, u32[]{:S(2)}) collective-permute-start(bf16[2,2,9216]{2,1,0:T(2,128)(2,1)S(1)} %collective-permute-done.2.refs_1_), channel_id=1, source_target_pairs={{0,1},{1,0},{2,3},{3,2},{4,5},{5,4},{6,7},{7,6},{8,9},{9,8},{10,11... | collective-permute-start | bytes 221192 | tf_op jit(solution)/shard_map/ppermute | solution.py:324
  17.3 1.3 %collective-permute-start.4 = (bf16[2,2,9216]{2,1,0:T(2,128)(2,1)S(1)}, bf16[2,2,9216]{2,1,0:T(2,128)(2,1)S(1)}, u32[]{:S(2)}, u32[]{:S(2)}) collective-permute-start(bf16[2,2,9216]{2,1,0:T(2,128)(2,1)S(1)} %collective-permute-done.1.refs_0_), channel_id=1, source_target_pairs={{0,1},{1,0},{2,3},{3,2},{4,5},{5,4},{6,7},{7,6},{8,9},{9,8},{10,11... | collective-permute-start | bytes 221192 | tf_op jit(solution)/shard_map/ppermute | solution.py:324

commit v8 on v7

--- a/solution.py
+++ b/solution.py
@@ -8,7 +8,7 @@
 from jax.sharding import PartitionSpec as P
 
 CAP = 2
-CHUNKS = 8
+CHUNKS = (3, 3, 3, 3, 2, 1, 1)
 F32 = jnp.float32
 BF16 = jnp.bfloat16
 HBM = pl.BlockSpec(memory_space=pltpu.HBM)
@@ -39,8 +39,8 @@
     half = len(order[0])
     send_refs, near_refs, give_ref = refs[8 : 8 + half], refs[8 + half : 8 + half + blocks], refs[8 + half + blocks]
     assign_ref, tokens_ref, pseudo_ref, qe_ref, qa_ref, qg_ref, ba_ref, bg_ref, sems = refs[9 + half + blocks :]
-    chunks = CHUNKS
-    deep = ba_ref.shape[0] // chunks
+    deep = ba_ref.shape[0] // sum(CHUNKS)
+    spans = [(sum(CHUNKS[:i]) * deep, part * deep) for i, part in enumerate(CHUNKS)]
     small = [
         pltpu.make_async_copy(src, dst, sems.at[i])
         for i, (src, dst) in enumerate(
@@ -57,9 +57,9 @@
     ]
     large = [
         pltpu.make_async_copy(
-            ba_hbm.at[pl.ds(i * deep, deep)], ba_ref.at[pl.ds(i * deep, deep)], sems.at[len(small) + i]
+            ba_hbm.at[pl.ds(at, size)], ba_ref.at[pl.ds(at, size)], sems.at[len(small) + i]
         )
-        for i in range(chunks)
+        for i, (at, size) in enumerate(spans)
     ]
     for copy in small + large:
         copy.start()
@@ -149,9 +149,9 @@
     small[6].wait()
     put_pair(act_cols, dot(my_grad, bg_ref[...]))
     act_part = jnp.zeros((my_act.shape[0], act_cols), F32)
-    for c in range(chunks):
-        large[c].wait()
-        act_part += dot(my_act[:, c * deep : (c + 1) * deep], ba_ref[c * deep : (c + 1) * deep])
+    for copy, (at, size) in zip(large, spans):
+        copy.wait()
+        act_part += dot(my_act[:, at : at + size], ba_ref[at : at + size])
     put_pair(0, act_part)
 
 
@@ -170,7 +170,7 @@
         in_specs=[HBM] * len(operands),
         out_specs=(VMEM,) * (half + blocks + 1),
         scratch_shapes=[pltpu.VMEM(x.shape, x.dtype) for x in operands]
-        + [pltpu.SemaphoreType.DMA((7 + CHUNKS,))],
+        + [pltpu.SemaphoreType.DMA((7 + len(CHUNKS),))],
         compiler_params=pltpu.CompilerParams(vmem_limit_bytes=32 * 1024 * 1024),
         name="select_rows_and_rotate_queries",
     )(*operands)

time: 22.8 us -> 22.8 us (level)
  no operation moved by 1% of the time
where the time goes in v8:
time: 22.8 us; the launch traced here: 22.6 us
  starting transfers between devices  8.49 us (37%)
  Pallas kernels  7.43 us (33%)
  waiting for transfers between devices  5.25 us (23%)
  between operations  1.32 us (6%)
    ppermute x3, starting transfers between devices, local(): lax.ppermute(sends[r].at[1].set(got[r]), ('expert', 'dp', 'mp'), pairs)  5.59 us
    pallas_call x1, Pallas kernels, factors(): pl.pallas_call(functools.partial(factor_kernel, act_width, row_out, round...  4.1 us
    ppermute x3, waiting for transfers between devices, local(): lax.ppermute(sends[r].at[1].set(got[r]), ('expert', 'dp', 'mp'), pairs)  3.31 us
    pallas_call x1, Pallas kernels, pack(): pl.pallas_call(functools.partial(pack_kernel, order, blocks, row_out), ou...  3.18 us
    ppermute x1, starting transfers between devices, local(): lax.ppermute(nears[dd], 'dp', [(d, d ^ dd) for d in range(blocks)])  1.55 us
    ppermute x1, waiting for transfers between devices, local(): got = lax.ppermute(give, 'mp', swap)  1.01 us
    ppermute x3, waiting for transfers between devices, local(): there = [lax.ppermute(rows, 'mp', swap) for rows in here]  0.93 us
    ppermute x3, starting transfers between devices, local(): there = [lax.ppermute(rows, 'mp', swap) for rows in here]  0.83 us
  transfers between devices with their start and end apart: 8, of which 5 were waited for; matrix products, arithmetic and copies ran while one was open for 0% of the time, Pallas kernels for 1%

profile of v8, /device:TPU:0, one launch (start us, length us, event | category | flops | bytes accessed | tf_op | source)
XLA Modules:
  0.0 22.6 jit_solution(4549946505021204542)
XLA Ops:
  0.6 3.2 %select_rows_and_rotate_queries.1 = (bf16[2,2,9216]{2,1,0:T(2,128)(2,1)S(1)}, bf16[2,2,9216]{2,1,0:T(2,128)(2,1)S(1)}, bf16[2,2,9216]{2,1,0:T(2,128)(2,1)S(1)}, ...) custom-call(s32[8,24]{1,0:T(8,128)} %bitcast.10, ...), custom_call_target="tpu_custom_call" | custom-call | tf_op jit(solution)/shard_map/select_rows_and_rotate_queries/pallas_call | solution.py:167
  3.8 0.5 %collective-permute-start = (bf16[4,2,9216]{2,1,0:T(2,128)(2,1)S(1)}, bf16[4,2,9216]{2,1,0:T(2,128)(2,1)S(1)}, u32[]{:S(2)}, u32[]{:S(2)}) collective-permute-start(bf16[4,2,9216]{2,1,0:T(2,128)(2,1)S(1)} %get-tuple-element.75), channel_id=1, source_target_pairs={{0,1},{1,0},{2,3},{3,2},{4,5},{5,4},{6,7},{7,6},{8,9},{9,8},{10,11... | collective-permute-start | bytes 442376 | tf_op jit(solution)/shard_map/ppermute | solution.py:310
  4.3 1.0 %collective-permute-done = bf16[4,2,9216]{2,1,0:T(2,128)(2,1)S(1)} collective-permute-done((bf16[4,2,9216]{2,1,0:T(2,128)(2,1)S(1)}, bf16[4,2,9216]{2,1,0:T(2,128)(2,1)S(1)}, u32[]{:S(2)}, u32[]{:S(2)}) %collective-permute-start) | collective-permute-done | bytes 147488 | tf_op jit(solution)/shard_map/ppermute | solution.py:310
  5.3 0.1 slice_dynamic-update-slice_fusion
  5.4 4.0 %collective-permute-start.3 = (bf16[2,2,9216]{2,1,0:T(2,128)(2,1)S(1)}, bf16[2,2,9216]{2,1,0:T(2,128)(2,1)S(1)}, u32[]{:S(2)}, u32[]{:S(2)}) collective-permute-start(bf16[2,2,9216]{2,1,0:T(2,128)(2,1)S(1)} %get-tuple-element.86), channel_id=1, source_target_pairs={{0,8},{1,11},{2,10},{3,9},{4,12},{5,15},{6,14},{7,13},{8,0},{9,3},... | collective-permute-start | bytes 221192 | tf_op jit(solution)/shard_map/ppermute | solution.py:323
  9.4 1.3 %collective-permute-start.2 = (bf16[2,2,9216]{2,1,0:T(2,128)(2,1)S(1)}, bf16[2,2,9216]{2,1,0:T(2,128)(2,1)S(1)}, u32[]{:S(2)}, u32[]{:S(2)}) collective-permute-start(bf16[2,2,9216]{2,1,0:T(2,128)(2,1)S(1)} %get-tuple-element.87), channel_id=1, source_target_pairs={{0,12},{1,15},{2,14},{3,13},{4,8},{5,11},{6,10},{7,9},{8,4},{9,7},... | collective-permute-start | bytes 221192 | tf_op jit(solution)/shard_map/ppermute | solution.py:323
  10.8 0.2 %collective-permute-start.1 = (bf16[2,2,9216]{2,1,0:T(2,128)(2,1)S(1)}, bf16[2,2,9216]{2,1,0:T(2,128)(2,1)S(1)}, u32[]{:S(2)}, u32[]{:S(2)}) collective-permute-start(bf16[2,2,9216]{2,1,0:T(2,128)(2,1)S(1)} %get-tuple-element.88), channel_id=1, source_target_pairs={{0,4},{1,7},{2,6},{3,5},{4,0},{5,3},{6,2},{7,1},{8,12},{9,15},{10,... | collective-permute-start | bytes 221192 | tf_op jit(solution)/shard_map/ppermute | solution.py:323
  11.1 1.6 %collective-permute-start.7 = (bf16[2,2,7424]{2,1,0:T(2,128)(2,1)S(1)}, bf16[2,2,7424]{2,1,0:T(2,128)(2,1)S(1)}, u32[]{:S(2)}, u32[]{:S(2)}) collective-permute-start(bf16[2,2,7424]{2,1,0:T(2,128)(2,1)S(1)} %get-tuple-element.84), channel_id=1, source_target_pairs={{0,2},{2,0},{1,3},{3,1},{4,6},{6,4},{5,7},{7,5},{8,10},{10,8},{9,1... | collective-permute-start | bytes 178184 | tf_op jit(solution)/shard_map/ppermute | solution.py:314
  13.3 0.0 collective-permute-done.3.refs_2_
  13.3 0.3 %collective-permute-start.6 = (bf16[2,2,9216]{2,1,0:T(2,128)(2,1)S(1)}, bf16[2,2,9216]{2,1,0:T(2,128)(2,1)S(1)}, u32[]{:S(2)}, u32[]{:S(2)}) collective-permute-start(bf16[2,2,9216]{2,1,0:T(2,128)(2,1)S(1)} %collective-permute-done.3.refs_2_), channel_id=1, source_target_pairs={{0,1},{1,0},{2,3},{3,2},{4,5},{5,4},{6,7},{7,6},{8,9},{9,8},{10,11... | collective-permute-start | bytes 221192 | tf_op jit(solution)/shard_map/ppermute | solution.py:324
  13.6 2.9 %collective-permute-done.2.refs_1_ = bf16[2,2,9216]{2,1,0:T(2,128)(2,1)S(1)} collective-permute-done((bf16[2,2,9216]{2,1,0:T(2,128)(2,1)S(1)}, bf16[2,2,9216]{2,1,0:T(2,128)(2,1)S(1)}, u32[]{:S(2)}, u32[]{:S(2)}) %collective-permute-start.2) | collective-permute-done | bytes 73760 | tf_op jit(solution)/shard_map/ppermute | solution.py:323
  16.4 0.4 %collective-permute-start.5 = (bf16[2,2,9216]{2,1,0:T(2,128)(2,1)S(1)}, bf16[2,2,9216]{2,1,0:T(2,128)(2,1)S(1)}, u32[]{:S(2)}, u32[]{:S(2)}) collective-permute-start(bf16[2,2,9216]{2,1,0:T(2,128)(2,1)S(1)} %collective-permute-done.2.refs_1_), channel_id=1, source_target_pairs={{0,1},{1,0},{2,3},{3,2},{4,5},{5,4},{6,7},{7,6},{8,9},{9,8},{10,11... | collective-permute-start | bytes 221192 | tf_op jit(solution)/shard_map/ppermute | solution.py:324
  16.8 0.4 %collective-permute-done.1.refs_0_ = bf16[2,2,9216]{2,1,0:T(2,128)(2,1)S(1)} collective-permute-done((bf16[2,2,9216]{2,1,0:T(2,128)(2,1)S(1)}, bf16[2,2,9216]{2,1,0:T(2,128)(2,1)S(1)}, u32[]{:S(2)}, u32[]{:S(2)}) %collective-permute-start.1) | collective-permute-done | bytes 73760 | tf_op jit(solution)/shard_map/ppermute | solution.py:323
  17.2 0.2 collective-permute-start.4
  17.4 0.0 collective-permute-done.7.refs_4_.refs_7_
  17.4 0.2 gather_rows.1.refs_8_
  17.6 0.0 collective-permute-done.6.refs_5_
  17.6 0.2 collective-permute-done.5.refs_4_
  17.7 0.8 %collective-permute-done.4.refs_3_ = bf16[2,2,9216]{2,1,0:T(2,128)(2,1)S(1)} collective-permute-done((bf16[2,2,9216]{2,1,0:T(2,128)(2,1)S(1)}, bf16[2,2,9216]{2,1,0:T(2,128)(2,1)S(1)}, u32[]{:S(2)}, u32[]{:S(2)}) %collective-permute-start.4) | collective-permute-done | bytes 73760 | tf_op jit(solution)/shard_map/ppermute | solution.py:324
  18.5 4.1 %factor_tiles.1 = (bf16[2048,2048]{1,0:T(8,128)(2,1)}, bf16[768,768]{1,0:T(8,128)(2,1)}, bf16[2,1024]{1,0:T(2,128)(2,1)}, bf16[2,768]{1,0:T(2,128)(2,1)}) custom-call(s32[1]{0:T(128)S(6)} %copy.18.count_ref, bf16[2,2,9216]{2,1,0:T(2,128)(2,1)S(1)} %collective-permute-done.1.refs_0_, bf16[2,2,9216]{2,1,0:T(2,128)(2,1)S(1)} %collective-permute-done.2.refs_1_, ...), custom_call_target="tpu_custom_call" | custom-call | tf_op jit(solution)/shard_map/factor_tiles/pallas_call | solution.py:274
  (1 shorter events, 0.0 us)
Async XLA Ops:
  3.8 1.5 %collective-permute-start = (bf16[4,2,9216]{2,1,0:T(2,128)(2,1)S(1)}, bf16[4,2,9216]{2,1,0:T(2,128)(2,1)S(1)}, u32[]{:S(2)}, u32[]{:S(2)}) collective-permute-start(bf16[4,2,9216]{2,1,0:T(2,128)(2,1)S(1)} %get-tuple-element.75), channel_id=1, source_target_pairs={{0,1},{1,0},{2,3},{3,2},{4,5},{5,4},{6,7},{7,6},{8,9},{9,8},{10,11... | collective-permute-start | bytes 442376 | tf_op jit(solution)/shard_map/ppermute | solution.py:310
  5.4 7.8 %collective-permute-start.3 = (bf16[2,2,9216]{2,1,0:T(2,128)(2,1)S(1)}, bf16[2,2,9216]{2,1,0:T(2,128)(2,1)S(1)}, u32[]{:S(2)}, u32[]{:S(2)}) collective-permute-start(bf16[2,2,9216]{2,1,0:T(2,128)(2,1)S(1)} %get-tuple-element.86), channel_id=1, source_target_pairs={{0,8},{1,11},{2,10},{3,9},{4,12},{5,15},{6,14},{7,13},{8,0},{9,3},... | collective-permute-start | bytes 221192 | tf_op jit(solution)/shard_map/ppermute | solution.py:323
  9.4 7.0 %collective-permute-start.2 = (bf16[2,2,9216]{2,1,0:T(2,128)(2,1)S(1)}, bf16[2,2,9216]{2,1,0:T(2,128)(2,1)S(1)}, u32[]{:S(2)}, u32[]{:S(2)}) collective-permute-start(bf16[2,2,9216]{2,1,0:T(2,128)(2,1)S(1)} %get-tuple-element.87), channel_id=1, source_target_pairs={{0,12},{1,15},{2,14},{3,13},{4,8},{5,11},{6,10},{7,9},{8,4},{9,7},... | collective-permute-start | bytes 221192 | tf_op jit(solution)/shard_map/ppermute | solution.py:323
  10.8 6.5 %collective-permute-start.1 = (bf16[2,2,9216]{2,1,0:T(2,128)(2,1)S(1)}, bf16[2,2,9216]{2,1,0:T(2,128)(2,1)S(1)}, u32[]{:S(2)}, u32[]{:S(2)}) collective-permute-start(bf16[2,2,9216]{2,1,0:T(2,128)(2,1)S(1)} %get-tuple-element.88), channel_id=1, source_target_pairs={{0,4},{1,7},{2,6},{3,5},{4,0},{5,3},{6,2},{7,1},{8,12},{9,15},{10,... | collective-permute-start | bytes 221192 | tf_op jit(solution)/shard_map/ppermute | solution.py:323
  11.1 6.4 %collective-permute-start.7 = (bf16[2,2,7424]{2,1,0:T(2,128)(2,1)S(1)}, bf16[2,2,7424]{2,1,0:T(2,128)(2,1)S(1)}, u32[]{:S(2)}, u32[]{:S(2)}) collective-permute-start(bf16[2,2,7424]{2,1,0:T(2,128)(2,1)S(1)} %get-tuple-element.84), channel_id=1, source_target_pairs={{0,2},{2,0},{1,3},{3,1},{4,6},{6,4},{5,7},{7,5},{8,10},{10,8},{9,1... | collective-permute-start | bytes 178184 | tf_op jit(solution)/shard_map/ppermute | solution.py:314
  13.3 4.3 %collective-permute-start.6 = (bf16[2,2,9216]{2,1,0:T(2,128)(2,1)S(1)}, bf16[2,2,9216]{2,1,0:T(2,128)(2,1)S(1)}, u32[]{:S(2)}, u32[]{:S(2)}) collective-permute-start(bf16[2,2,9216]{2,1,0:T(2,128)(2,1)S(1)} %collective-permute-done.3.refs_2_), channel_id=1, source_target_pairs={{0,1},{1,0},{2,3},{3,2},{4,5},{5,4},{6,7},{7,6},{8,9},{9,8},{10,11... | collective-permute-start | bytes 221192 | tf_op jit(solution)/shard_map/ppermute | solution.py:324
  16.4 1.3 %collective-permute-start.5 = (bf16[2,2,9216]{2,1,0:T(2,128)(2,1)S(1)}, bf16[2,2,9216]{2,1,0:T(2,128)(2,1)S(1)}, u32[]{:S(2)}, u32[]{:S(2)}) collective-permute-start(bf16[2,2,9216]{2,1,0:T(2,128)(2,1)S(1)} %collective-permute-done.2.refs_1_), channel_id=1, source_target_pairs={{0,1},{1,0},{2,3},{3,2},{4,5},{5,4},{6,7},{7,6},{8,9},{9,8},{10,11... | collective-permute-start | bytes 221192 | tf_op jit(solution)/shard_map/ppermute | solution.py:324
  17.2 1.3 %collective-permute-start.4 = (bf16[2,2,9216]{2,1,0:T(2,128)(2,1)S(1)}, bf16[2,2,9216]{2,1,0:T(2,128)(2,1)S(1)}, u32[]{:S(2)}, u32[]{:S(2)}) collective-permute-start(bf16[2,2,9216]{2,1,0:T(2,128)(2,1)S(1)} %collective-permute-done.1.refs_0_), channel_id=1, source_target_pairs={{0,1},{1,0},{2,3},{3,2},{4,5},{5,4},{6,7},{7,6},{8,9},{9,8},{10,11... | collective-permute-start | bytes 221192 | tf_op jit(solution)/shard_map/ppermute | solution.py:324

commit v9 on v8

--- a/solution.py
+++ b/solution.py
@@ -196,7 +196,7 @@
 
 
 def row_steps(rows):
-    return [(i * 128, 64 if i < 2 else 128) for i in range(rows // 128)]
+    return [(i * 128, 64 if i < 4 else 128) for i in range(rows // 128)]
 
 
 def factor_kernel(act_width, row_out, rounds, blocks, count_ref, *refs):
@@ -278,7 +278,7 @@
         out_specs=(HBM,) * 4,
         scratch_shapes=[pltpu.VMEM((2 * CAP * (2 * rounds + blocks), act_tile[1]), BF16)]
         + [pltpu.VMEM(shape, BF16) for shape in shapes]
-        + [pltpu.SemaphoreType.DMA((act_tile[0] // 128 + 5,))],
+        + [pltpu.SemaphoreType.DMA((act_tile[0] // 128 + 7,))],
         compiler_params=pltpu.CompilerParams(vmem_limit_bytes=40 * 1024 * 1024),
         name="factor_tiles",
     )(counts, *here, *there, *near, ready)

time: 22.8 us -> 22.8 us (level)
  no operation moved by 1% of the time
where the time goes in v9:
time: 22.8 us; the launch traced here: 22.6 us
  starting transfers between devices  8.49 us (37%)
  Pallas kernels  7.46 us (33%)
  waiting for transfers between devices  5.25 us (23%)
  between operations  1.32 us (6%)
    ppermute x3, starting transfers between devices, local(): lax.ppermute(sends[r].at[1].set(got[r]), ('expert', 'dp', 'mp'), pairs)  5.59 us
    pallas_call x1, Pallas kernels, factors(): pl.pallas_call(functools.partial(factor_kernel, act_width, row_out, round...  4.13 us
    ppermute x3, waiting for transfers between devices, local(): lax.ppermute(sends[r].at[1].set(got[r]), ('expert', 'dp', 'mp'), pairs)  3.31 us
    pallas_call x1, Pallas kernels, pack(): pl.pallas_call(functools.partial(pack_kernel, order, blocks, row_out), ou...  3.18 us
    ppermute x1, starting transfers between devices, local(): lax.ppermute(nears[dd], 'dp', [(d, d ^ dd) for d in range(blocks)])  1.55 us
    ppermute x1, waiting for transfers between devices, local(): got = lax.ppermute(give, 'mp', swap)  1.01 us
    ppermute x3, waiting for transfers between devices, local(): there = [lax.ppermute(rows, 'mp', swap) for rows in here]  0.93 us
    ppermute x3, starting transfers between devices, local(): there = [lax.ppermute(rows, 'mp', swap) for rows in here]  0.83 us
  transfers between devices with their start and end apart: 8, of which 5 were waited for; matrix products, arithmetic and copies ran while one was open for 0% of the time, Pallas kernels for 1%

profile of v9, /device:TPU:0, one launch (start us, length us, event | category | flops | bytes accessed | tf_op | source)
XLA Modules:
  0.0 22.6 jit_solution(7524042905597002966)
XLA Ops:
  0.6 3.2 %select_rows_and_rotate_queries.1 = (bf16[2,2,9216]{2,1,0:T(2,128)(2,1)S(1)}, bf16[2,2,9216]{2,1,0:T(2,128)(2,1)S(1)}, bf16[2,2,9216]{2,1,0:T(2,128)(2,1)S(1)}, ...) custom-call(s32[8,24]{1,0:T(8,128)} %bitcast.10, ...), custom_call_target="tpu_custom_call" | custom-call | tf_op jit(solution)/shard_map/select_rows_and_rotate_queries/pallas_call | solution.py:167
  3.8 0.5 %collective-permute-start = (bf16[4,2,9216]{2,1,0:T(2,128)(2,1)S(1)}, bf16[4,2,9216]{2,1,0:T(2,128)(2,1)S(1)}, u32[]{:S(2)}, u32[]{:S(2)}) collective-permute-start(bf16[4,2,9216]{2,1,0:T(2,128)(2,1)S(1)} %get-tuple-element.75), channel_id=1, source_target_pairs={{0,1},{1,0},{2,3},{3,2},{4,5},{5,4},{6,7},{7,6},{8,9},{9,8},{10,11... | collective-permute-start | bytes 442376 | tf_op jit(solution)/shard_map/ppermute | solution.py:310
  4.3 1.0 %collective-permute-done = bf16[4,2,9216]{2,1,0:T(2,128)(2,1)S(1)} collective-permute-done((bf16[4,2,9216]{2,1,0:T(2,128)(2,1)S(1)}, bf16[4,2,9216]{2,1,0:T(2,128)(2,1)S(1)}, u32[]{:S(2)}, u32[]{:S(2)}) %collective-permute-start) | collective-permute-done | bytes 147488 | tf_op jit(solution)/shard_map/ppermute | solution.py:310
  5.3 0.1 slice_dynamic-update-slice_fusion
  5.4 4.0 %collective-permute-start.3 = (bf16[2,2,9216]{2,1,0:T(2,128)(2,1)S(1)}, bf16[2,2,9216]{2,1,0:T(2,128)(2,1)S(1)}, u32[]{:S(2)}, u32[]{:S(2)}) collective-permute-start(bf16[2,2,9216]{2,1,0:T(2,128)(2,1)S(1)} %get-tuple-element.86), channel_id=1, source_target_pairs={{0,8},{1,11},{2,10},{3,9},{4,12},{5,15},{6,14},{7,13},{8,0},{9,3},... | collective-permute-start | bytes 221192 | tf_op jit(solution)/shard_map/ppermute | solution.py:323
  9.4 1.3 %collective-permute-start.2 = (bf16[2,2,9216]{2,1,0:T(2,128)(2,1)S(1)}, bf16[2,2,9216]{2,1,0:T(2,128)(2,1)S(1)}, u32[]{:S(2)}, u32[]{:S(2)}) collective-permute-start(bf16[2,2,9216]{2,1,0:T(2,128)(2,1)S(1)} %get-tuple-element.87), channel_id=1, source_target_pairs={{0,12},{1,15},{2,14},{3,13},{4,8},{5,11},{6,10},{7,9},{8,4},{9,7},... | collective-permute-start | bytes 221192 | tf_op jit(solution)/shard_map/ppermute | solution.py:323
  10.8 0.2 %collective-permute-start.1 = (bf16[2,2,9216]{2,1,0:T(2,128)(2,1)S(1)}, bf16[2,2,9216]{2,1,0:T(2,128)(2,1)S(1)}, u32[]{:S(2)}, u32[]{:S(2)}) collective-permute-start(bf16[2,2,9216]{2,1,0:T(2,128)(2,1)S(1)} %get-tuple-element.88), channel_id=1, source_target_pairs={{0,4},{1,7},{2,6},{3,5},{4,0},{5,3},{6,2},{7,1},{8,12},{9,15},{10,... | collective-permute-start | bytes 221192 | tf_op jit(solution)/shard_map/ppermute | solution.py:323
  11.1 1.6 %collective-permute-start.7 = (bf16[2,2,7424]{2,1,0:T(2,128)(2,1)S(1)}, bf16[2,2,7424]{2,1,0:T(2,128)(2,1)S(1)}, u32[]{:S(2)}, u32[]{:S(2)}) collective-permute-start(bf16[2,2,7424]{2,1,0:T(2,128)(2,1)S(1)} %get-tuple-element.84), channel_id=1, source_target_pairs={{0,2},{2,0},{1,3},{3,1},{4,6},{6,4},{5,7},{7,5},{8,10},{10,8},{9,1... | collective-permute-start | bytes 178184 | tf_op jit(solution)/shard_map/ppermute | solution.py:314
  13.3 0.0 collective-permute-done.3.refs_2_
  13.3 0.3 %collective-permute-start.6 = (bf16[2,2,9216]{2,1,0:T(2,128)(2,1)S(1)}, bf16[2,2,9216]{2,1,0:T(2,128)(2,1)S(1)}, u32[]{:S(2)}, u32[]{:S(2)}) collective-permute-start(bf16[2,2,9216]{2,1,0:T(2,128)(2,1)S(1)} %collective-permute-done.3.refs_2_), channel_id=1, source_target_pairs={{0,1},{1,0},{2,3},{3,2},{4,5},{5,4},{6,7},{7,6},{8,9},{9,8},{10,11... | collective-permute-start | bytes 221192 | tf_op jit(solution)/shard_map/ppermute | solution.py:324
  13.6 2.9 %collective-permute-done.2.refs_1_ = bf16[2,2,9216]{2,1,0:T(2,128)(2,1)S(1)} collective-permute-done((bf16[2,2,9216]{2,1,0:T(2,128)(2,1)S(1)}, bf16[2,2,9216]{2,1,0:T(2,128)(2,1)S(1)}, u32[]{:S(2)}, u32[]{:S(2)}) %collective-permute-start.2) | collective-permute-done | bytes 73760 | tf_op jit(solution)/shard_map/ppermute | solution.py:323
  16.4 0.4 %collective-permute-start.5 = (bf16[2,2,9216]{2,1,0:T(2,128)(2,1)S(1)}, bf16[2,2,9216]{2,1,0:T(2,128)(2,1)S(1)}, u32[]{:S(2)}, u32[]{:S(2)}) collective-permute-start(bf16[2,2,9216]{2,1,0:T(2,128)(2,1)S(1)} %collective-permute-done.2.refs_1_), channel_id=1, source_target_pairs={{0,1},{1,0},{2,3},{3,2},{4,5},{5,4},{6,7},{7,6},{8,9},{9,8},{10,11... | collective-permute-start | bytes 221192 | tf_op jit(solution)/shard_map/ppermute | solution.py:324
  16.8 0.4 %collective-permute-done.1.refs_0_ = bf16[2,2,9216]{2,1,0:T(2,128)(2,1)S(1)} collective-permute-done((bf16[2,2,9216]{2,1,0:T(2,128)(2,1)S(1)}, bf16[2,2,9216]{2,1,0:T(2,128)(2,1)S(1)}, u32[]{:S(2)}, u32[]{:S(2)}) %collective-permute-start.1) | collective-permute-done | bytes 73760 | tf_op jit(solution)/shard_map/ppermute | solution.py:323
  17.2 0.2 collective-permute-start.4
  17.4 0.0 collective-permute-done.7.refs_4_.refs_7_
  17.4 0.2 gather_rows.1.refs_8_
  17.6 0.0 collective-permute-done.6.refs_5_
  17.6 0.2 collective-permute-done.5.refs_4_
  17.7 0.8 %collective-permute-done.4.refs_3_ = bf16[2,2,9216]{2,1,0:T(2,128)(2,1)S(1)} collective-permute-done((bf16[2,2,9216]{2,1,0:T(2,128)(2,1)S(1)}, bf16[2,2,9216]{2,1,0:T(2,128)(2,1)S(1)}, u32[]{:S(2)}, u32[]{:S(2)}) %collective-permute-start.4) | collective-permute-done | bytes 73760 | tf_op jit(solution)/shard_map/ppermute | solution.py:324
  18.5 4.1 %factor_tiles.1 = (bf16[2048,2048]{1,0:T(8,128)(2,1)}, bf16[768,768]{1,0:T(8,128)(2,1)}, bf16[2,1024]{1,0:T(2,128)(2,1)}, bf16[2,768]{1,0:T(2,128)(2,1)}) custom-call(s32[1]{0:T(128)S(6)} %copy.18.count_ref, bf16[2,2,9216]{2,1,0:T(2,128)(2,1)S(1)} %collective-permute-done.1.refs_0_, bf16[2,2,9216]{2,1,0:T(2,128)(2,1)S(1)} %collective-permute-done.2.refs_1_, ...), custom_call_target="tpu_custom_call" | custom-call | tf_op jit(solution)/shard_map/factor_tiles/pallas_call | solution.py:274
  (1 shorter events, 0.0 us)
Async XLA Ops:
  3.8 1.5 %collective-permute-start = (bf16[4,2,9216]{2,1,0:T(2,128)(2,1)S(1)}, bf16[4,2,9216]{2,1,0:T(2,128)(2,1)S(1)}, u32[]{:S(2)}, u32[]{:S(2)}) collective-permute-start(bf16[4,2,9216]{2,1,0:T(2,128)(2,1)S(1)} %get-tuple-element.75), channel_id=1, source_target_pairs={{0,1},{1,0},{2,3},{3,2},{4,5},{5,4},{6,7},{7,6},{8,9},{9,8},{10,11... | collective-permute-start | bytes 442376 | tf_op jit(solution)/shard_map/ppermute | solution.py:310
  5.4 7.8 %collective-permute-start.3 = (bf16[2,2,9216]{2,1,0:T(2,128)(2,1)S(1)}, bf16[2,2,9216]{2,1,0:T(2,128)(2,1)S(1)}, u32[]{:S(2)}, u32[]{:S(2)}) collective-permute-start(bf16[2,2,9216]{2,1,0:T(2,128)(2,1)S(1)} %get-tuple-element.86), channel_id=1, source_target_pairs={{0,8},{1,11},{2,10},{3,9},{4,12},{5,15},{6,14},{7,13},{8,0},{9,3},... | collective-permute-start | bytes 221192 | tf_op jit(solution)/shard_map/ppermute | solution.py:323
  9.4 7.0 %collective-permute-start.2 = (bf16[2,2,9216]{2,1,0:T(2,128)(2,1)S(1)}, bf16[2,2,9216]{2,1,0:T(2,128)(2,1)S(1)}, u32[]{:S(2)}, u32[]{:S(2)}) collective-permute-start(bf16[2,2,9216]{2,1,0:T(2,128)(2,1)S(1)} %get-tuple-element.87), channel_id=1, source_target_pairs={{0,12},{1,15},{2,14},{3,13},{4,8},{5,11},{6,10},{7,9},{8,4},{9,7},... | collective-permute-start | bytes 221192 | tf_op jit(solution)/shard_map/ppermute | solution.py:323
  10.8 6.5 %collective-permute-start.1 = (bf16[2,2,9216]{2,1,0:T(2,128)(2,1)S(1)}, bf16[2,2,9216]{2,1,0:T(2,128)(2,1)S(1)}, u32[]{:S(2)}, u32[]{:S(2)}) collective-permute-start(bf16[2,2,9216]{2,1,0:T(2,128)(2,1)S(1)} %get-tuple-element.88), channel_id=1, source_target_pairs={{0,4},{1,7},{2,6},{3,5},{4,0},{5,3},{6,2},{7,1},{8,12},{9,15},{10,... | collective-permute-start | bytes 221192 | tf_op jit(solution)/shard_map/ppermute | solution.py:323
  11.1 6.4 %collective-permute-start.7 = (bf16[2,2,7424]{2,1,0:T(2,128)(2,1)S(1)}, bf16[2,2,7424]{2,1,0:T(2,128)(2,1)S(1)}, u32[]{:S(2)}, u32[]{:S(2)}) collective-permute-start(bf16[2,2,7424]{2,1,0:T(2,128)(2,1)S(1)} %get-tuple-element.84), channel_id=1, source_target_pairs={{0,2},{2,0},{1,3},{3,1},{4,6},{6,4},{5,7},{7,5},{8,10},{10,8},{9,1... | collective-permute-start | bytes 178184 | tf_op jit(solution)/shard_map/ppermute | solution.py:314
  13.3 4.3 %collective-permute-start.6 = (bf16[2,2,9216]{2,1,0:T(2,128)(2,1)S(1)}, bf16[2,2,9216]{2,1,0:T(2,128)(2,1)S(1)}, u32[]{:S(2)}, u32[]{:S(2)}) collective-permute-start(bf16[2,2,9216]{2,1,0:T(2,128)(2,1)S(1)} %collective-permute-done.3.refs_2_), channel_id=1, source_target_pairs={{0,1},{1,0},{2,3},{3,2},{4,5},{5,4},{6,7},{7,6},{8,9},{9,8},{10,11... | collective-permute-start | bytes 221192 | tf_op jit(solution)/shard_map/ppermute | solution.py:324
  16.4 1.3 %collective-permute-start.5 = (bf16[2,2,9216]{2,1,0:T(2,128)(2,1)S(1)}, bf16[2,2,9216]{2,1,0:T(2,128)(2,1)S(1)}, u32[]{:S(2)}, u32[]{:S(2)}) collective-permute-start(bf16[2,2,9216]{2,1,0:T(2,128)(2,1)S(1)} %collective-permute-done.2.refs_1_), channel_id=1, source_target_pairs={{0,1},{1,0},{2,3},{3,2},{4,5},{5,4},{6,7},{7,6},{8,9},{9,8},{10,11... | collective-permute-start | bytes 221192 | tf_op jit(solution)/shard_map/ppermute | solution.py:324
  17.2 1.3 %collective-permute-start.4 = (bf16[2,2,9216]{2,1,0:T(2,128)(2,1)S(1)}, bf16[2,2,9216]{2,1,0:T(2,128)(2,1)S(1)}, u32[]{:S(2)}, u32[]{:S(2)}) collective-permute-start(bf16[2,2,9216]{2,1,0:T(2,128)(2,1)S(1)} %collective-permute-done.1.refs_0_), channel_id=1, source_target_pairs={{0,1},{1,0},{2,3},{3,2},{4,5},{5,4},{6,7},{7,6},{8,9},{9,8},{10,11... | collective-permute-start | bytes 221192 | tf_op jit(solution)/shard_map/ppermute | solution.py:324
